TPU v7x, 32 devices: a whole 2x2x4 slice. The times are simulated.
32 devices in a mesh: parts: 2 (over y), seq: 4 (over z), chan: 4 (over x, core).
Axes of the slice: x: 2, y: 2, z: 4, core: 2. Of those that a mesh axis runs over, the one named last changes fastest.
Arguments:
- records: bfloat16 [8, 1536, 512], P('parts', 'seq', 'chan'), parts along dimension 0, may hold values from -6 to 6
- norm_gain: float32 [512], replicated, may hold values from 0.1 to 1.9
- in_projection: bfloat16 [512, 3, 512], P(None, None, 'chan'), may hold values from -0.25 to 0.25
- short_kernel: float32 [3, 3, 512], P(None, None, 'chan'), may hold values from -3.5 to 3.5
- long_filter: bfloat16 [16, 1536], P('chan', 'seq'), may hold values from -1.6 to 1.6
- skip_gain: float32 [512], P('chan'), may hold values from 0.5 to 1.5
- out_projection: bfloat16 [512, 512], P('chan'), may hold values from -0.25 to 0.25
Outputs:
- mixed: bfloat16 [8, 1536, 512], P('parts', 'seq', 'chan'), parts along dimension 0
There are 2 independent parts, one for each index of `parts`. A program takes and returns all parts, laid end to end along the dimension named above; an argument that names none is the same for every part. Nothing has to cross between parts.
All inputs are finite; a program needn't handle non-finite values.
Results may differ from a plain program's by a relative error of at most 0.015.
Values may be sent and summed in bfloat16 or wider, within the bound.
No kernel may reach another device: no remote copies, remote signals or barrier semaphores. Data moves between devices by JAX's collectives and lax.ppermute only.
A program may use at most 128 MiB of HBM per device.

v0:
```python
import jax
import jax.numpy as jnp
from jax import lax
from jax.sharding import PartitionSpec as P


def from_behind(block, axis, distance):
    devices = range(lax.axis_size(axis))
    route = [(i - distance, i) for i in devices if i - distance in devices]
    return lax.ppermute(block, axis, route)


def block_terms(taps_padded, offset, block_source, block_len):
    filter_count = taps_padded.shape[0]
    window = lax.dynamic_slice_in_dim(taps_padded, offset + 1, 2 * block_len - 1, 1)
    flipped = window[:, ::-1]
    padded = jnp.pad(flipped, ((0, 0), (0, 1)))
    tiled_taps = jnp.tile(padded, (1, block_len))
    toeplitz = tiled_taps[:, block_len - 1 : block_len - 1 + block_len * (2 * block_len - 1)]
    toeplitz = toeplitz.reshape(filter_count, block_len, 2 * block_len - 1)[:, :, :block_len]
    record_count = block_source.shape[0]
    grouped = block_source.reshape(record_count, block_len, filter_count, -1)
    return jnp.einsum("fab,rbfg->rafg", toeplitz, grouped, preferred_element_type=jnp.float32)


def body(records, norm_gain, in_projection, short_kernel, long_filter, skip_gain, out_projection):
    gathered = lax.all_gather(records, "chan", axis=2, tiled=True)
    widened = gathered.astype(jnp.float32)
    inv_rms = lax.rsqrt(jnp.mean(widened * widened, axis=-1, keepdims=True) + 1e-06)
    normed = (widened * inv_rms * norm_gain).astype(jnp.bfloat16)
    projected = jnp.einsum(
        "rtd,dkc->rtkc", normed, in_projection, preferred_element_type=jnp.float32
    ).astype(jnp.bfloat16)
    rim_rows = from_behind(projected[:, -2:], "seq", 1)
    extended = jnp.concatenate([rim_rows, projected], axis=1).astype(jnp.float32)
    streams = (
        short_kernel[0] * extended[:, 2:]
        + short_kernel[1] * extended[:, 1:-1]
        + short_kernel[2] * extended[:, :-2]
    )
    query_gate = streams[:, :, 0]
    gated_source = (streams[:, :, 1] * streams[:, :, 2]).astype(jnp.bfloat16)
    record_count = gated_source.shape[0]
    block_len = gated_source.shape[1]
    channels = gated_source.shape[2]
    all_taps = lax.all_gather(long_filter, "seq", axis=1, tiled=True)
    taps_padded = jnp.concatenate(
        [jnp.zeros((all_taps.shape[0], block_len), jnp.bfloat16), all_taps], axis=1
    )
    my_start = lax.axis_index("seq") * block_len
    cycle_stops = lax.axis_size("seq")
    long_sum = block_terms(taps_padded, 0, gated_source, block_len)

    def advance(stop_index, state):
        running_sum, visiting = state
        visiting = from_behind(visiting, "seq", 1)
        lag_start = stop_index * block_len
        running_sum = lax.cond(
            lag_start <= my_start,
            lambda running: running + block_terms(taps_padded, lag_start, visiting, block_len),
            lambda running: running,
            running_sum,
        )
        return (running_sum, visiting)

    long_sum, visiting = lax.fori_loop(1, cycle_stops, advance, (long_sum, gated_source))
    long_out = long_sum.reshape(
        record_count, block_len, channels
    ) + skip_gain * gated_source.astype(jnp.float32)
    gated = (query_gate * long_out).astype(jnp.bfloat16)
    partial_terms = jnp.einsum(
        "rtc,cd->rtd", gated, out_projection, preferred_element_type=jnp.float32
    )
    return lax.psum_scatter(
        partial_terms.astype(jnp.bfloat16), "chan", scatter_dimension=2, tiled=True
    )


def solution(mesh):
    placed = (
        P("parts", "seq", "chan"),
        P(),
        P(None, None, "chan"),
        P(None, None, "chan"),
        P("chan", "seq"),
        P("chan"),
        P("chan", None),
    )
    return jax.shard_map(
        body, mesh=mesh, in_specs=placed, out_specs=P("parts", "seq", "chan"), check_vma=False
    )
```

profile of v0, /device:TPU:0, one launch (start us, length us, event | category | flops | bytes accessed | tf_op | source)
XLA Modules:
  0.0 202.3 jit_solution(438159001702864460)
XLA Ops:
  6.5 0.0 copy-start
  6.5 0.0 copy-start.9
  6.5 0.0 all-gather.2.cloned.1.call-start
  6.5 0.7 all-gather.2.cloned.1.call-update
  7.3 0.0 reduce-scatter.4.cloned.1.call-start
  7.3 14.9 %all_gather.7 = bf16[4,1536]{1,0:T(4,128)(2,1)S(1)} all-gather(bf16[4,384]{1,0:T(4,128)(2,1)} %param.15), channel_id=1, replica_groups=mesh['parts'=2,'seq'=4,'chan'=4] {'seq'}, dimensions={1}, use_global_device_ids=true | all-gather | bytes 15360 | tf_op jit(solution)/shard_map/all_gather | solution.py:46
  22.2 0.1 pad_slice_fusion
  22.2 0.5 reverse.1
  22.8 0.1 slice.94
  22.9 0.2 broadcast_bitcast_fusion.1
  23.0 8.4 %all-gather.2.cloned.1.call-done = bf16[4,384,512]{2,1,0:T(8,128)(2,1)} async-done(((bf16[4,384,128]{2,1,0:T(8,128)(2,1)}), bf16[4,384,512]{2,1,0:T(8,128)(2,1)}) %all-gather.2.cloned.1.call-update) | async-done | bytes 1572880 | tf_op jit(solution)/shard_map/all_gather | solution.py:27
  31.5 1.8 fusion.2
  33.3 0.0 copy-done
  33.3 0.0 copy-done.9
  33.3 0.0 copy-start.7
  33.3 2.4 %fusion.12 = bf16[4,384,3,128]{3,1,2,0:T(8,128)(2,1)S(1)} fusion(bf16[4,384,512]{2,1,0:T(8,128)(2,1)} %all-gather.2.cloned.1.call-done, f32[512]{0:T(512)S(1)} %copy-done.9, f32[4,384]{1,0:T(4,128)S(1)} %add_rsqrt_fusion, bf16[512,3,128]{2,0,1:T(8,128)(2,1)S(1)} %copy-done), kind=kOutput, calls=%fused_computation.19 | convolution fusion | flops 607715328 | bytes 3153920 | tf_op jit(solution)/shard_map/rtd,dkc->rtkc/dot_general | solution.py:31
  35.8 0.0 copy-start.5
  35.8 3.4 %collective-permute-start.1 = (bf16[4,2,3,128]{3,1,2,0:T(2,128)(2,1)S(1)}, bf16[4,2,3,128]{3,1,2,0:T(2,128)(2,1)S(1)}, u32[]{:S(2)}, u32[]{:S(2)}) collective-permute-start(bf16[4,2,3,128]{3,1,2,0:T(2,128)(2,1)S(1)} %slice.56), channel_id=1, source_target_pairs={{0,4},{4,8},{8,12},{1,5},{5,9},{9,13},{2,6},{6,10},{10,14},{3,7},{... | collective-permute-start | bytes 18440 | tf_op jit(solution)/shard_map/ppermute | solution.py:10
  39.2 0.0 copy-done.7
  39.2 0.0 copy-done.5
  39.2 1.8 copy.32
  41.1 2.8 %slice.63 = bf16[4,294528]{1,0:T(4,128)(2,1)} slice(bf16[4,294912]{1,0:T(4,128)(2,1)S(1)} %bitcast.67), slice={[0:4], [383:294911]} | slice | bytes 4712448 | tf_op jit(solution)/shard_map/slice | solution.py:19
  43.9 3.3 %reshape.52 = bf16[1178112]{0:T(1024)(128)(2,1)S(1)} reshape(bf16[4,294528]{1,0:T(4,128)(2,1)} %slice.63) | data formatting | bytes 4712448
  47.2 6.5 %reshape.40 = bf16[4,384,767]{2,1,0:T(8,128)(2,1)} reshape(bf16[1178112]{0:T(1024)(128)(2,1)S(1)} %reshape.52) | data formatting | bytes 4712448 | tf_op jit(solution)/shard_map/reshape | solution.py:20
  53.7 0.0 collective-permute-done.1
  53.7 1.5 maximum_convert_fusion
  55.2 0.7 fusion.5
  55.9 0.0 copy-start.1
  55.9 0.0 copy-start.2
  55.9 0.1 fusion.15
  56.0 1.3 copy-done.1
  57.3 0.0 copy-start.3
  57.3 0.8 fusion.25
  58.1 0.2 copy.21
  58.4 1.9 copy.23
  60.3 0.0 copy-done.2
  60.3 1.4 convolution_bitcast_fusion
  61.7 0.0 copy-done.3
  61.7 57.2 %while.18 = (s32[]{:T(128)}, f32[4,384,4,32]{1,3,0,2:T(8,128)}, bf16[4,384,128]{1,2,0:T(8,128)(2,1)}, s32[]{:T(128)}, bf16[4,1920]{1,0:T(4,128)(2,1)S(1)}, /*index=5*/s32[]{:T(128)}, s32[]{:T(128)}) while((s32[]{:T(128)}, f32[4,384,4,32]{1,3,0,2:T(8,128)}, bf16[4,384,128]{1,2,0:T(8,128)(2,1)}, s32[]{:T(128)}, bf16[4,1920]{1,0:T(4,128)(2,1)S(1)}, ...), condition=%wide.region_4.5_spmd, body=%wide.region_1.4_spmd.sunk | while | flops 151191552 | bytes 29135044 | solution.py:66
  61.7 3.4 %collective-permute-start = (bf16[4,384,128]{1,2,0:T(8,128)(2,1)}, bf16[4,384,128]{1,2,0:T(8,128)(2,1)S(1)}, u32[]{:S(2)}, u32[]{:S(2)}) collective-permute-start(bf16[4,384,128]{1,2,0:T(8,128)(2,1)} %get-tuple-element.183), channel_id=1, source_target_pairs={{0,4},{4,8},{8,12},{1,5},{5,9},{9,13},{2,6},{6,10},{10,14},{3,7},{... | collective-permute-start | bytes 1179656 | tf_op jit(solution)/shard_map/while/body/eval_jaxpr/ppermute | solution.py:10
  65.1 8.8 %collective-permute-done = bf16[4,384,128]{1,2,0:T(8,128)(2,1)S(1)} collective-permute-done((bf16[4,384,128]{1,2,0:T(8,128)(2,1)}, bf16[4,384,128]{1,2,0:T(8,128)(2,1)S(1)}, u32[]{:S(2)}, u32[]{:S(2)}) %collective-permute-start) | collective-permute-done | bytes 393248 | tf_op jit(solution)/shard_map/while/body/eval_jaxpr/ppermute | solution.py:10
  73.9 0.8 copy.46
  74.7 23.5 %collective-permute-start = (bf16[4,384,128]{1,2,0:T(8,128)(2,1)}, bf16[4,384,128]{1,2,0:T(8,128)(2,1)S(1)}, u32[]{:S(2)}, u32[]{:S(2)}) collective-permute-start(bf16[4,384,128]{1,2,0:T(8,128)(2,1)} %get-tuple-element.183), channel_id=1, source_target_pairs={{0,4},{4,8},{8,12},{1,5},{5,9},{9,13},{2,6},{6,10},{10,14},{3,7},{... | collective-permute-start | bytes 1179656 | tf_op jit(solution)/shard_map/while/body/eval_jaxpr/ppermute | solution.py:10
  98.2 7.9 %collective-permute-done = bf16[4,384,128]{1,2,0:T(8,128)(2,1)S(1)} collective-permute-done((bf16[4,384,128]{1,2,0:T(8,128)(2,1)}, bf16[4,384,128]{1,2,0:T(8,128)(2,1)S(1)}, u32[]{:S(2)}, u32[]{:S(2)}) %collective-permute-start) | collective-permute-done | bytes 393248 | tf_op jit(solution)/shard_map/while/body/eval_jaxpr/ppermute | solution.py:10
  106.1 0.8 copy.46
  106.9 4.3 %collective-permute-start = (bf16[4,384,128]{1,2,0:T(8,128)(2,1)}, bf16[4,384,128]{1,2,0:T(8,128)(2,1)S(1)}, u32[]{:S(2)}, u32[]{:S(2)}) collective-permute-start(bf16[4,384,128]{1,2,0:T(8,128)(2,1)} %get-tuple-element.183), channel_id=1, source_target_pairs={{0,4},{4,8},{8,12},{1,5},{5,9},{9,13},{2,6},{6,10},{10,14},{3,7},{... | collective-permute-start | bytes 1179656 | tf_op jit(solution)/shard_map/while/body/eval_jaxpr/ppermute | solution.py:10
  111.2 7.0 %collective-permute-done = bf16[4,384,128]{1,2,0:T(8,128)(2,1)S(1)} collective-permute-done((bf16[4,384,128]{1,2,0:T(8,128)(2,1)}, bf16[4,384,128]{1,2,0:T(8,128)(2,1)S(1)}, u32[]{:S(2)}, u32[]{:S(2)}) %collective-permute-start) | collective-permute-done | bytes 393248 | tf_op jit(solution)/shard_map/while/body/eval_jaxpr/ppermute | solution.py:10
  118.2 0.8 copy.46
  118.9 0.0 copy-start.4
  118.9 0.0 copy-start.6
  118.9 0.0 copy-start.8
  118.9 1.2 copy.24
  120.2 1.2 copy.25
  121.4 0.0 copy-done.4
  121.4 0.0 copy-done.6
  121.4 0.0 copy-done.8
  121.4 1.9 convolution_convert_fusion
  123.3 1.4 copy.28
  124.8 1.4 copy.33
  126.2 0.0 reduce-scatter.4.cloned.1.call-update
  126.2 67.1 %reduce-scatter.4.cloned.1.call-done = bf16[128,1536]{1,0:T(8,128)(2,1)} async-done(((bf16[512,1536]{1,0:T(8,128)(2,1)}), bf16[128,1536]{1,0:T(8,128)(2,1)}) %reduce-scatter.4.cloned.1.call-update) | async-done | bytes 393232
  193.4 1.1 reshape.49
  194.4 1.0 copy.29
  (8 shorter events, 0.0 us)
Async XLA Ops:
  6.5 26.8 %copy-start = (bf16[512,3,128]{2,0,1:T(8,128)(2,1)S(1)}, bf16[512,3,128]{2,0,1:T(8,128)(2,1)}, u32[]{:S(2)}) copy-start(bf16[512,3,128]{2,0,1:T(8,128)(2,1)} %param.13) | copy-start | bytes 1179652
  6.5 26.8 %copy-start.9 = (f32[512]{0:T(512)S(1)}, f32[512]{0:T(512)}, u32[]{:S(2)}) copy-start(f32[512]{0:T(512)} %param.12) | copy-start | bytes 6148
  6.5 24.9 %all-gather.2.cloned.1.call-start = ((), (), s32[]{:S(2)}) async-start(), calls=%async_computation.1 | async-start | bytes 1966080 | tf_op jit(solution)/shard_map/all_gather | solution.py:27
  7.3 186.1 %reduce-scatter.4.cloned.1.call-start = ((), (), s32[]{:S(2)}) async-start(), calls=%async_computation.2 | async-start | bytes 1966080
  33.3 5.9 %copy-start.7 = (f32[3,3,128]{2,1,0:T(4,128)S(1)}, f32[3,3,128]{2,1,0:T(4,128)}, u32[]{:S(2)}) copy-start(f32[3,3,128]{2,1,0:T(4,128)} %param.14) | copy-start | bytes 13828
  35.8 3.5 %copy-start.5 = (bf16[4,384,3,128]{3,1,2,0:T(8,128)(2,1)}, bf16[4,384,3,128]{3,1,2,0:T(8,128)(2,1)S(1)}, u32[]{:S(2)}) copy-start(bf16[4,384,3,128]{3,1,2,0:T(8,128)(2,1)S(1)} %fusion.12) | copy-start | bytes 3538948
  35.8 17.9 %collective-permute-start.1 = (bf16[4,2,3,128]{3,1,2,0:T(2,128)(2,1)S(1)}, bf16[4,2,3,128]{3,1,2,0:T(2,128)(2,1)S(1)}, u32[]{:S(2)}, u32[]{:S(2)}) collective-permute-start(bf16[4,2,3,128]{3,1,2,0:T(2,128)(2,1)S(1)} %slice.56), channel_id=1, source_target_pairs={{0,4},{4,8},{8,12},{1,5},{5,9},{9,13},{2,6},{6,10},{10,14},{3,7},{... | collective-permute-start | bytes 18440 | tf_op jit(solution)/shard_map/ppermute | solution.py:10
  55.9 1.4 copy-start.1
  55.9 4.4 %copy-start.2 = (bf16[4,384,767]{2,1,0:T(8,128)(2,1)S(1)}, bf16[4,384,767]{2,1,0:T(8,128)(2,1)}, u32[]{:S(2)}) copy-start(bf16[4,384,767]{2,1,0:T(8,128)(2,1)} %reshape.40) | copy-start | bytes 7068676
  57.3 4.4 %copy-start.3 = (bf16[4,384,1,128]{3,1,2,0:T(8,128)(2,1)}, bf16[4,384,1,128]{3,1,2,0:T(8,128)(2,1)S(1)}, u32[]{:S(2)}) copy-start(bf16[4,384,1,128]{3,1,2,0:T(8,128)(2,1)S(1)} %fusion.15) | copy-start | bytes 1179652
  61.7 12.2 %collective-permute-start = (bf16[4,384,128]{1,2,0:T(8,128)(2,1)}, bf16[4,384,128]{1,2,0:T(8,128)(2,1)S(1)}, u32[]{:S(2)}, u32[]{:S(2)}) collective-permute-start(bf16[4,384,128]{1,2,0:T(8,128)(2,1)} %get-tuple-element.183), channel_id=1, source_target_pairs={{0,4},{4,8},{8,12},{1,5},{5,9},{9,13},{2,6},{6,10},{10,14},{3,7},{... | collective-permute-start | bytes 1179656 | tf_op jit(solution)/shard_map/while/body/eval_jaxpr/ppermute | solution.py:10
  74.7 31.5 %collective-permute-start = (bf16[4,384,128]{1,2,0:T(8,128)(2,1)}, bf16[4,384,128]{1,2,0:T(8,128)(2,1)S(1)}, u32[]{:S(2)}, u32[]{:S(2)}) collective-permute-start(bf16[4,384,128]{1,2,0:T(8,128)(2,1)} %get-tuple-element.183), channel_id=1, source_target_pairs={{0,4},{4,8},{8,12},{1,5},{5,9},{9,13},{2,6},{6,10},{10,14},{3,7},{... | collective-permute-start | bytes 1179656 | tf_op jit(solution)/shard_map/while/body/eval_jaxpr/ppermute | solution.py:10
  106.9 11.3 %collective-permute-start = (bf16[4,384,128]{1,2,0:T(8,128)(2,1)}, bf16[4,384,128]{1,2,0:T(8,128)(2,1)S(1)}, u32[]{:S(2)}, u32[]{:S(2)}) collective-permute-start(bf16[4,384,128]{1,2,0:T(8,128)(2,1)} %get-tuple-element.183), channel_id=1, source_target_pairs={{0,4},{4,8},{8,12},{1,5},{5,9},{9,13},{2,6},{6,10},{10,14},{3,7},{... | collective-permute-start | bytes 1179656 | tf_op jit(solution)/shard_map/while/body/eval_jaxpr/ppermute | solution.py:10
  118.9 2.4 %copy-start.4 = (bf16[4,384,1,128]{3,1,2,0:T(8,128)(2,1)S(1)}, bf16[4,384,1,128]{3,1,2,0:T(8,128)(2,1)}, u32[]{:S(2)}) copy-start(bf16[4,384,1,128]{3,1,2,0:T(8,128)(2,1)} %copy-done.3) | copy-start | bytes 1179652
  118.9 2.4 %copy-start.6 = (bf16[128,512]{1,0:T(8,128)(2,1)S(1)}, bf16[128,512]{1,0:T(8,128)(2,1)}, u32[]{:S(2)}) copy-start(bf16[128,512]{1,0:T(8,128)(2,1)} %param.17) | copy-start | bytes 393220
  118.9 2.4 %copy-start.8 = (f32[128]{0:T(128)S(1)}, f32[128]{0:T(128)}, u32[]{:S(2)}) copy-start(f32[128]{0:T(128)} %param.16) | copy-start | bytes 1540
Sparse Core Ops, SparseCore 0:
  8.9 22.5 all-gather.1
  126.3 66.9 reduce-scatter.3
where the time goes:
time: 203 us; the launch traced here: 202 us
  waiting for transfers between devices  100 us (49%)
  starting transfers between devices  34.6 us (17%)
  local copies, waits for them, and re-layouts  28.4 us (14%)
  blocking collectives  14.9 us (7%)
  between operations  13.6 us (7%)
  matrix products  5.77 us (3%)
  other arithmetic  4.91 us (2%)
    unnamed x3, waiting for transfers between devices  67.9 us
    ppermute x4, starting transfers between devices, from_behind(): return lax.ppermute(block, axis, route)  34.6 us
    ppermute x4, waiting for transfers between devices, from_behind(): return lax.ppermute(block, axis, route)  23.7 us
    all_gather x1, blocking collectives, body(): all_taps = lax.all_gather(long_filter, 'seq', axis=1, tiled=True)  14.9 us
    unnamed x29, local copies, waits for them, and re-layouts  12.2 us
    all_gather x1, waiting for transfers between devices, body(): gathered = lax.all_gather(records, 'chan', axis=2, tiled=True)  8.44 us
    reshape x1, local copies, waits for them, and re-layouts, block_terms(): toeplitz.reshape(filter_count, block_len, 2 * block_len - 1)  6.49 us
  transfers between devices with their start and end apart: 6, of which 5 were waited for; matrix products, arithmetic and copies ran while one was open for 8% of the time, Pallas kernels for 0%

commit v1 on v0

--- a/solution.py
+++ b/solution.py
@@ -1,7 +1,14 @@
 import jax
 import jax.numpy as jnp
 from jax import lax
+from jax.experimental import pallas as pl
+from jax.experimental.pallas import tpu as pltpu
 from jax.sharding import PartitionSpec as P
+
+LANES = 128
+EXTRA = 32
+BACK = 16
+VMEM = pltpu.VMEM
 
 
 def from_behind(block, axis, distance):
@@ -23,7 +30,7 @@
     return jnp.einsum("fab,rbfg->rafg", toeplitz, grouped, preferred_element_type=jnp.float32)
 
 
-def body(records, norm_gain, in_projection, short_kernel, long_filter, skip_gain, out_projection):
+def ring_body(records, norm_gain, in_projection, short_kernel, long_filter, skip_gain, out_projection):
     gathered = lax.all_gather(records, "chan", axis=2, tiled=True)
     widened = gathered.astype(jnp.float32)
     inv_rms = lax.rsqrt(jnp.mean(widened * widened, axis=-1, keepdims=True) + 1e-06)
@@ -40,9 +47,7 @@
     )
     query_gate = streams[:, :, 0]
     gated_source = (streams[:, :, 1] * streams[:, :, 2]).astype(jnp.bfloat16)
-    record_count = gated_source.shape[0]
-    block_len = gated_source.shape[1]
-    channels = gated_source.shape[2]
+    record_count, block_len, channels = gated_source.shape
     all_taps = lax.all_gather(long_filter, "seq", axis=1, tiled=True)
     taps_padded = jnp.concatenate(
         [jnp.zeros((all_taps.shape[0], block_len), jnp.bfloat16), all_taps], axis=1
@@ -63,7 +68,7 @@
         )
         return (running_sum, visiting)
 
-    long_sum, visiting = lax.fori_loop(1, cycle_stops, advance, (long_sum, gated_source))
+    long_sum, _ = lax.fori_loop(1, cycle_stops, advance, (long_sum, gated_source))
     long_out = long_sum.reshape(
         record_count, block_len, channels
     ) + skip_gain * gated_source.astype(jnp.float32)
@@ -73,6 +78,299 @@
     )
     return lax.psum_scatter(
         partial_terms.astype(jnp.bfloat16), "chan", scatter_dimension=2, tiled=True
+    )
+
+
+def rotate(block, axis, distance):
+    n = lax.axis_size(axis)
+    return lax.ppermute(block, axis, [(i, (i + distance) % n) for i in range(n)])
+
+
+def exchange(block, axis, mask):
+    return lax.ppermute(block, axis, [(i, i ^ mask) for i in range(lax.axis_size(axis))])
+
+
+def vmem_call(kernel, outs, scratch, flops, *operands):
+    moved = sum(x.size * x.dtype.itemsize for x in (*operands, *outs))
+    return pl.pallas_call(
+        kernel,
+        out_shape=tuple(outs),
+        in_specs=[pl.BlockSpec(memory_space=VMEM)] * len(operands),
+        out_specs=tuple(pl.BlockSpec(memory_space=VMEM) for _ in outs),
+        scratch_shapes=scratch,
+        compiler_params=pltpu.CompilerParams(vmem_limit_bytes=40 * 1024 * 1024),
+        cost_estimate=pl.CostEstimate(flops=flops, bytes_accessed=moved, transcendentals=0),
+    )(*operands)
+
+
+def pick_records(records, offsets):
+    count = records.shape[0]
+
+    def kernel(records_ref, out_ref, sems):
+        z = lax.axis_index("seq")
+        copies = [
+            pltpu.make_async_copy(records_ref.at[lax.rem(z + k, count)], out_ref.at[i], sems.at[i])
+            for i, k in enumerate(offsets)
+        ]
+        for copy in copies:
+            copy.start()
+        for copy in copies:
+            copy.wait()
+
+    return pl.pallas_call(
+        kernel,
+        out_shape=jax.ShapeDtypeStruct((len(offsets), *records.shape[1:]), records.dtype),
+        in_specs=[pl.BlockSpec(memory_space=pl.ANY)],
+        out_specs=pl.BlockSpec(memory_space=VMEM),
+        scratch_shapes=[pltpu.SemaphoreType.DMA((len(offsets),))],
+    )(records)
+
+
+def pick_columns(out_projection):
+    rows = out_projection.shape[0]
+
+    def kernel(w_ref, one_ref, two_ref):
+        me = lax.axis_index("chan")
+        for mask, ref, start in ((1, one_ref, 0), (2, two_ref, 0), (3, two_ref, rows)):
+            first = pl.multiple_of(jnp.bitwise_xor(me, mask) * LANES, LANES)
+            ref[start : start + rows, :] = w_ref[:, pl.ds(first, LANES)]
+
+    shape = lambda n: jax.ShapeDtypeStruct((n, LANES), out_projection.dtype)
+    return vmem_call(kernel, [shape(rows), shape(2 * rows)], [], 0, out_projection)
+
+
+def project(records, beside, across, diagonal, norm_gain, weights, short_kernel, taps, offsets):
+    count, block_len, _ = records.shape
+    picked = len(offsets)
+    depth = weights.shape[1]
+    f32, bf16 = jnp.float32, jnp.bfloat16
+
+    def kernel(own_ref, beside_ref, across_ref, diagonal_ref, gain_ref, w_ref, short_ref, taps_ref, *rest):
+        chunk_refs, (query_ref, w_all, shifted) = rest[:picked], rest[picked:]
+        me = lax.axis_index("chan")
+        z = lax.axis_index("seq")
+        for j in range(4):
+            first = pl.multiple_of(jnp.bitwise_xor(me, j) * LANES, LANES)
+            for s in range(3):
+                w_all[j * LANES : (j + 1) * LANES, s * LANES : (s + 1) * LANES] = w_ref[s, pl.ds(first, LANES), :]
+        shifted[0:8, :] = jnp.zeros((8, 3 * LANES), f32)
+        taps_block = taps_ref[...]
+        flip = (
+            lax.broadcasted_iota(jnp.int32, (LANES, LANES), 0)
+            + lax.broadcasted_iota(jnp.int32, (LANES, LANES), 1)
+            == LANES - 1
+        ).astype(bf16)
+        tap_rows = [
+            jnp.dot(taps_block[:, b * LANES : (b + 1) * LANES], flip, preferred_element_type=f32)
+            for b in range(block_len // LANES)
+        ]
+        for i, k in enumerate(offsets):
+            rec = lax.rem(z + k, count)
+            slabs = [own_ref[rec], beside_ref[rec], across_ref[i], diagonal_ref[i]]
+            slabs = [s.astype(f32) for s in slabs]
+            squares = slabs[0] * slabs[0]
+            for s in slabs[1:]:
+                squares = squares + s * s
+            inv_rms = lax.rsqrt(jnp.sum(squares, axis=1, keepdims=True) * (1.0 / depth) + 1e-06)
+            normed = [
+                (s * inv_rms * gain_ref[pl.ds(jnp.bitwise_xor(me, j), 1), :]).astype(bf16)
+                for j, s in enumerate(slabs)
+            ]
+            projected = jnp.dot(jnp.concatenate(normed, axis=1), w_all[...], preferred_element_type=f32)
+            shifted[8:, :] = projected.astype(bf16).astype(f32)
+            streams = []
+            for s in range(3):
+                cols = slice(s * LANES, (s + 1) * LANES)
+                streams.append(
+                    short_ref[0, s : s + 1, :] * shifted[8 : 8 + block_len, cols]
+                    + short_ref[1, s : s + 1, :] * shifted[7 : 7 + block_len, cols]
+                    + short_ref[2, s : s + 1, :] * shifted[6 : 6 + block_len, cols]
+                )
+            query_ref[i] = streams[0]
+            chunk_refs[i][0:block_len, :] = (streams[1] * streams[2]).astype(bf16)
+            heads = shifted[8:10, LANES:]
+            tails = shifted[6 + block_len : 8 + block_len, :]
+            rim = [heads[:, :LANES], heads[:, LANES:], tails[:, LANES : 2 * LANES], tails[:, 2 * LANES :], tails[:, :LANES]]
+            extra = jnp.concatenate(tap_rows + rim + [jnp.zeros((EXTRA - 22, LANES), f32)], axis=0)
+            chunk_refs[i][block_len:, :] = extra.astype(bf16)
+
+    chunk = jax.ShapeDtypeStruct((block_len + EXTRA, LANES), bf16)
+    query = jax.ShapeDtypeStruct((picked, block_len, LANES), f32)
+    scratch = [pltpu.VMEM((4 * LANES, 3 * LANES), bf16), pltpu.VMEM((8 + block_len, 3 * LANES), f32)]
+    out = vmem_call(
+        kernel, [chunk] * picked + [query], scratch, 2 * picked * block_len * 512 * 384,
+        records, beside, across, diagonal, norm_gain, weights, short_kernel, taps,
+    )
+    return out[:picked], out[picked]
+
+
+def long_convolution(chunks, distances, short_kernel, skip_gain):
+    n = len(chunks)
+    block_len = chunks[0].shape[0] - EXTRA
+    length = n * block_len
+    pieces = block_len // LANES
+    f32, bf16 = jnp.float32, jnp.bfloat16
+
+    def kernel(*refs):
+        chunk_refs, (short_ref, skip_ref), out_refs = refs[:n], refs[n : n + 2], refs[n + 2 : 2 * n + 2]
+        inputs, source, bands, sums = refs[2 * n + 2 :]
+        z = lax.axis_index("seq")
+        for ref, k in zip(chunk_refs, distances):
+            inputs[lax.rem(z - k + n, n)] = ref[...]
+        lane = lax.broadcasted_iota(jnp.int32, (LANES, LANES), 1)
+        tap_rows = [inputs[q, block_len : block_len + 4 * pieces, :].astype(f32) for q in range(n)]
+        for f in range(4):
+            row = [
+                tap_rows[q][4 * b + f : 4 * b + f + 1, :] for q in reversed(range(n)) for b in reversed(range(pieces))
+            ]
+            row = jnp.concatenate(row + [jnp.zeros((1, LANES), f32)], axis=1)
+            wide = jnp.broadcast_to(row, (LANES, length + LANES))
+            band = pltpu.roll(wide, 1, 1, stride=1, stride_axis=0)
+            bands[f * LANES : (f + 1) * LANES, :] = band.astype(bf16)
+        short = [[short_ref[j, s : s + 1, :] for j in range(3)] for s in range(3)]
+        for q in range(n):
+            source[q * block_len : (q + 1) * block_len, :] = inputs[q, :block_len, :]
+            if q == 0:
+                continue
+            here = inputs[q, block_len : block_len + EXTRA, :].astype(f32)[4 * pieces :]
+            past = inputs[q - 1, block_len : block_len + EXTRA, :].astype(f32)[4 * pieces :]
+            fixed = []
+            for s in (1, 2):
+                head, tail = here[2 * s - 2 : 2 * s], past[2 * s + 2 : 2 * s + 4]
+                k0, k1, k2 = short[s]
+                fixed.append(
+                    (
+                        k0 * head[0:1] + k1 * tail[1:2] + k2 * tail[0:1],
+                        k0 * head[1:2] + k1 * head[0:1] + k2 * tail[1:2],
+                    )
+                )
+            rows = [fixed[0][t] * fixed[1][t] for t in range(2)]
+            first = source[q * block_len : q * block_len + 16, :].astype(f32)
+            first = jnp.concatenate(rows + [first[2:]], axis=0)
+            source[q * block_len : q * block_len + 16, :] = first.astype(bf16)
+        for p in range(length // LANES):
+            reach = (p + 1) * LANES
+            terms = jnp.dot(bands[:, length + LANES - reach :], source[0:reach, :], preferred_element_type=f32)
+            total = terms[0:LANES]
+            for f in range(1, 4):
+                total = jnp.where(lane >= f * 32, terms[f * LANES : (f + 1) * LANES], total)
+            total = total + skip_ref[...] * source[reach - LANES : reach, :].astype(f32)
+            q, b = divmod(p, pieces)
+            sums[q, b * LANES : (b + 1) * LANES, :] = total.astype(bf16)
+        for q in range(n):
+            if q == 0:
+                tail = jnp.zeros((2, LANES), f32)
+            else:
+                tail = inputs[q - 1, block_len : block_len + EXTRA, :].astype(f32)[20:22]
+            sums[q, block_len:, :] = jnp.concatenate([tail, jnp.zeros((BACK - 2, LANES), f32)], axis=0).astype(bf16)
+        for ref, k in zip(out_refs, distances):
+            ref[...] = sums[lax.rem(z + k, n)]
+
+    back = jax.ShapeDtypeStruct((block_len + BACK, LANES), bf16)
+    scratch = [
+        pltpu.VMEM((n, block_len + EXTRA, LANES), bf16),
+        pltpu.VMEM((length, LANES), bf16),
+        pltpu.VMEM((4 * LANES, length + LANES), bf16),
+        pltpu.VMEM((n, block_len + BACK, LANES), bf16),
+    ]
+    return vmem_call(kernel, [back] * n, scratch, 4 * length * length * LANES, *chunks, short_kernel, skip_gain)
+
+
+def gate(sums, queries, short_kernel):
+    block_len = sums[0].shape[0] - BACK
+    n = len(sums)
+    f32, bf16 = jnp.float32, jnp.bfloat16
+    arrays = []
+    for array, _ in queries:
+        if not any(array is a for a in arrays):
+            arrays.append(array)
+    places = [([a is array for a in arrays].index(True), index) for array, index in queries]
+
+    def kernel(*refs):
+        sum_refs, query_refs, short_ref, out_ref = refs[:n], refs[n:-2], refs[-2], refs[-1]
+        for i, (a, index) in enumerate(places):
+            tail = sum_refs[i][block_len:, :].astype(f32)
+            k1, k2 = short_ref[1, 0:1, :], short_ref[2, 0:1, :]
+            rim = [k1 * tail[1:2] + k2 * tail[0:1], k2 * tail[1:2], jnp.zeros((6, LANES), f32)]
+            query = query_refs[a][index]
+            query = jnp.concatenate([query[0:8] + jnp.concatenate(rim, axis=0), query[8:]], axis=0)
+            out = query * sum_refs[i][0:block_len, :].astype(f32)
+            out_ref[i * block_len : (i + 1) * block_len, :] = out.astype(bf16)
+
+    out = jax.ShapeDtypeStruct((n * block_len, LANES), bf16)
+    return vmem_call(kernel, [out], [], 0, *sums, *arrays, short_kernel)[0]
+
+
+def mix(slabs, weights, distances, block_len):
+    f32, bf16 = jnp.float32, jnp.bfloat16
+    count = sum(len(d) for d in distances)
+    groups = len(slabs)
+
+    def kernel(*refs):
+        slab_refs, (own_ref, beside_ref, far_ref, diagonal_ref) = refs[: 4 * groups], refs[4 * groups : 4 * groups + 4]
+        out_ref, w_all = refs[-2:]
+        me = lax.axis_index("chan")
+        z = lax.axis_index("seq")
+        w_all[0:LANES, :] = own_ref[:, pl.ds(pl.multiple_of(me * LANES, LANES), LANES)]
+        w_all[LANES : 2 * LANES, :] = beside_ref[...]
+        w_all[2 * LANES : 3 * LANES, :] = far_ref[0:LANES, :]
+        w_all[3 * LANES :, :] = diagonal_ref[LANES:, :]
+        for g in range(groups):
+            for i, k in enumerate(distances[g]):
+                rows = slice(i * block_len, (i + 1) * block_len)
+                lhs = jnp.concatenate([ref[rows, :] for ref in slab_refs[4 * g : 4 * g + 4]], axis=1)
+                out_ref[lax.rem(z + k, count)] = jnp.dot(lhs, w_all[...], preferred_element_type=f32).astype(bf16)
+
+    out = jax.ShapeDtypeStruct((count, block_len, LANES), bf16)
+    operands = [x for slab in slabs for x in slab] + list(weights)
+    scratch = [pltpu.VMEM((4 * LANES, LANES), bf16)]
+    return vmem_call(kernel, [out], scratch, 2 * count * block_len * 512 * LANES, *operands)[0]
+
+
+def exchange_body(records, norm_gain, in_projection, short_kernel, long_filter, skip_gain, out_projection):
+    block_len = records.shape[1]
+    first = pick_records(records, (2, 1))
+    across_first = exchange(first, "chan", 2)
+    second = pick_records(records, (3, 0))
+    across_second = exchange(second, "chan", 2)
+    beside = exchange(records, "chan", 1)
+    weights = jnp.transpose(in_projection, (1, 0, 2))
+    gain = norm_gain.reshape(4, LANES)
+    skip = skip_gain.reshape(1, LANES)
+
+    diagonal_first = exchange(across_first, "chan", 1)
+    (to_two, to_one), query_first = project(
+        records, beside, across_first, diagonal_first, gain, weights, short_kernel, long_filter, (2, 1)
+    )
+    from_two = rotate(to_two, "seq", 2)
+    from_one = rotate(to_one, "seq", 1)
+    diagonal_second = exchange(across_second, "chan", 1)
+    (to_three, kept), query_second = project(
+        records, beside, across_second, diagonal_second, gain, weights, short_kernel, long_filter, (3, 0)
+    )
+    from_three = rotate(to_three, "seq", 3)
+
+    w_beside, w_far = pick_columns(out_projection)
+    w_beside = exchange(w_beside, "chan", 1)
+    w_far = exchange(w_far, "chan", 2)
+    w_diagonal = exchange(w_far, "chan", 1)
+
+    back_two, back_one, back_three, back_own = long_convolution(
+        (from_two, from_one, from_three, kept), (2, 1, 3, 0), short_kernel, skip
+    )
+    sums_two = rotate(back_two, "seq", 2)
+    sums_one = rotate(back_one, "seq", 1)
+    sums_three = rotate(back_three, "seq", 3)
+
+    def share(gated):
+        across = exchange(gated, "chan", 2)
+        return (gated, exchange(gated, "chan", 1), across, exchange(across, "chan", 1))
+
+    own = share(gate([back_own], [(query_second, 1)], short_kernel))
+    near = share(gate([sums_one, sums_three], [(query_second, 0), (query_first, 1)], short_kernel))
+    far = share(gate([sums_two], [(query_first, 0)], short_kernel))
+    return mix(
+        (own, near, far), (out_projection, w_beside, w_far, w_diagonal), ((0,), (3, 1), (2,)), block_len
     )
 
 
@@ -86,6 +384,20 @@
         P("chan"),
         P("chan", None),
     )
+
+    def body(records, norm_gain, in_projection, short_kernel, long_filter, skip_gain, out_projection):
+        count, block_len, channels = records.shape
+        fits = (
+            count == 4
+            and mesh.shape["seq"] == count
+            and mesh.shape["chan"] == 4
+            and channels == LANES
+            and block_len == 3 * LANES
+            and long_filter.shape[0] == 4
+        )
+        chosen = exchange_body if fits else ring_body
+        return chosen(records, norm_gain, in_projection, short_kernel, long_filter, skip_gain, out_projection)
+
     return jax.shard_map(
         body, mesh=mesh, in_specs=placed, out_specs=P("parts", "seq", "chan"), check_vma=False
     )

time: 203 us -> 60.8 us (0.30)
  waiting for transfers between devices: 100 us -> 28.6 us
  local copies, waits for them, and re-layouts: 28.4 us -> 2.05 us
  blocking collectives: 14.9 us -> 0 us
  starting transfers between devices: 34.6 us -> 20.1 us
  between operations: 13.6 us -> 0.14 us
  Pallas kernels: 0 us -> 9.69 us
  matrix products: 5.77 us -> 0 us
  other arithmetic: 4.91 us -> 0 us
    unnamed x3 -> x0, waiting for transfers between devices: 67.9 us -> none
    all_gather x1 -> x0, blocking collectives: 14.9 us -> none  [body(): all_taps = lax.all_gather(long_filter, 'seq', axis=1, tiled=True)]
    ppermute x4 -> x23, starting transfers between devices: 34.6 us -> 20.1 us  [the longest x6 10.3 us: rotate(): lax.ppermute(block, axis, [(i, (i + distance) % n) for i in range(n)])]
    unnamed x29 -> x16, local copies, waits for them, and re-layouts: 12.2 us -> 2.05 us
    pallas_call x0 -> x10, Pallas kernels: none -> 9.69 us  [the longest x8 6.35 us: vmem_call(): pl.pallas_call(kernel, out_shape=tuple(outs), in_specs=[pl.BlockSpec(memo...]
    all_gather x1 -> x0, waiting for transfers between devices: 8.44 us -> none  [body(): gathered = lax.all_gather(records, 'chan', axis=2, tiled=True)]
    reshape x2 -> x0, local copies, waits for them, and re-layouts: 7.64 us -> none  [the longest x1 6.49 us: block_terms(): toeplitz.reshape(filter_count, block_len, 2 * block_len - 1)]
    dot_general x3 -> x0, matrix products: 5.77 us -> none  [the longest x1 2.44 us: body(): jnp.einsum('rtd,dkc->rtkc', normed, in_projection, preferred_element_type...]
  transfers between devices with their start and end apart: 6 -> 23, of which waited for: 5 -> 11; matrix products, arithmetic and copies ran while one was open for 8% -> 0% of each run, Pallas kernels for 0% -> 6%
where the time goes in v1:
time: 60.8 us; the launch traced here: 60.6 us
  waiting for transfers between devices  28.6 us (47%)
  starting transfers between devices  20.1 us (33%)
  Pallas kernels  9.69 us (16%)
  local copies, waits for them, and re-layouts  2.05 us (3%)
    ppermute x17, waiting for transfers between devices, exchange(): lax.ppermute(block, axis, [(i, i ^ mask) for i in range(lax.axis_size(axi...  15.3 us
    ppermute x6, waiting for transfers between devices, rotate(): lax.ppermute(block, axis, [(i, (i + distance) % n) for i in range(n)])  13.3 us
    ppermute x6, starting transfers between devices, rotate(): lax.ppermute(block, axis, [(i, (i + distance) % n) for i in range(n)])  10.3 us
    ppermute x17, starting transfers between devices, exchange(): lax.ppermute(block, axis, [(i, i ^ mask) for i in range(lax.axis_size(axi...  9.75 us
    pallas_call x8, Pallas kernels, vmem_call(): pl.pallas_call(kernel, out_shape=tuple(outs), in_specs=[pl.BlockSpec(memo...  6.35 us
    pallas_call x2, Pallas kernels, pick_records(): pl.pallas_call(kernel, out_shape=jax.ShapeDtypeStruct((len(offsets), *rec...  3.34 us
    unnamed x16, local copies, waits for them, and re-layouts  2.05 us
  transfers between devices with their start and end apart: 23, of which 11 were waited for; matrix products, arithmetic and copies ran while one was open for 0% of the time, Pallas kernels for 6%

profile of v1, /device:TPU:0, one launch (start us, length us, event | category | flops | bytes accessed | tf_op | source)
XLA Modules:
  0.0 60.6 jit_solution(7909598762695505148)
XLA Ops:
  0.0 0.0 copy-start
  0.0 1.7 %shard_map.75 = bf16[2,384,128]{2,1,0:T(8,128)(2,1)} custom-call(bf16[4,384,128]{2,1,0:T(8,128)(2,1)} %own_ref.3), custom_call_target="tpu_custom_call" | custom-call | tf_op jit(solution)/shard_map/pallas_call | solution.py:120
  1.7 0.0 copy-start.1
  1.7 3.0 %collective-permute-start.5 = (bf16[2,384,128]{2,1,0:T(8,128)(2,1)}, bf16[2,384,128]{2,1,0:T(8,128)(2,1)S(1)}, u32[]{:S(2)}, u32[]{:S(2)}) collective-permute-start(bf16[2,384,128]{2,1,0:T(8,128)(2,1)} %shard_map.75), channel_id=1, source_target_pairs={{0,2},{1,3},{2,0},{3,1},{4,6},{5,7},{6,4},{7,5},{8,10},{9,11},{10,... | collective-permute-start | bytes 589832 | tf_op jit(solution)/shard_map/ppermute | solution.py:90
  4.7 0.0 copy-done
  4.7 0.0 collective-permute-start
  4.7 1.6 %shard_map.73 = bf16[2,384,128]{2,1,0:T(8,128)(2,1)} custom-call(bf16[4,384,128]{2,1,0:T(8,128)(2,1)} %own_ref.3), custom_call_target="tpu_custom_call" | custom-call | tf_op jit(solution)/shard_map/pallas_call | solution.py:120
  6.4 0.0 copy-start.5
  6.4 0.2 collective-permute-start.1
  6.6 3.8 %collective-permute-done.5.across_ref = bf16[2,384,128]{2,1,0:T(8,128)(2,1)S(1)} collective-permute-done((bf16[2,384,128]{2,1,0:T(8,128)(2,1)}, bf16[2,384,128]{2,1,0:T(8,128)(2,1)S(1)}, u32[]{:S(2)}, u32[]{:S(2)}) %collective-permute-start.5) | collective-permute-done | bytes 196640 | tf_op jit(solution)/shard_map/ppermute | solution.py:90
  10.4 0.0 collective-permute-start.6
  10.4 3.7 %collective-permute-done.1.across_ref = bf16[2,384,128]{2,1,0:T(8,128)(2,1)S(1)} collective-permute-done((bf16[2,384,128]{2,1,0:T(8,128)(2,1)}, bf16[2,384,128]{2,1,0:T(8,128)(2,1)S(1)}, u32[]{:S(2)}, u32[]{:S(2)}) %collective-permute-start.1) | collective-permute-done | bytes 196640 | tf_op jit(solution)/shard_map/ppermute | solution.py:90
  14.1 0.0 collective-permute-start.2
  14.1 0.0 collective-permute-done.6.diagonal_ref
  14.1 0.0 collective-permute-done.beside_ref
  14.1 0.0 copy-done.2
  14.1 0.0 copy-done.1
  14.1 0.0 copy-done.5
  14.1 0.0 copy-start.4
  14.1 0.7 %copy-done.4 = f32[3,3,128]{2,1,0:T(4,128)S(1)} copy-done((f32[3,3,128]{2,1,0:T(4,128)S(1)}, f32[3,3,128]{2,1,0:T(4,128)}, u32[]{:S(2)}) %copy-start.4) | copy-done | bytes 4632
  14.8 0.7 %copy-done.6 = f32[512]{0:T(512)S(1)} copy-done((f32[512]{0:T(512)S(1)}, f32[512]{0:T(512)}, u32[]{:S(2)}) %copy-start.6) | copy-done | bytes 2072
  15.5 0.9 %shard_map.76 = (bf16[416,128]{1,0:T(8,128)(2,1)S(1)}, bf16[416,128]{1,0:T(8,128)(2,1)S(1)}, f32[2,384,128]{2,1,0:T(8,128)S(1)}) custom-call(bf16[4,384,128]{2,1,0:T(8,128)(2,1)S(1)} %copy-done.1, bf16[4,384,128]{2,1,0:T(8,128)(2,1)S(1)} %collective-permute-done.beside_ref, bf16[2,384,128]{2,1,0:T(8,128)(2,1)S(1)} %collective-permute-done.5.across_ref, ...), custom_call_target="tpu_custom_call" | custom-call | flops 301989888 | bytes 2188800 | tf_op jit(solution)/shard_map/pallas_call | solution.py:95
  16.4 3.9 %collective-permute-start.7 = (bf16[416,128]{1,0:T(8,128)(2,1)S(1)}, bf16[416,128]{1,0:T(8,128)(2,1)S(1)}, u32[]{:S(2)}, u32[]{:S(2)}) collective-permute-start(bf16[416,128]{1,0:T(8,128)(2,1)S(1)} %get-tuple-element.19), channel_id=1, source_target_pairs={{0,12},{4,0},{8,4},{12,8},{1,13},{5,1},{9,5},{13,9},{2,14},{6,2},{... | collective-permute-start | bytes 319496 | tf_op jit(solution)/shard_map/ppermute | solution.py:86
  20.3 0.0 collective-permute-done.2.diagonal_ref
  20.3 0.9 %shard_map.74 = (bf16[416,128]{1,0:T(8,128)(2,1)S(1)}, bf16[416,128]{1,0:T(8,128)(2,1)S(1)}, f32[2,384,128]{2,1,0:T(8,128)S(1)}) custom-call(bf16[4,384,128]{2,1,0:T(8,128)(2,1)S(1)} %copy-done.1, bf16[4,384,128]{2,1,0:T(8,128)(2,1)S(1)} %collective-permute-done.beside_ref, bf16[2,384,128]{2,1,0:T(8,128)(2,1)S(1)} %collective-permute-done.1.across_ref, ...), custom_call_target="tpu_custom_call" | custom-call | flops 301989888 | bytes 2188800 | tf_op jit(solution)/shard_map/pallas_call | solution.py:95
  21.2 0.1 collective-permute-start.3
  21.3 1.0 %collective-permute-start.4 = (bf16[416,128]{1,0:T(8,128)(2,1)S(1)}, bf16[416,128]{1,0:T(8,128)(2,1)S(1)}, u32[]{:S(2)}, u32[]{:S(2)}) collective-permute-start(bf16[416,128]{1,0:T(8,128)(2,1)S(1)} %get-tuple-element.18), channel_id=1, source_target_pairs={{0,4},{4,8},{8,12},{12,0},{1,5},{5,9},{9,13},{13,1},{2,6},{6,10},{... | collective-permute-start | bytes 319496 | tf_op jit(solution)/shard_map/ppermute | solution.py:86
  22.3 1.3 %collective-permute-done.7.refs_2_ = bf16[416,128]{1,0:T(8,128)(2,1)S(1)} collective-permute-done((bf16[416,128]{1,0:T(8,128)(2,1)S(1)}, bf16[416,128]{1,0:T(8,128)(2,1)S(1)}, u32[]{:S(2)}, u32[]{:S(2)}) %collective-permute-start.7) | collective-permute-done | bytes 106528 | tf_op jit(solution)/shard_map/ppermute | solution.py:86
  23.6 7.3 %collective-permute-done.3.refs_0_ = bf16[416,128]{1,0:T(8,128)(2,1)S(1)} collective-permute-done((bf16[416,128]{1,0:T(8,128)(2,1)S(1)}, bf16[416,128]{1,0:T(8,128)(2,1)S(1)}, u32[]{:S(2)}, u32[]{:S(2)}) %collective-permute-start.3) | collective-permute-done | bytes 106528 | tf_op jit(solution)/shard_map/ppermute | solution.py:86
  30.9 0.0 collective-permute-done.4.refs_1_
  30.9 0.7 %copy-done.7 = f32[128]{0:T(128)S(1)} copy-done((f32[128]{0:T(128)S(1)}, f32[128]{0:T(128)}, u32[]{:S(2)}) %copy-start.7) | copy-done | bytes 536
  31.6 3.1 %shard_map.77 = (bf16[400,128]{1,0:T(8,128)(2,1)S(1)}, bf16[400,128]{1,0:T(8,128)(2,1)S(1)}, bf16[400,128]{1,0:T(8,128)(2,1)S(1)}, bf16[400,128]{1,0:T(8,128)(2,1)S(1)}) custom-call(bf16[416,128]{1,0:T(8,128)(2,1)S(1)} %collective-permute-done.3.refs_0_, bf16[416,128]{1,0:T(8,128)(2,1)S(1)} %collective-permute-done.4.refs_1_, ...), custom_call_target="tpu_custom_call" | custom-call | flops 1207959552 | bytes 840704 | tf_op jit(solution)/shard_map/pallas_call | solution.py:95
  34.7 0.6 %collective-permute-start.11 = (bf16[400,128]{1,0:T(8,128)(2,1)S(1)}, bf16[400,128]{1,0:T(8,128)(2,1)S(1)}, u32[]{:S(2)}, u32[]{:S(2)}) collective-permute-start(bf16[400,128]{1,0:T(8,128)(2,1)S(1)} %get-tuple-element.23), channel_id=1, source_target_pairs={{0,4},{4,8},{8,12},{12,0},{1,5},{5,9},{9,13},{13,1},{2,6},{6,10},{... | collective-permute-start | bytes 307208 | tf_op jit(solution)/shard_map/ppermute | solution.py:86
  35.3 3.3 %collective-permute-start.12 = (bf16[400,128]{1,0:T(8,128)(2,1)S(1)}, bf16[400,128]{1,0:T(8,128)(2,1)S(1)}, u32[]{:S(2)}, u32[]{:S(2)}) collective-permute-start(bf16[400,128]{1,0:T(8,128)(2,1)S(1)} %get-tuple-element.24), channel_id=1, source_target_pairs={{0,12},{4,0},{8,4},{12,8},{1,13},{5,1},{9,5},{13,9},{2,14},{6,2},{... | collective-permute-start | bytes 307208 | tf_op jit(solution)/shard_map/ppermute | solution.py:86
  38.6 3.7 %collective-permute-done.11.refs_0_ = bf16[400,128]{1,0:T(8,128)(2,1)S(1)} collective-permute-done((bf16[400,128]{1,0:T(8,128)(2,1)S(1)}, bf16[400,128]{1,0:T(8,128)(2,1)S(1)}, u32[]{:S(2)}, u32[]{:S(2)}) %collective-permute-start.11) | collective-permute-done | bytes 102432 | tf_op jit(solution)/shard_map/ppermute | solution.py:86
  42.3 0.5 collective-permute-done.12.refs_1_
  42.8 1.6 %collective-permute-start.14 = (bf16[768,128]{1,0:T(8,128)(2,1)S(1)}, bf16[768,128]{1,0:T(8,128)(2,1)S(1)}, u32[]{:S(2)}, u32[]{:S(2)}) collective-permute-start(bf16[768,128]{1,0:T(8,128)(2,1)S(1)} %shard_map.79.refs_4_), channel_id=1, source_target_pairs={{0,2},{1,3},{2,0},{3,1},{4,6},{5,7},{6,4},{7,5},{8,10},{9,11},{10,... | collective-permute-start | bytes 589832 | tf_op jit(solution)/shard_map/ppermute | solution.py:90
  44.4 0.0 copy-done.3
  44.4 0.9 %collective-permute-start.21 = (bf16[256,128]{1,0:T(8,128)(2,1)S(1)}, bf16[256,128]{1,0:T(8,128)(2,1)S(1)}, u32[]{:S(2)}, u32[]{:S(2)}) collective-permute-start(bf16[256,128]{1,0:T(8,128)(2,1)S(1)} %get-tuple-element.28), channel_id=1, source_target_pairs={{0,2},{1,3},{2,0},{3,1},{4,6},{5,7},{6,4},{7,5},{8,10},{9,11},{10,... | collective-permute-start | bytes 196616 | tf_op jit(solution)/shard_map/ppermute | solution.py:90
  45.3 1.5 %collective-permute-start.16 = (bf16[400,128]{1,0:T(8,128)(2,1)S(1)}, bf16[400,128]{1,0:T(8,128)(2,1)S(1)}, u32[]{:S(2)}, u32[]{:S(2)}) collective-permute-start(bf16[400,128]{1,0:T(8,128)(2,1)S(1)} %get-tuple-element.26), channel_id=1, source_target_pairs={{0,8},{4,12},{8,0},{12,4},{1,9},{5,13},{9,1},{13,5},{2,10},{6,14},... | collective-permute-start | bytes 307208 | tf_op jit(solution)/shard_map/ppermute | solution.py:86
  46.7 3.2 %collective-permute-done.21.refs_14_ = bf16[256,128]{1,0:T(8,128)(2,1)S(1)} collective-permute-done((bf16[256,128]{1,0:T(8,128)(2,1)S(1)}, bf16[256,128]{1,0:T(8,128)(2,1)S(1)}, u32[]{:S(2)}, u32[]{:S(2)}) %collective-permute-start.21) | collective-permute-done | bytes 65568 | tf_op jit(solution)/shard_map/ppermute | solution.py:90
  49.9 0.0 collective-permute-start.22
  50.0 0.5 collective-permute-start.20
  50.5 1.6 %collective-permute-start.9 = (bf16[384,128]{1,0:T(8,128)(2,1)S(1)}, bf16[384,128]{1,0:T(8,128)(2,1)S(1)}, u32[]{:S(2)}, u32[]{:S(2)}) collective-permute-start(bf16[384,128]{1,0:T(8,128)(2,1)S(1)} %shard_map.78.refs_0_), channel_id=1, source_target_pairs={{0,2},{1,3},{2,0},{3,1},{4,6},{5,7},{6,4},{7,5},{8,10},{9,11},{10,... | collective-permute-start | bytes 294920 | tf_op jit(solution)/shard_map/ppermute | solution.py:90
  52.1 0.4 collective-permute-done.16.refs_0_
  52.5 0.0 collective-permute-start.8
  52.5 0.0 collective-permute-done.20.refs_13_
  52.5 0.6 collective-permute-start.13
  53.1 0.0 collective-permute-done.22.refs_15_
  53.1 1.0 %collective-permute-start.18 = (bf16[384,128]{1,0:T(8,128)(2,1)S(1)}, bf16[384,128]{1,0:T(8,128)(2,1)S(1)}, u32[]{:S(2)}, u32[]{:S(2)}) collective-permute-start(bf16[384,128]{1,0:T(8,128)(2,1)S(1)} %shard_map.80.refs_8_), channel_id=1, source_target_pairs={{0,2},{1,3},{2,0},{3,1},{4,6},{5,7},{6,4},{7,5},{8,10},{9,11},{10,... | collective-permute-start | bytes 294920 | tf_op jit(solution)/shard_map/ppermute | solution.py:90
  54.1 0.0 collective-permute-done.14.refs_6_
  54.1 0.0 collective-permute-start.15
  54.1 1.2 %collective-permute-done.9.refs_2_ = bf16[384,128]{1,0:T(8,128)(2,1)S(1)} collective-permute-done((bf16[384,128]{1,0:T(8,128)(2,1)S(1)}, bf16[384,128]{1,0:T(8,128)(2,1)S(1)}, u32[]{:S(2)}, u32[]{:S(2)}) %collective-permute-start.9) | collective-permute-done | bytes 98336 | tf_op jit(solution)/shard_map/ppermute | solution.py:90
  55.3 0.0 collective-permute-start.10
  55.3 0.0 collective-permute-done.8.refs_1_
  55.3 0.5 collective-permute-start.17
  55.8 2.1 %collective-permute-done.18.refs_10_ = bf16[384,128]{1,0:T(8,128)(2,1)S(1)} collective-permute-done((bf16[384,128]{1,0:T(8,128)(2,1)S(1)}, bf16[384,128]{1,0:T(8,128)(2,1)S(1)}, u32[]{:S(2)}, u32[]{:S(2)}) %collective-permute-start.18) | collective-permute-done | bytes 98336 | tf_op jit(solution)/shard_map/ppermute | solution.py:90
  57.9 0.0 collective-permute-start.19
  57.9 0.0 collective-permute-done.10.refs_3_
  57.9 0.0 collective-permute-done.17.refs_9_
  57.9 0.0 collective-permute-done.13.refs_5_
  57.9 1.3 %collective-permute-done.19.refs_11_ = bf16[384,128]{1,0:T(8,128)(2,1)S(1)} collective-permute-done((bf16[384,128]{1,0:T(8,128)(2,1)S(1)}, bf16[384,128]{1,0:T(8,128)(2,1)S(1)}, u32[]{:S(2)}, u32[]{:S(2)}) %collective-permute-start.19) | collective-permute-done | bytes 98336 | tf_op jit(solution)/shard_map/ppermute | solution.py:90
  59.2 0.0 collective-permute-done.15.refs_7_
  59.2 1.3 %shard_map.82 = bf16[4,384,128]{2,1,0:T(8,128)(2,1)} custom-call(bf16[384,128]{1,0:T(8,128)(2,1)S(1)} %shard_map.78.refs_0_, bf16[384,128]{1,0:T(8,128)(2,1)S(1)} %collective-permute-done.8.refs_1_, bf16[384,128]{1,0:T(8,128)(2,1)S(1)} %collective-permute-done.9.refs_2_, bf16[384,128]{1,0:T(8,128)(2,1)S(1)} %collective-permute-done.10.refs_3_, ...), custom_call_target="tpu_custom_call" | custom-call | flops 201326592 | bytes 2260992 | tf_op jit(solution)/shard_map/pallas_call | solution.py:95
  (8 shorter events, 0.1 us)
Async XLA Ops:
  0.0 4.7 %copy-start = (bf16[4,384,128]{2,1,0:T(8,128)(2,1)S(1)}, bf16[4,384,128]{2,1,0:T(8,128)(2,1)}, u32[]{:S(2)}) copy-start(bf16[4,384,128]{2,1,0:T(8,128)(2,1)} %own_ref.3) | copy-start | bytes 1179652
  0.0 14.1 %copy-start.2 = (bf16[512,3,128]{2,0,1:T(8,128)(2,1)S(1)}, bf16[512,3,128]{2,0,1:T(8,128)(2,1)}, u32[]{:S(2)}) copy-start(bf16[512,3,128]{2,0,1:T(8,128)(2,1)} %param.9) | copy-start | bytes 1179652
  1.7 12.4 %copy-start.1 = (bf16[4,384,128]{2,1,0:T(8,128)(2,1)S(1)}, bf16[4,384,128]{2,1,0:T(8,128)(2,1)}, u32[]{:S(2)}) copy-start(bf16[4,384,128]{2,1,0:T(8,128)(2,1)} %own_ref.3) | copy-start | bytes 1179652
  1.7 8.6 %collective-permute-start.5 = (bf16[2,384,128]{2,1,0:T(8,128)(2,1)}, bf16[2,384,128]{2,1,0:T(8,128)(2,1)S(1)}, u32[]{:S(2)}, u32[]{:S(2)}) collective-permute-start(bf16[2,384,128]{2,1,0:T(8,128)(2,1)} %shard_map.75), channel_id=1, source_target_pairs={{0,2},{1,3},{2,0},{3,1},{4,6},{5,7},{6,4},{7,5},{8,10},{9,11},{10,... | collective-permute-start | bytes 589832 | tf_op jit(solution)/shard_map/ppermute | solution.py:90
  4.7 9.3 %collective-permute-start = (bf16[4,384,128]{2,1,0:T(8,128)(2,1)S(1)}, bf16[4,384,128]{2,1,0:T(8,128)(2,1)S(1)}, u32[]{:S(2)}, u32[]{:S(2)}) collective-permute-start(bf16[4,384,128]{2,1,0:T(8,128)(2,1)S(1)} %copy-done), channel_id=1, source_target_pairs={{0,1},{1,0},{2,3},{3,2},{4,5},{5,4},{6,7},{7,6},{8,9},{9,8},{10,11... | collective-permute-start | bytes 1179656 | tf_op jit(solution)/shard_map/ppermute | solution.py:90
  6.4 7.7 %copy-start.5 = (bf16[4,384]{1,0:T(4,128)(2,1)S(1)}, bf16[4,384]{1,0:T(4,128)(2,1)}, u32[]{:S(2)}) copy-start(bf16[4,384]{1,0:T(4,128)(2,1)} %taps_ref.3) | copy-start | bytes 9220
  6.4 7.7 %collective-permute-start.1 = (bf16[2,384,128]{2,1,0:T(8,128)(2,1)}, bf16[2,384,128]{2,1,0:T(8,128)(2,1)S(1)}, u32[]{:S(2)}, u32[]{:S(2)}) collective-permute-start(bf16[2,384,128]{2,1,0:T(8,128)(2,1)} %shard_map.73), channel_id=1, source_target_pairs={{0,2},{1,3},{2,0},{3,1},{4,6},{5,7},{6,4},{7,5},{8,10},{9,11},{10,... | collective-permute-start | bytes 589832 | tf_op jit(solution)/shard_map/ppermute | solution.py:90
  10.4 3.7 %collective-permute-start.6 = (bf16[2,384,128]{2,1,0:T(8,128)(2,1)S(1)}, bf16[2,384,128]{2,1,0:T(8,128)(2,1)S(1)}, u32[]{:S(2)}, u32[]{:S(2)}) collective-permute-start(bf16[2,384,128]{2,1,0:T(8,128)(2,1)S(1)} %collective-permute-done.5.across_ref), channel_id=1, source_target_pairs={{0,1},{1,0},{2,3},{3,2},{4,5},{5,4},{6,7},{7,6},{8,9},{9,8},{10,11... | collective-permute-start | bytes 589832 | tf_op jit(solution)/shard_map/ppermute | solution.py:90
  14.1 6.2 %collective-permute-start.2 = (bf16[2,384,128]{2,1,0:T(8,128)(2,1)S(1)}, bf16[2,384,128]{2,1,0:T(8,128)(2,1)S(1)}, u32[]{:S(2)}, u32[]{:S(2)}) collective-permute-start(bf16[2,384,128]{2,1,0:T(8,128)(2,1)S(1)} %collective-permute-done.1.across_ref), channel_id=1, source_target_pairs={{0,1},{1,0},{2,3},{3,2},{4,5},{5,4},{6,7},{7,6},{8,9},{9,8},{10,11... | collective-permute-start | bytes 589832 | tf_op jit(solution)/shard_map/ppermute | solution.py:90
  14.1 0.7 %copy-start.4 = (f32[3,3,128]{2,1,0:T(4,128)S(1)}, f32[3,3,128]{2,1,0:T(4,128)}, u32[]{:S(2)}) copy-start(f32[3,3,128]{2,1,0:T(4,128)} %refs_2_.3) | copy-start | bytes 13828
  14.8 0.7 %copy-start.6 = (f32[512]{0:T(512)S(1)}, f32[512]{0:T(512)}, u32[]{:S(2)}) copy-start(f32[512]{0:T(512)} %param.8) | copy-start | bytes 6148
  16.4 7.2 %collective-permute-start.7 = (bf16[416,128]{1,0:T(8,128)(2,1)S(1)}, bf16[416,128]{1,0:T(8,128)(2,1)S(1)}, u32[]{:S(2)}, u32[]{:S(2)}) collective-permute-start(bf16[416,128]{1,0:T(8,128)(2,1)S(1)} %get-tuple-element.19), channel_id=1, source_target_pairs={{0,12},{4,0},{8,4},{12,8},{1,13},{5,1},{9,5},{13,9},{2,14},{6,2},{... | collective-permute-start | bytes 319496 | tf_op jit(solution)/shard_map/ppermute | solution.py:86
  21.2 9.7 %collective-permute-start.3 = (bf16[416,128]{1,0:T(8,128)(2,1)S(1)}, bf16[416,128]{1,0:T(8,128)(2,1)S(1)}, u32[]{:S(2)}, u32[]{:S(2)}) collective-permute-start(bf16[416,128]{1,0:T(8,128)(2,1)S(1)} %get-tuple-element.17), channel_id=1, source_target_pairs={{0,8},{4,12},{8,0},{12,4},{1,9},{5,13},{9,1},{13,5},{2,10},{6,14},... | collective-permute-start | bytes 319496 | tf_op jit(solution)/shard_map/ppermute | solution.py:86
  21.3 9.7 %collective-permute-start.4 = (bf16[416,128]{1,0:T(8,128)(2,1)S(1)}, bf16[416,128]{1,0:T(8,128)(2,1)S(1)}, u32[]{:S(2)}, u32[]{:S(2)}) collective-permute-start(bf16[416,128]{1,0:T(8,128)(2,1)S(1)} %get-tuple-element.18), channel_id=1, source_target_pairs={{0,4},{4,8},{8,12},{12,0},{1,5},{5,9},{9,13},{13,1},{2,6},{6,10},{... | collective-permute-start | bytes 319496 | tf_op jit(solution)/shard_map/ppermute | solution.py:86
  30.9 0.7 %copy-start.7 = (f32[128]{0:T(128)S(1)}, f32[128]{0:T(128)}, u32[]{:S(2)}) copy-start(f32[128]{0:T(128)} %param.12) | copy-start | bytes 1540
  34.7 7.6 %collective-permute-start.11 = (bf16[400,128]{1,0:T(8,128)(2,1)S(1)}, bf16[400,128]{1,0:T(8,128)(2,1)S(1)}, u32[]{:S(2)}, u32[]{:S(2)}) collective-permute-start(bf16[400,128]{1,0:T(8,128)(2,1)S(1)} %get-tuple-element.23), channel_id=1, source_target_pairs={{0,4},{4,8},{8,12},{12,0},{1,5},{5,9},{9,13},{13,1},{2,6},{6,10},{... | collective-permute-start | bytes 307208 | tf_op jit(solution)/shard_map/ppermute | solution.py:86
  35.3 7.5 %collective-permute-start.12 = (bf16[400,128]{1,0:T(8,128)(2,1)S(1)}, bf16[400,128]{1,0:T(8,128)(2,1)S(1)}, u32[]{:S(2)}, u32[]{:S(2)}) collective-permute-start(bf16[400,128]{1,0:T(8,128)(2,1)S(1)} %get-tuple-element.24), channel_id=1, source_target_pairs={{0,12},{4,0},{8,4},{12,8},{1,13},{5,1},{9,5},{13,9},{2,14},{6,2},{... | collective-permute-start | bytes 307208 | tf_op jit(solution)/shard_map/ppermute | solution.py:86
  42.8 1.6 %copy-start.3 = (bf16[128,512]{1,0:T(8,128)(2,1)S(1)}, bf16[128,512]{1,0:T(8,128)(2,1)}, u32[]{:S(2)}) copy-start(bf16[128,512]{1,0:T(8,128)(2,1)} %refs_12_.1) | copy-start | bytes 393220
  42.8 11.3 %collective-permute-start.14 = (bf16[768,128]{1,0:T(8,128)(2,1)S(1)}, bf16[768,128]{1,0:T(8,128)(2,1)S(1)}, u32[]{:S(2)}, u32[]{:S(2)}) collective-permute-start(bf16[768,128]{1,0:T(8,128)(2,1)S(1)} %shard_map.79.refs_4_), channel_id=1, source_target_pairs={{0,2},{1,3},{2,0},{3,1},{4,6},{5,7},{6,4},{7,5},{8,10},{9,11},{10,... | collective-permute-start | bytes 589832 | tf_op jit(solution)/shard_map/ppermute | solution.py:90
  44.4 5.5 %collective-permute-start.21 = (bf16[256,128]{1,0:T(8,128)(2,1)S(1)}, bf16[256,128]{1,0:T(8,128)(2,1)S(1)}, u32[]{:S(2)}, u32[]{:S(2)}) collective-permute-start(bf16[256,128]{1,0:T(8,128)(2,1)S(1)} %get-tuple-element.28), channel_id=1, source_target_pairs={{0,2},{1,3},{2,0},{3,1},{4,6},{5,7},{6,4},{7,5},{8,10},{9,11},{10,... | collective-permute-start | bytes 196616 | tf_op jit(solution)/shard_map/ppermute | solution.py:90
  45.3 7.2 %collective-permute-start.16 = (bf16[400,128]{1,0:T(8,128)(2,1)S(1)}, bf16[400,128]{1,0:T(8,128)(2,1)S(1)}, u32[]{:S(2)}, u32[]{:S(2)}) collective-permute-start(bf16[400,128]{1,0:T(8,128)(2,1)S(1)} %get-tuple-element.26), channel_id=1, source_target_pairs={{0,8},{4,12},{8,0},{12,4},{1,9},{5,13},{9,1},{13,5},{2,10},{6,14},... | collective-permute-start | bytes 307208 | tf_op jit(solution)/shard_map/ppermute | solution.py:86
  49.9 3.2 %collective-permute-start.22 = (bf16[256,128]{1,0:T(8,128)(2,1)S(1)}, bf16[256,128]{1,0:T(8,128)(2,1)S(1)}, u32[]{:S(2)}, u32[]{:S(2)}) collective-permute-start(bf16[256,128]{1,0:T(8,128)(2,1)S(1)} %collective-permute-done.21.refs_14_), channel_id=1, source_target_pairs={{0,1},{1,0},{2,3},{3,2},{4,5},{5,4},{6,7},{7,6},{8,9},{9,8},{10,11... | collective-permute-start | bytes 196616 | tf_op jit(solution)/shard_map/ppermute | solution.py:90
  50.0 2.6 %collective-permute-start.20 = (bf16[128,128]{1,0:T(8,128)(2,1)S(1)}, bf16[128,128]{1,0:T(8,128)(2,1)S(1)}, u32[]{:S(2)}, u32[]{:S(2)}) collective-permute-start(bf16[128,128]{1,0:T(8,128)(2,1)S(1)} %get-tuple-element.27), channel_id=1, source_target_pairs={{0,1},{1,0},{2,3},{3,2},{4,5},{5,4},{6,7},{7,6},{8,9},{9,8},{10,11... | collective-permute-start | bytes 98312 | tf_op jit(solution)/shard_map/ppermute | solution.py:90
  50.5 4.8 %collective-permute-start.9 = (bf16[384,128]{1,0:T(8,128)(2,1)S(1)}, bf16[384,128]{1,0:T(8,128)(2,1)S(1)}, u32[]{:S(2)}, u32[]{:S(2)}) collective-permute-start(bf16[384,128]{1,0:T(8,128)(2,1)S(1)} %shard_map.78.refs_0_), channel_id=1, source_target_pairs={{0,2},{1,3},{2,0},{3,1},{4,6},{5,7},{6,4},{7,5},{8,10},{9,11},{10,... | collective-permute-start | bytes 294920 | tf_op jit(solution)/shard_map/ppermute | solution.py:90
  52.5 2.8 %collective-permute-start.8 = (bf16[384,128]{1,0:T(8,128)(2,1)S(1)}, bf16[384,128]{1,0:T(8,128)(2,1)S(1)}, u32[]{:S(2)}, u32[]{:S(2)}) collective-permute-start(bf16[384,128]{1,0:T(8,128)(2,1)S(1)} %shard_map.78.refs_0_), channel_id=1, source_target_pairs={{0,1},{1,0},{2,3},{3,2},{4,5},{5,4},{6,7},{7,6},{8,9},{9,8},{10,11... | collective-permute-start | bytes 294920 | tf_op jit(solution)/shard_map/ppermute | solution.py:90
  52.5 5.4 %collective-permute-start.13 = (bf16[768,128]{1,0:T(8,128)(2,1)S(1)}, bf16[768,128]{1,0:T(8,128)(2,1)S(1)}, u32[]{:S(2)}, u32[]{:S(2)}) collective-permute-start(bf16[768,128]{1,0:T(8,128)(2,1)S(1)} %shard_map.79.refs_4_), channel_id=1, source_target_pairs={{0,1},{1,0},{2,3},{3,2},{4,5},{5,4},{6,7},{7,6},{8,9},{9,8},{10,11... | collective-permute-start | bytes 589832 | tf_op jit(solution)/shard_map/ppermute | solution.py:90
  53.1 4.8 %collective-permute-start.18 = (bf16[384,128]{1,0:T(8,128)(2,1)S(1)}, bf16[384,128]{1,0:T(8,128)(2,1)S(1)}, u32[]{:S(2)}, u32[]{:S(2)}) collective-permute-start(bf16[384,128]{1,0:T(8,128)(2,1)S(1)} %shard_map.80.refs_8_), channel_id=1, source_target_pairs={{0,2},{1,3},{2,0},{3,1},{4,6},{5,7},{6,4},{7,5},{8,10},{9,11},{10,... | collective-permute-start | bytes 294920 | tf_op jit(solution)/shard_map/ppermute | solution.py:90
  54.1 5.1 %collective-permute-start.15 = (bf16[768,128]{1,0:T(8,128)(2,1)S(1)}, bf16[768,128]{1,0:T(8,128)(2,1)S(1)}, u32[]{:S(2)}, u32[]{:S(2)}) collective-permute-start(bf16[768,128]{1,0:T(8,128)(2,1)S(1)} %collective-permute-done.14.refs_6_), channel_id=1, source_target_pairs={{0,1},{1,0},{2,3},{3,2},{4,5},{5,4},{6,7},{7,6},{8,9},{9,8},{10,11... | collective-permute-start | bytes 589832 | tf_op jit(solution)/shard_map/ppermute | solution.py:90
  55.3 2.7 %collective-permute-start.10 = (bf16[384,128]{1,0:T(8,128)(2,1)S(1)}, bf16[384,128]{1,0:T(8,128)(2,1)S(1)}, u32[]{:S(2)}, u32[]{:S(2)}) collective-permute-start(bf16[384,128]{1,0:T(8,128)(2,1)S(1)} %collective-permute-done.9.refs_2_), channel_id=1, source_target_pairs={{0,1},{1,0},{2,3},{3,2},{4,5},{5,4},{6,7},{7,6},{8,9},{9,8},{10,11... | collective-permute-start | bytes 294920 | tf_op jit(solution)/shard_map/ppermute | solution.py:90
  55.3 2.7 %collective-permute-start.17 = (bf16[384,128]{1,0:T(8,128)(2,1)S(1)}, bf16[384,128]{1,0:T(8,128)(2,1)S(1)}, u32[]{:S(2)}, u32[]{:S(2)}) collective-permute-start(bf16[384,128]{1,0:T(8,128)(2,1)S(1)} %shard_map.80.refs_8_), channel_id=1, source_target_pairs={{0,1},{1,0},{2,3},{3,2},{4,5},{5,4},{6,7},{7,6},{8,9},{9,8},{10,11... | collective-permute-start | bytes 294920 | tf_op jit(solution)/shard_map/ppermute | solution.py:90
  57.9 1.3 %collective-permute-start.19 = (bf16[384,128]{1,0:T(8,128)(2,1)S(1)}, bf16[384,128]{1,0:T(8,128)(2,1)S(1)}, u32[]{:S(2)}, u32[]{:S(2)}) collective-permute-start(bf16[384,128]{1,0:T(8,128)(2,1)S(1)} %collective-permute-done.18.refs_10_), channel_id=1, source_target_pairs={{0,1},{1,0},{2,3},{3,2},{4,5},{5,4},{6,7},{7,6},{8,9},{9,8},{10,11... | collective-permute-start | bytes 294920 | tf_op jit(solution)/shard_map/ppermute | solution.py:90

commit v2 on v1

--- a/solution.py
+++ b/solution.py
@@ -7,6 +7,10 @@
 
 LANES = 128
 EXTRA = 32
+SPLIT = 2
+SPACE = 1 << 30
+FAR = 1 << 33
+COST = pl.CostEstimate(flops=0, bytes_accessed=0, transcendentals=0)
 BACK = 16
 VMEM = pltpu.VMEM
 
@@ -90,8 +94,7 @@
     return lax.ppermute(block, axis, [(i, i ^ mask) for i in range(lax.axis_size(axis))])
 
 
-def vmem_call(kernel, outs, scratch, flops, *operands):
-    moved = sum(x.size * x.dtype.itemsize for x in (*operands, *outs))
+def vmem_call(kernel, outs, scratch, *operands, cost=0):
     return pl.pallas_call(
         kernel,
         out_shape=tuple(outs),
@@ -99,54 +102,54 @@
         out_specs=tuple(pl.BlockSpec(memory_space=VMEM) for _ in outs),
         scratch_shapes=scratch,
         compiler_params=pltpu.CompilerParams(vmem_limit_bytes=40 * 1024 * 1024),
-        cost_estimate=pl.CostEstimate(flops=flops, bytes_accessed=moved, transcendentals=0),
+        cost_estimate=pl.CostEstimate(flops=cost, bytes_accessed=0, transcendentals=0),
     )(*operands)
 
 
-def pick_records(records, offsets):
-    count = records.shape[0]
-
-    def kernel(records_ref, out_ref, sems):
+def after(value, *done):
+    return lax.optimization_barrier((value, *done))[0]
+
+
+def pick(records, groups):
+    count, block_len, _ = records.shape
+    flat = [len(group) * block_len for group in groups]
+
+    def kernel(records_ref, *rest):
+        out_refs, sems = rest[:-1], rest[-1]
         z = lax.axis_index("seq")
-        copies = [
-            pltpu.make_async_copy(records_ref.at[lax.rem(z + k, count)], out_ref.at[i], sems.at[i])
-            for i, k in enumerate(offsets)
-        ]
+        copies = []
+        for ref, group in zip(out_refs, groups):
+            for i, k in enumerate(group):
+                place = ref.at[pl.ds(i * block_len, block_len)]
+                copies.append(
+                    pltpu.make_async_copy(records_ref.at[lax.rem(z + k, count)], place, sems.at[len(copies)])
+                )
         for copy in copies:
             copy.start()
         for copy in copies:
             copy.wait()
 
+    shapes = [VMEM((n, LANES), records.dtype) for n in flat]
     return pl.pallas_call(
         kernel,
-        out_shape=jax.ShapeDtypeStruct((len(offsets), *records.shape[1:]), records.dtype),
+        out_shape=tuple(shapes),
         in_specs=[pl.BlockSpec(memory_space=pl.ANY)],
-        out_specs=pl.BlockSpec(memory_space=VMEM),
-        scratch_shapes=[pltpu.SemaphoreType.DMA((len(offsets),))],
+        out_specs=tuple(pl.BlockSpec(memory_space=VMEM) for _ in shapes),
+        scratch_shapes=[pltpu.SemaphoreType.DMA((count,))],
+        cost_estimate=COST,
     )(records)
 
 
-def pick_columns(out_projection):
-    rows = out_projection.shape[0]
-
-    def kernel(w_ref, one_ref, two_ref):
-        me = lax.axis_index("chan")
-        for mask, ref, start in ((1, one_ref, 0), (2, two_ref, 0), (3, two_ref, rows)):
-            first = pl.multiple_of(jnp.bitwise_xor(me, mask) * LANES, LANES)
-            ref[start : start + rows, :] = w_ref[:, pl.ds(first, LANES)]
-
-    shape = lambda n: jax.ShapeDtypeStruct((n, LANES), out_projection.dtype)
-    return vmem_call(kernel, [shape(rows), shape(2 * rows)], [], 0, out_projection)
-
-
-def project(records, beside, across, diagonal, norm_gain, weights, short_kernel, taps, offsets):
-    count, block_len, _ = records.shape
+def project(own, beside, across, diagonal, norm_gain, weights, short_kernel, taps, offsets):
+    count, block_len, _ = beside.shape
     picked = len(offsets)
     depth = weights.shape[1]
     f32, bf16 = jnp.float32, jnp.bfloat16
 
-    def kernel(own_ref, beside_ref, across_ref, diagonal_ref, gain_ref, w_ref, short_ref, taps_ref, *rest):
+    def kernel(own_ref, beside_ref, across_ref, gain_ref, w_ref, short_ref, taps_ref, *rest):
+        diagonal_refs, rest = rest[: len(diagonal)], rest[len(diagonal) :]
         chunk_refs, (query_ref, w_all, shifted) = rest[:picked], rest[picked:]
+        per = len(diagonal) // picked
         me = lax.axis_index("chan")
         z = lax.axis_index("seq")
         for j in range(4):
@@ -166,7 +169,9 @@
         ]
         for i, k in enumerate(offsets):
             rec = lax.rem(z + k, count)
-            slabs = [own_ref[rec], beside_ref[rec], across_ref[i], diagonal_ref[i]]
+            rows = slice(i * block_len, (i + 1) * block_len)
+            pieces = [ref[...] for ref in diagonal_refs[i * per : (i + 1) * per]]
+            slabs = [own_ref[rows, :], beside_ref[rec], across_ref[rows, :], jnp.concatenate(pieces, axis=0)]
             slabs = [s.astype(f32) for s in slabs]
             squares = slabs[0] * slabs[0]
             for s in slabs[1:]:
@@ -198,13 +203,20 @@
     query = jax.ShapeDtypeStruct((picked, block_len, LANES), f32)
     scratch = [pltpu.VMEM((4 * LANES, 3 * LANES), bf16), pltpu.VMEM((8 + block_len, 3 * LANES), f32)]
     out = vmem_call(
-        kernel, [chunk] * picked + [query], scratch, 2 * picked * block_len * 512 * 384,
-        records, beside, across, diagonal, norm_gain, weights, short_kernel, taps,
+        kernel, [chunk] * picked + [query], scratch,
+        own, beside, across, norm_gain, weights, short_kernel, taps, *diagonal,
     )
     return out[:picked], out[picked]
 
 
-def long_convolution(chunks, distances, short_kernel, skip_gain):
+def tail_rows(block, cost):
+    def kernel(block_ref, out_ref):
+        out_ref[...] = block_ref[-EXTRA:, :]
+
+    return vmem_call(kernel, [jax.ShapeDtypeStruct((EXTRA, LANES), block.dtype)], [], block, cost=cost)[0]
+
+
+def long_convolution(chunks, distances, first_tail, short_kernel, skip_gain):
     n = len(chunks)
     block_len = chunks[0].shape[0] - EXTRA
     length = n * block_len
@@ -212,11 +224,12 @@
     f32, bf16 = jnp.float32, jnp.bfloat16
 
     def kernel(*refs):
-        chunk_refs, (short_ref, skip_ref), out_refs = refs[:n], refs[n : n + 2], refs[n + 2 : 2 * n + 2]
-        inputs, source, bands, sums = refs[2 * n + 2 :]
+        chunk_refs, (tail_ref, short_ref, skip_ref), out_refs = refs[:n], refs[n : n + 3], refs[n + 3 : 2 * n + 3]
+        inputs, source, bands, sums = refs[2 * n + 3 :]
         z = lax.axis_index("seq")
         for ref, k in zip(chunk_refs, distances):
             inputs[lax.rem(z - k + n, n)] = ref[...]
+        inputs[lax.rem(z - distances[0] + n, n), block_len:, :] = tail_ref[...]
         lane = lax.broadcasted_iota(jnp.int32, (LANES, LANES), 1)
         tap_rows = [inputs[q, block_len : block_len + 4 * pieces, :].astype(f32) for q in range(n)]
         for f in range(4):
@@ -273,10 +286,10 @@
         pltpu.VMEM((4 * LANES, length + LANES), bf16),
         pltpu.VMEM((n, block_len + BACK, LANES), bf16),
     ]
-    return vmem_call(kernel, [back] * n, scratch, 4 * length * length * LANES, *chunks, short_kernel, skip_gain)
-
-
-def gate(sums, queries, short_kernel):
+    return vmem_call(kernel, [back] * n, scratch, *chunks, first_tail, short_kernel, skip_gain)
+
+
+def gate(sums, queries, short_kernel, out_projection=None, cost=0):
     block_len = sums[0].shape[0] - BACK
     n = len(sums)
     f32, bf16 = jnp.float32, jnp.bfloat16
@@ -286,8 +299,17 @@
             arrays.append(array)
     places = [([a is array for a in arrays].index(True), index) for array, index in queries]
 
+    masks = [()] if out_projection is None else [(2, 3), (1,)]
+
     def kernel(*refs):
-        sum_refs, query_refs, short_ref, out_ref = refs[:n], refs[n:-2], refs[-2], refs[-1]
+        sum_refs, query_refs = refs[:n], refs[n : n + len(arrays)]
+        short_ref, w_refs, out_refs = refs[n + len(arrays)], refs[n + len(arrays) + 1 : -len(masks)], refs[-len(masks) :]
+        me = lax.axis_index("chan")
+        for ref, targets in zip(out_refs, masks):
+            for i, mask in enumerate(targets):
+                first = pl.multiple_of(jnp.bitwise_xor(me, mask) * LANES, LANES)
+                start = n * block_len + i * LANES
+                ref[start : start + LANES, :] = w_refs[0][:, pl.ds(first, LANES)]
         for i, (a, index) in enumerate(places):
             tail = sum_refs[i][block_len:, :].astype(f32)
             k1, k2 = short_ref[1, 0:1, :], short_ref[2, 0:1, :]
@@ -295,26 +317,28 @@
             query = query_refs[a][index]
             query = jnp.concatenate([query[0:8] + jnp.concatenate(rim, axis=0), query[8:]], axis=0)
             out = query * sum_refs[i][0:block_len, :].astype(f32)
-            out_ref[i * block_len : (i + 1) * block_len, :] = out.astype(bf16)
-
-    out = jax.ShapeDtypeStruct((n * block_len, LANES), bf16)
-    return vmem_call(kernel, [out], [], 0, *sums, *arrays, short_kernel)[0]
-
-
-def mix(slabs, weights, distances, block_len):
+            for ref in out_refs:
+                ref[i * block_len : (i + 1) * block_len, :] = out.astype(bf16)
+
+    outs = [jax.ShapeDtypeStruct((n * block_len + len(m) * LANES, LANES), bf16) for m in masks]
+    extra = [] if out_projection is None else [out_projection]
+    return vmem_call(kernel, outs, [], *sums, *arrays, short_kernel, *extra, cost=cost)
+
+
+def mix(slabs, out_projection, distances, block_len):
     f32, bf16 = jnp.float32, jnp.bfloat16
     count = sum(len(d) for d in distances)
     groups = len(slabs)
 
     def kernel(*refs):
-        slab_refs, (own_ref, beside_ref, far_ref, diagonal_ref) = refs[: 4 * groups], refs[4 * groups : 4 * groups + 4]
-        out_ref, w_all = refs[-2:]
+        slab_refs, (w_ref, out_ref, w_all) = refs[: 4 * groups], refs[4 * groups :]
         me = lax.axis_index("chan")
         z = lax.axis_index("seq")
-        w_all[0:LANES, :] = own_ref[:, pl.ds(pl.multiple_of(me * LANES, LANES), LANES)]
-        w_all[LANES : 2 * LANES, :] = beside_ref[...]
-        w_all[2 * LANES : 3 * LANES, :] = far_ref[0:LANES, :]
-        w_all[3 * LANES :, :] = diagonal_ref[LANES:, :]
+        start = len(distances[0]) * block_len
+        w_all[0:LANES, :] = w_ref[:, pl.ds(pl.multiple_of(me * LANES, LANES), LANES)]
+        w_all[LANES : 2 * LANES, :] = slab_refs[1][start : start + LANES, :]
+        w_all[2 * LANES : 3 * LANES, :] = slab_refs[2][start : start + LANES, :]
+        w_all[3 * LANES :, :] = slab_refs[3][start + LANES : start + 2 * LANES, :]
         for g in range(groups):
             for i, k in enumerate(distances[g]):
                 rows = slice(i * block_len, (i + 1) * block_len)
@@ -322,56 +346,55 @@
                 out_ref[lax.rem(z + k, count)] = jnp.dot(lhs, w_all[...], preferred_element_type=f32).astype(bf16)
 
     out = jax.ShapeDtypeStruct((count, block_len, LANES), bf16)
-    operands = [x for slab in slabs for x in slab] + list(weights)
-    scratch = [pltpu.VMEM((4 * LANES, LANES), bf16)]
-    return vmem_call(kernel, [out], scratch, 2 * count * block_len * 512 * LANES, *operands)[0]
+    operands = [x for slab in slabs for x in slab] + [out_projection]
+    return vmem_call(kernel, [out], [pltpu.VMEM((4 * LANES, LANES), bf16)], *operands)[0]
 
 
 def exchange_body(records, norm_gain, in_projection, short_kernel, long_filter, skip_gain, out_projection):
     block_len = records.shape[1]
-    first = pick_records(records, (2, 1))
-    across_first = exchange(first, "chan", 2)
-    second = pick_records(records, (3, 0))
-    across_second = exchange(second, "chan", 2)
-    beside = exchange(records, "chan", 1)
     weights = jnp.transpose(in_projection, (1, 0, 2))
     gain = norm_gain.reshape(4, LANES)
     skip = skip_gain.reshape(1, LANES)
 
-    diagonal_first = exchange(across_first, "chan", 1)
-    (to_two, to_one), query_first = project(
-        records, beside, across_first, diagonal_first, gain, weights, short_kernel, long_filter, (2, 1)
-    )
+    groups = ((2,), (1, 3, 0))
+    picked = pick(records, groups)
+    across = [exchange(block, "chan", 2) for block in picked]
+    beside = exchange(records, "chan", 1)
+    def projected(g, far):
+        pieces = SPLIT * len(groups[g])
+        size = far.shape[0] // pieces
+        diagonal = [exchange(far[i * size : (i + 1) * size], "chan", 1) for i in range(pieces)]
+        return project(
+            picked[g], beside, far, diagonal, gain, weights, short_kernel, long_filter, groups[g]
+        )
+
+    (to_two,), query_two = projected(0, across[0])
     from_two = rotate(to_two, "seq", 2)
+    (to_one, to_three, kept), query_rest = projected(1, after(across[1], to_two))
     from_one = rotate(to_one, "seq", 1)
-    diagonal_second = exchange(across_second, "chan", 1)
-    (to_three, kept), query_second = project(
-        records, beside, across_second, diagonal_second, gain, weights, short_kernel, long_filter, (3, 0)
-    )
     from_three = rotate(to_three, "seq", 3)
 
-    w_beside, w_far = pick_columns(out_projection)
-    w_beside = exchange(w_beside, "chan", 1)
-    w_far = exchange(w_far, "chan", 2)
-    w_diagonal = exchange(w_far, "chan", 1)
-
     back_two, back_one, back_three, back_own = long_convolution(
-        (from_two, from_one, from_three, kept), (2, 1, 3, 0), short_kernel, skip
+        (from_two, from_one, from_three, kept),
+        (2, 1, 3, 0),
+        tail_rows(from_two, SPACE),
+        short_kernel,
+        skip,
     )
     sums_two = rotate(back_two, "seq", 2)
     sums_one = rotate(back_one, "seq", 1)
     sums_three = rotate(back_three, "seq", 3)
 
-    def share(gated):
-        across = exchange(gated, "chan", 2)
-        return (gated, exchange(gated, "chan", 1), across, exchange(across, "chan", 1))
-
-    own = share(gate([back_own], [(query_second, 1)], short_kernel))
-    near = share(gate([sums_one, sums_three], [(query_second, 0), (query_first, 1)], short_kernel))
-    far = share(gate([sums_two], [(query_first, 0)], short_kernel))
-    return mix(
-        (own, near, far), (out_projection, w_beside, w_far, w_diagonal), ((0,), (3, 1), (2,)), block_len
-    )
+    own, own_beside = gate([back_own], [(query_rest, 2)], short_kernel, out_projection)
+    own_over = exchange(own, "chan", 2)
+    (near,) = gate([after(sums_one, own), after(sums_three, own)], [(query_rest, 1), (query_rest, 0)], short_kernel)
+    (far,) = gate([after(sums_two, near, own_over)], [(query_two, 0)], short_kernel, cost=FAR)
+    slabs = []
+    for gated, beside, over in ((own, own_beside, own_over), (near, near, None), (far, far, None)):
+        if over is None:
+            over = exchange(gated, "chan", 2)
+        slabs.append((gated, exchange(beside, "chan", 1), over, exchange(after(over, far), "chan", 1)))
+    return mix(slabs, out_projection, ((0,), (3, 1), (2,)), block_len)
 
 
 def solution(mesh):

time: 60.8 us -> 52.1 us (0.86)
  waiting for transfers between devices: 28.6 us -> 24.1 us
  Pallas kernels: 9.69 us -> 7.53 us
  local copies, waits for them, and re-layouts: 2.05 us -> 0.7 us
    ppermute x17 -> x20, waiting for transfers between devices: 15.3 us -> 11.2 us  [exchange(): lax.ppermute(block, axis, [(i, i ^ mask) for i in range(lax.axis_size(axi...]
    pallas_call x2 -> x1, Pallas kernels: 3.34 us -> 1.07 us  [pick(): pl.pallas_call(kernel, out_shape=tuple(shapes), in_specs=[pl.BlockSpec(me...]
    unnamed x16 -> x12, local copies, waits for them, and re-layouts: 2.05 us -> 0.68 us
    ppermute x17 -> x20, starting transfers between devices: 9.75 us -> 9.26 us  [exchange(): lax.ppermute(block, axis, [(i, i ^ mask) for i in range(lax.axis_size(axi...]
  transfers between devices with their start and end apart: 23 -> 26, of which waited for: 11 -> 17; matrix products, arithmetic and copies ran while one was open for 0% -> 0% of each run, Pallas kernels for 6% -> 6%
where the time goes in v2:
time: 52.1 us; the launch traced here: 52 us
  waiting for transfers between devices  24.1 us (46%)
  starting transfers between devices  19.5 us (37%)
  Pallas kernels  7.53 us (14%)
  local copies, waits for them, and re-layouts  0.7 us (1%)
    ppermute x6, waiting for transfers between devices, rotate(): lax.ppermute(block, axis, [(i, (i + distance) % n) for i in range(n)])  13 us
    ppermute x20, waiting for transfers between devices, exchange(): lax.ppermute(block, axis, [(i, i ^ mask) for i in range(lax.axis_size(axi...  11.2 us
    ppermute x6, starting transfers between devices, rotate(): lax.ppermute(block, axis, [(i, (i + distance) % n) for i in range(n)])  10.2 us
    ppermute x20, starting transfers between devices, exchange(): lax.ppermute(block, axis, [(i, i ^ mask) for i in range(lax.axis_size(axi...  9.26 us
    pallas_call x8, Pallas kernels, vmem_call(): pl.pallas_call(kernel, out_shape=tuple(outs), in_specs=[pl.BlockSpec(memo...  6.46 us
    pallas_call x1, Pallas kernels, pick(): pl.pallas_call(kernel, out_shape=tuple(shapes), in_specs=[pl.BlockSpec(me...  1.07 us
  transfers between devices with their start and end apart: 26, of which 17 were waited for; matrix products, arithmetic and copies ran while one was open for 0% of the time, Pallas kernels for 6%

profile of v2, /device:TPU:0, one launch (start us, length us, event | category | flops | bytes accessed | tf_op | source)
XLA Modules:
  0.0 52.0 jit_solution(10395368706083023928)
XLA Ops:
  0.0 0.5 collective-permute-start
  0.5 1.1 %shard_map.73 = (bf16[384,128]{1,0:T(8,128)(2,1)S(1)}, bf16[1152,128]{1,0:T(8,128)(2,1)S(1)}) custom-call(bf16[4,384,128]{2,1,0:T(8,128)(2,1)} %records_ref.1), custom_call_target="tpu_custom_call" | custom-call | tf_op jit(solution)/shard_map/pallas_call | solution.py:133
  1.5 2.6 %collective-permute-start.1 = (bf16[384,128]{1,0:T(8,128)(2,1)S(1)}, bf16[384,128]{1,0:T(8,128)(2,1)S(1)}, u32[]{:S(2)}, u32[]{:S(2)}) collective-permute-start(bf16[384,128]{1,0:T(8,128)(2,1)S(1)} %get-tuple-element.26.own_ref), channel_id=1, source_target_pairs={{0,2},{1,3},{2,0},{3,1},{4,6},{5,7},{6,4},{7,5},{8,10},{9,11},{10,... | collective-permute-start | bytes 294920 | tf_op jit(solution)/shard_map/ppermute | solution.py:94
  4.1 0.1 collective-permute-start.5
  4.2 3.6 %collective-permute-done.1.across_ref = bf16[384,128]{1,0:T(8,128)(2,1)S(1)} collective-permute-done((bf16[384,128]{1,0:T(8,128)(2,1)S(1)}, bf16[384,128]{1,0:T(8,128)(2,1)S(1)}, u32[]{:S(2)}, u32[]{:S(2)}) %collective-permute-start.1) | collective-permute-done | bytes 98336 | tf_op jit(solution)/shard_map/ppermute | solution.py:94
  7.8 0.0 copy-start.2
  7.8 0.1 collective-permute-start.2
  7.9 0.5 collective-permute-start.3
  8.4 0.7 %collective-permute-done.2.rest_0_ = bf16[192,128]{1,0:T(8,128)(2,1)S(1)} collective-permute-done((bf16[192,128]{1,0:T(8,128)(2,1)S(1)}, bf16[192,128]{1,0:T(8,128)(2,1)S(1)}, u32[]{:S(2)}, u32[]{:S(2)}) %collective-permute-start.2) | collective-permute-done | bytes 49184 | tf_op jit(solution)/shard_map/ppermute | solution.py:94
  9.1 0.2 collective-permute-done.3.rest_1_
  9.3 0.0 collective-permute-done.beside_ref
  9.3 0.0 copy-done
  9.3 0.0 copy-done.3
  9.3 0.0 copy-done.4
  9.3 0.0 copy-done.2
  9.3 0.6 %shard_map.74 = (bf16[416,128]{1,0:T(8,128)(2,1)S(1)}, f32[1,384,128]{2,1,0:T(8,128)S(1)}) custom-call(bf16[384,128]{1,0:T(8,128)(2,1)S(1)} %get-tuple-element.26.own_ref, bf16[4,384,128]{2,1,0:T(8,128)(2,1)S(1)} %collective-permute-done.beside_ref, bf16[384,128]{1,0:T(8,128)(2,1)S(1)} %collective-permute-done.1.across_ref, f32[4,128]{1,0:T(4,128)S(1)} %bitcast.5, ...), custom_call_target="tpu_custom_call" | custom-call | tf_op jit(solution)/shard_map/pallas_call | solution.py:98
  9.9 3.1 %collective-permute-start.4 = (bf16[416,128]{1,0:T(8,128)(2,1)S(1)}, bf16[416,128]{1,0:T(8,128)(2,1)S(1)}, u32[]{:S(2)}, u32[]{:S(2)}) collective-permute-start(bf16[416,128]{1,0:T(8,128)(2,1)S(1)} %get-tuple-element.27), channel_id=1, source_target_pairs={{0,8},{4,12},{8,0},{12,4},{1,9},{5,13},{9,1},{13,5},{2,10},{6,14},... | collective-permute-start | bytes 319496 | tf_op jit(solution)/shard_map/ppermute | solution.py:90
  13.0 0.8 %collective-permute-done.5.across_ref = bf16[1152,128]{1,0:T(8,128)(2,1)S(1)} collective-permute-done((bf16[1152,128]{1,0:T(8,128)(2,1)S(1)}, bf16[1152,128]{1,0:T(8,128)(2,1)S(1)}, u32[]{:S(2)}, u32[]{:S(2)}) %collective-permute-start.5) | collective-permute-done | bytes 294944 | tf_op jit(solution)/shard_map/ppermute | solution.py:94
  13.9 0.1 collective-permute-start.10
  14.0 0.5 collective-permute-start.11
  14.5 0.1 collective-permute-start.6
  14.6 0.4 collective-permute-start.7
  15.0 0.2 collective-permute-done.10.rest_4_
  15.2 0.2 collective-permute-start.8
  15.4 0.0 collective-permute-done.11.rest_5_
  15.4 0.3 collective-permute-start.9
  15.7 0.0 collective-permute-done.6.rest_0_
  15.7 0.2 collective-permute-done.7.rest_1_
  15.9 0.6 %collective-permute-done.8.rest_2_ = bf16[192,128]{1,0:T(8,128)(2,1)S(1)} collective-permute-done((bf16[192,128]{1,0:T(8,128)(2,1)S(1)}, bf16[192,128]{1,0:T(8,128)(2,1)S(1)}, u32[]{:S(2)}, u32[]{:S(2)}) %collective-permute-start.8) | collective-permute-done | bytes 49184 | tf_op jit(solution)/shard_map/ppermute | solution.py:94
  16.4 0.2 collective-permute-done.9.rest_3_
  16.6 1.3 %shard_map.75 = (bf16[416,128]{1,0:T(8,128)(2,1)S(1)}, bf16[416,128]{1,0:T(8,128)(2,1)S(1)}, bf16[416,128]{1,0:T(8,128)(2,1)S(1)}, f32[3,384,128]{2,1,0:T(8,128)S(1)}) custom-call(bf16[1152,128]{1,0:T(8,128)(2,1)S(1)} %get-tuple-element.28.own_ref, bf16[4,384,128]{2,1,0:T(8,128)(2,1)S(1)} %collective-permute-done.beside_ref, ...), custom_call_target="tpu_custom_call" | custom-call | tf_op jit(solution)/shard_map/pallas_call | solution.py:98
  17.9 1.9 %collective-permute-start.12 = (bf16[416,128]{1,0:T(8,128)(2,1)S(1)}, bf16[416,128]{1,0:T(8,128)(2,1)S(1)}, u32[]{:S(2)}, u32[]{:S(2)}) collective-permute-start(bf16[416,128]{1,0:T(8,128)(2,1)S(1)} %get-tuple-element.30), channel_id=1, source_target_pairs={{0,4},{4,8},{8,12},{12,0},{1,5},{5,9},{9,13},{13,1},{2,6},{6,10},{... | collective-permute-start | bytes 319496 | tf_op jit(solution)/shard_map/ppermute | solution.py:90
  19.8 2.1 %collective-permute-start.13 = (bf16[416,128]{1,0:T(8,128)(2,1)S(1)}, bf16[416,128]{1,0:T(8,128)(2,1)S(1)}, u32[]{:S(2)}, u32[]{:S(2)}) collective-permute-start(bf16[416,128]{1,0:T(8,128)(2,1)S(1)} %get-tuple-element.31), channel_id=1, source_target_pairs={{0,12},{4,0},{8,4},{12,8},{1,13},{5,1},{9,5},{13,9},{2,14},{6,2},{... | collective-permute-start | bytes 319496 | tf_op jit(solution)/shard_map/ppermute | solution.py:90
  21.9 0.0 collective-permute-done.4.block_ref.refs_0_
  21.9 3.8 %collective-permute-done.12.refs_1_ = bf16[416,128]{1,0:T(8,128)(2,1)S(1)} collective-permute-done((bf16[416,128]{1,0:T(8,128)(2,1)S(1)}, bf16[416,128]{1,0:T(8,128)(2,1)S(1)}, u32[]{:S(2)}, u32[]{:S(2)}) %collective-permute-start.12) | collective-permute-done | bytes 106528 | tf_op jit(solution)/shard_map/ppermute | solution.py:90
  25.6 1.4 %collective-permute-done.13.refs_2_ = bf16[416,128]{1,0:T(8,128)(2,1)S(1)} collective-permute-done((bf16[416,128]{1,0:T(8,128)(2,1)S(1)}, bf16[416,128]{1,0:T(8,128)(2,1)S(1)}, u32[]{:S(2)}, u32[]{:S(2)}) %collective-permute-start.13) | collective-permute-done | bytes 106528 | tf_op jit(solution)/shard_map/ppermute | solution.py:90
  27.0 0.7 %copy-done.5 = f32[128]{0:T(128)S(1)} copy-done((f32[128]{0:T(128)S(1)}, f32[128]{0:T(128)}, u32[]{:S(2)}) %copy-start.5) | copy-done | bytes 536
  27.7 3.1 %shard_map.77 = (bf16[400,128]{1,0:T(8,128)(2,1)S(1)}, bf16[400,128]{1,0:T(8,128)(2,1)S(1)}, bf16[400,128]{1,0:T(8,128)(2,1)S(1)}, bf16[400,128]{1,0:T(8,128)(2,1)S(1)}) custom-call(bf16[416,128]{1,0:T(8,128)(2,1)S(1)} %collective-permute-done.4.block_ref.refs_0_, bf16[416,128]{1,0:T(8,128)(2,1)S(1)} %collective-permute-done.12.refs_1_, ...), custom_call_target="tpu_custom_call" | custom-call | tf_op jit(solution)/shard_map/pallas_call | solution.py:98
  30.8 0.0 copy-done.1
  30.8 1.6 %collective-permute-start.15 = (bf16[640,128]{1,0:T(8,128)(2,1)S(1)}, bf16[640,128]{1,0:T(8,128)(2,1)S(1)}, u32[]{:S(2)}, u32[]{:S(2)}) collective-permute-start(bf16[640,128]{1,0:T(8,128)(2,1)S(1)} %get-tuple-element.35.refs_0_), channel_id=1, source_target_pairs={{0,2},{1,3},{2,0},{3,1},{4,6},{5,7},{6,4},{7,5},{8,10},{9,11},{10,... | collective-permute-start | bytes 491528 | tf_op jit(solution)/shard_map/ppermute | solution.py:94
  32.4 2.3 %collective-permute-start.18 = (bf16[400,128]{1,0:T(8,128)(2,1)S(1)}, bf16[400,128]{1,0:T(8,128)(2,1)S(1)}, u32[]{:S(2)}, u32[]{:S(2)}) collective-permute-start(bf16[400,128]{1,0:T(8,128)(2,1)S(1)} %get-tuple-element.40), channel_id=1, source_target_pairs={{0,12},{4,0},{8,4},{12,8},{1,13},{5,1},{9,5},{13,9},{2,14},{6,2},{... | collective-permute-start | bytes 307208 | tf_op jit(solution)/shard_map/ppermute | solution.py:90
  34.7 0.0 collective-permute-start.17
  34.7 0.9 %collective-permute-start.16 = (bf16[400,128]{1,0:T(8,128)(2,1)S(1)}, bf16[400,128]{1,0:T(8,128)(2,1)S(1)}, u32[]{:S(2)}, u32[]{:S(2)}) collective-permute-start(bf16[400,128]{1,0:T(8,128)(2,1)S(1)} %get-tuple-element.37), channel_id=1, source_target_pairs={{0,8},{4,12},{8,0},{12,4},{1,9},{5,13},{9,1},{13,5},{2,10},{6,14},... | collective-permute-start | bytes 307208 | tf_op jit(solution)/shard_map/ppermute | solution.py:90
  35.5 0.0 collective-permute-start.14
  35.5 2.5 %collective-permute-done.18.refs_1_ = bf16[400,128]{1,0:T(8,128)(2,1)S(1)} collective-permute-done((bf16[400,128]{1,0:T(8,128)(2,1)S(1)}, bf16[400,128]{1,0:T(8,128)(2,1)S(1)}, u32[]{:S(2)}, u32[]{:S(2)}) %collective-permute-start.18) | collective-permute-done | bytes 102432 | tf_op jit(solution)/shard_map/ppermute | solution.py:90
  38.1 3.2 %collective-permute-done.17.refs_0_ = bf16[400,128]{1,0:T(8,128)(2,1)S(1)} collective-permute-done((bf16[400,128]{1,0:T(8,128)(2,1)S(1)}, bf16[400,128]{1,0:T(8,128)(2,1)S(1)}, u32[]{:S(2)}, u32[]{:S(2)}) %collective-permute-start.17) | collective-permute-done | bytes 102432 | tf_op jit(solution)/shard_map/ppermute | solution.py:90
  41.3 0.8 %collective-permute-start.21 = (bf16[768,128]{1,0:T(8,128)(2,1)S(1)}, bf16[768,128]{1,0:T(8,128)(2,1)S(1)}, u32[]{:S(2)}, u32[]{:S(2)}) collective-permute-start(bf16[768,128]{1,0:T(8,128)(2,1)S(1)} %shard_map.79.refs_4_), channel_id=1, source_target_pairs={{0,2},{1,3},{2,0},{3,1},{4,6},{5,7},{6,4},{7,5},{8,10},{9,11},{10,... | collective-permute-start | bytes 589832 | tf_op jit(solution)/shard_map/ppermute | solution.py:94
  42.1 2.1 %collective-permute-done.16.refs_0_ = bf16[400,128]{1,0:T(8,128)(2,1)S(1)} collective-permute-done((bf16[400,128]{1,0:T(8,128)(2,1)S(1)}, bf16[400,128]{1,0:T(8,128)(2,1)S(1)}, u32[]{:S(2)}, u32[]{:S(2)}) %collective-permute-start.16) | collective-permute-done | bytes 102432 | tf_op jit(solution)/shard_map/ppermute | solution.py:90
  44.2 0.0 collective-permute-done.15.refs_2_
  44.2 0.6 %collective-permute-start.24 = (bf16[384,128]{1,0:T(8,128)(2,1)S(1)}, bf16[384,128]{1,0:T(8,128)(2,1)S(1)}, u32[]{:S(2)}, u32[]{:S(2)}) collective-permute-start(bf16[384,128]{1,0:T(8,128)(2,1)S(1)} %shard_map.80.refs_8_), channel_id=1, source_target_pairs={{0,2},{1,3},{2,0},{3,1},{4,6},{5,7},{6,4},{7,5},{8,10},{9,11},{10,... | collective-permute-start | bytes 294920 | tf_op jit(solution)/shard_map/ppermute | solution.py:94
  44.8 0.0 collective-permute-start.20
  44.8 2.9 %collective-permute-done.21.refs_6_ = bf16[768,128]{1,0:T(8,128)(2,1)S(1)} collective-permute-done((bf16[768,128]{1,0:T(8,128)(2,1)S(1)}, bf16[768,128]{1,0:T(8,128)(2,1)S(1)}, u32[]{:S(2)}, u32[]{:S(2)}) %collective-permute-start.21) | collective-permute-done | bytes 196640 | tf_op jit(solution)/shard_map/ppermute | solution.py:94
  47.8 0.0 collective-permute-start.22
  47.8 0.5 collective-permute-start.19
  48.3 0.9 %collective-permute-done.24.refs_10_ = bf16[384,128]{1,0:T(8,128)(2,1)S(1)} collective-permute-done((bf16[384,128]{1,0:T(8,128)(2,1)S(1)}, bf16[384,128]{1,0:T(8,128)(2,1)S(1)}, u32[]{:S(2)}, u32[]{:S(2)}) %collective-permute-start.24) | collective-permute-done | bytes 98336 | tf_op jit(solution)/shard_map/ppermute | solution.py:94
  49.2 0.0 collective-permute-start.23
  49.2 0.0 collective-permute-done.14.refs_1_
  49.2 0.5 collective-permute-start.25
  49.7 0.8 %collective-permute-done.23.refs_9_ = bf16[384,128]{1,0:T(8,128)(2,1)S(1)} collective-permute-done((bf16[384,128]{1,0:T(8,128)(2,1)S(1)}, bf16[384,128]{1,0:T(8,128)(2,1)S(1)}, u32[]{:S(2)}, u32[]{:S(2)}) %collective-permute-start.23) | collective-permute-done | bytes 98336 | tf_op jit(solution)/shard_map/ppermute | solution.py:94
  50.5 0.0 collective-permute-done.20.refs_5_
  50.5 0.0 collective-permute-done.19.refs_3_
  50.5 0.2 collective-permute-done.25.refs_11_
  50.6 0.0 collective-permute-done.22.refs_7_
  50.6 1.3 %shard_map.81 = bf16[4,384,128]{2,1,0:T(8,128)(2,1)} custom-call(bf16[640,128]{1,0:T(8,128)(2,1)S(1)} %get-tuple-element.35.refs_0_, bf16[512,128]{1,0:T(8,128)(2,1)S(1)} %collective-permute-done.14.refs_1_, bf16[640,128]{1,0:T(8,128)(2,1)S(1)} %collective-permute-done.15.refs_2_, bf16[640,128]{1,0:T(8,128)(2,1)S(1)} %collective-permute-done.19.refs_3_, ...), custom_call_target="tpu_custom_call" | custom-call | tf_op jit(solution)/shard_map/pallas_call | solution.py:98
  (11 shorter events, 0.2 us)
Async XLA Ops:
  0.0 9.3 %copy-start = (bf16[512,3,128]{2,0,1:T(8,128)(2,1)S(1)}, bf16[512,3,128]{2,0,1:T(8,128)(2,1)}, u32[]{:S(2)}) copy-start(bf16[512,3,128]{2,0,1:T(8,128)(2,1)} %param.9) | copy-start | bytes 1179652
  0.0 9.3 %collective-permute-start = (bf16[4,384,128]{2,1,0:T(8,128)(2,1)}, bf16[4,384,128]{2,1,0:T(8,128)(2,1)S(1)}, u32[]{:S(2)}, u32[]{:S(2)}) collective-permute-start(bf16[4,384,128]{2,1,0:T(8,128)(2,1)} %records_ref.1), channel_id=1, source_target_pairs={{0,1},{1,0},{2,3},{3,2},{4,5},{5,4},{6,7},{7,6},{8,9},{9,8},{10,11... | collective-permute-start | bytes 1179656 | tf_op jit(solution)/shard_map/ppermute | solution.py:94
  1.5 6.3 %collective-permute-start.1 = (bf16[384,128]{1,0:T(8,128)(2,1)S(1)}, bf16[384,128]{1,0:T(8,128)(2,1)S(1)}, u32[]{:S(2)}, u32[]{:S(2)}) collective-permute-start(bf16[384,128]{1,0:T(8,128)(2,1)S(1)} %get-tuple-element.26.own_ref), channel_id=1, source_target_pairs={{0,2},{1,3},{2,0},{3,1},{4,6},{5,7},{6,4},{7,5},{8,10},{9,11},{10,... | collective-permute-start | bytes 294920 | tf_op jit(solution)/shard_map/ppermute | solution.py:94
  4.1 9.7 %collective-permute-start.5 = (bf16[1152,128]{1,0:T(8,128)(2,1)S(1)}, bf16[1152,128]{1,0:T(8,128)(2,1)S(1)}, u32[]{:S(2)}, u32[]{:S(2)}) collective-permute-start(bf16[1152,128]{1,0:T(8,128)(2,1)S(1)} %get-tuple-element.28.own_ref), channel_id=1, source_target_pairs={{0,2},{1,3},{2,0},{3,1},{4,6},{5,7},{6,4},{7,5},{8,10},{9,11},{10,... | collective-permute-start | bytes 884744 | tf_op jit(solution)/shard_map/ppermute | solution.py:94
  7.8 1.5 %copy-start.3 = (bf16[4,384]{1,0:T(4,128)(2,1)S(1)}, bf16[4,384]{1,0:T(4,128)(2,1)}, u32[]{:S(2)}) copy-start(bf16[4,384]{1,0:T(4,128)(2,1)} %taps_ref.3) | copy-start | bytes 9220
  7.8 1.5 %copy-start.4 = (f32[512]{0:T(512)S(1)}, f32[512]{0:T(512)}, u32[]{:S(2)}) copy-start(f32[512]{0:T(512)} %param.8) | copy-start | bytes 6148
  7.8 1.5 %copy-start.2 = (f32[3,3,128]{2,1,0:T(4,128)S(1)}, f32[3,3,128]{2,1,0:T(4,128)}, u32[]{:S(2)}) copy-start(f32[3,3,128]{2,1,0:T(4,128)} %refs_2_.3) | copy-start | bytes 13828
  7.8 1.3 %collective-permute-start.2 = (bf16[192,128]{1,0:T(8,128)(2,1)S(1)}, bf16[192,128]{1,0:T(8,128)(2,1)S(1)}, u32[]{:S(2)}, u32[]{:S(2)}) collective-permute-start(bf16[192,128]{1,0:T(8,128)(2,1)S(1)} %get-tuple-element.54), channel_id=1, source_target_pairs={{0,1},{1,0},{2,3},{3,2},{4,5},{5,4},{6,7},{7,6},{8,9},{9,8},{10,11... | collective-permute-start | bytes 147464 | tf_op jit(solution)/shard_map/ppermute | solution.py:94
  7.9 1.4 %collective-permute-start.3 = (bf16[192,128]{1,0:T(8,128)(2,1)S(1)}, bf16[192,128]{1,0:T(8,128)(2,1)S(1)}, u32[]{:S(2)}, u32[]{:S(2)}) collective-permute-start(bf16[192,128]{1,0:T(8,128)(2,1)S(1)} %get-tuple-element.53), channel_id=1, source_target_pairs={{0,1},{1,0},{2,3},{3,2},{4,5},{5,4},{6,7},{7,6},{8,9},{9,8},{10,11... | collective-permute-start | bytes 147464 | tf_op jit(solution)/shard_map/ppermute | solution.py:94
  9.9 12.0 %collective-permute-start.4 = (bf16[416,128]{1,0:T(8,128)(2,1)S(1)}, bf16[416,128]{1,0:T(8,128)(2,1)S(1)}, u32[]{:S(2)}, u32[]{:S(2)}) collective-permute-start(bf16[416,128]{1,0:T(8,128)(2,1)S(1)} %get-tuple-element.27), channel_id=1, source_target_pairs={{0,8},{4,12},{8,0},{12,4},{1,9},{5,13},{9,1},{13,5},{2,10},{6,14},... | collective-permute-start | bytes 319496 | tf_op jit(solution)/shard_map/ppermute | solution.py:90
  13.9 1.3 %collective-permute-start.10 = (bf16[192,128]{1,0:T(8,128)(2,1)S(1)}, bf16[192,128]{1,0:T(8,128)(2,1)S(1)}, u32[]{:S(2)}, u32[]{:S(2)}) collective-permute-start(bf16[192,128]{1,0:T(8,128)(2,1)S(1)} %get-tuple-element.48), channel_id=1, source_target_pairs={{0,1},{1,0},{2,3},{3,2},{4,5},{5,4},{6,7},{7,6},{8,9},{9,8},{10,11... | collective-permute-start | bytes 147464 | tf_op jit(solution)/shard_map/ppermute | solution.py:94
  14.0 1.4 %collective-permute-start.11 = (bf16[192,128]{1,0:T(8,128)(2,1)S(1)}, bf16[192,128]{1,0:T(8,128)(2,1)S(1)}, u32[]{:S(2)}, u32[]{:S(2)}) collective-permute-start(bf16[192,128]{1,0:T(8,128)(2,1)S(1)} %get-tuple-element.47), channel_id=1, source_target_pairs={{0,1},{1,0},{2,3},{3,2},{4,5},{5,4},{6,7},{7,6},{8,9},{9,8},{10,11... | collective-permute-start | bytes 147464 | tf_op jit(solution)/shard_map/ppermute | solution.py:94
  14.5 1.2 %collective-permute-start.6 = (bf16[192,128]{1,0:T(8,128)(2,1)S(1)}, bf16[192,128]{1,0:T(8,128)(2,1)S(1)}, u32[]{:S(2)}, u32[]{:S(2)}) collective-permute-start(bf16[192,128]{1,0:T(8,128)(2,1)S(1)} %get-tuple-element.52), channel_id=1, source_target_pairs={{0,1},{1,0},{2,3},{3,2},{4,5},{5,4},{6,7},{7,6},{8,9},{9,8},{10,11... | collective-permute-start | bytes 147464 | tf_op jit(solution)/shard_map/ppermute | solution.py:94
  14.6 1.3 %collective-permute-start.7 = (bf16[192,128]{1,0:T(8,128)(2,1)S(1)}, bf16[192,128]{1,0:T(8,128)(2,1)S(1)}, u32[]{:S(2)}, u32[]{:S(2)}) collective-permute-start(bf16[192,128]{1,0:T(8,128)(2,1)S(1)} %get-tuple-element.51), channel_id=1, source_target_pairs={{0,1},{1,0},{2,3},{3,2},{4,5},{5,4},{6,7},{7,6},{8,9},{9,8},{10,11... | collective-permute-start | bytes 147464 | tf_op jit(solution)/shard_map/ppermute | solution.py:94
  15.2 1.2 %collective-permute-start.8 = (bf16[192,128]{1,0:T(8,128)(2,1)S(1)}, bf16[192,128]{1,0:T(8,128)(2,1)S(1)}, u32[]{:S(2)}, u32[]{:S(2)}) collective-permute-start(bf16[192,128]{1,0:T(8,128)(2,1)S(1)} %get-tuple-element.50), channel_id=1, source_target_pairs={{0,1},{1,0},{2,3},{3,2},{4,5},{5,4},{6,7},{7,6},{8,9},{9,8},{10,11... | collective-permute-start | bytes 147464 | tf_op jit(solution)/shard_map/ppermute | solution.py:94
  15.4 1.2 %collective-permute-start.9 = (bf16[192,128]{1,0:T(8,128)(2,1)S(1)}, bf16[192,128]{1,0:T(8,128)(2,1)S(1)}, u32[]{:S(2)}, u32[]{:S(2)}) collective-permute-start(bf16[192,128]{1,0:T(8,128)(2,1)S(1)} %get-tuple-element.49), channel_id=1, source_target_pairs={{0,1},{1,0},{2,3},{3,2},{4,5},{5,4},{6,7},{7,6},{8,9},{9,8},{10,11... | collective-permute-start | bytes 147464 | tf_op jit(solution)/shard_map/ppermute | solution.py:94
  17.9 7.7 %collective-permute-start.12 = (bf16[416,128]{1,0:T(8,128)(2,1)S(1)}, bf16[416,128]{1,0:T(8,128)(2,1)S(1)}, u32[]{:S(2)}, u32[]{:S(2)}) collective-permute-start(bf16[416,128]{1,0:T(8,128)(2,1)S(1)} %get-tuple-element.30), channel_id=1, source_target_pairs={{0,4},{4,8},{8,12},{12,0},{1,5},{5,9},{9,13},{13,1},{2,6},{6,10},{... | collective-permute-start | bytes 319496 | tf_op jit(solution)/shard_map/ppermute | solution.py:90
  19.8 7.2 %collective-permute-start.13 = (bf16[416,128]{1,0:T(8,128)(2,1)S(1)}, bf16[416,128]{1,0:T(8,128)(2,1)S(1)}, u32[]{:S(2)}, u32[]{:S(2)}) collective-permute-start(bf16[416,128]{1,0:T(8,128)(2,1)S(1)} %get-tuple-element.31), channel_id=1, source_target_pairs={{0,12},{4,0},{8,4},{12,8},{1,13},{5,1},{9,5},{13,9},{2,14},{6,2},{... | collective-permute-start | bytes 319496 | tf_op jit(solution)/shard_map/ppermute | solution.py:90
  27.0 0.7 %copy-start.5 = (f32[128]{0:T(128)S(1)}, f32[128]{0:T(128)}, u32[]{:S(2)}) copy-start(f32[128]{0:T(128)} %param.12) | copy-start | bytes 1540
  27.7 3.1 %copy-start.1 = (bf16[128,512]{1,0:T(8,128)(2,1)S(1)}, bf16[128,512]{1,0:T(8,128)(2,1)}, u32[]{:S(2)}) copy-start(bf16[128,512]{1,0:T(8,128)(2,1)} %refs_12_.1) | copy-start | bytes 393220
  30.8 13.4 %collective-permute-start.15 = (bf16[640,128]{1,0:T(8,128)(2,1)S(1)}, bf16[640,128]{1,0:T(8,128)(2,1)S(1)}, u32[]{:S(2)}, u32[]{:S(2)}) collective-permute-start(bf16[640,128]{1,0:T(8,128)(2,1)S(1)} %get-tuple-element.35.refs_0_), channel_id=1, source_target_pairs={{0,2},{1,3},{2,0},{3,1},{4,6},{5,7},{6,4},{7,5},{8,10},{9,11},{10,... | collective-permute-start | bytes 491528 | tf_op jit(solution)/shard_map/ppermute | solution.py:94
  32.4 5.7 %collective-permute-start.18 = (bf16[400,128]{1,0:T(8,128)(2,1)S(1)}, bf16[400,128]{1,0:T(8,128)(2,1)S(1)}, u32[]{:S(2)}, u32[]{:S(2)}) collective-permute-start(bf16[400,128]{1,0:T(8,128)(2,1)S(1)} %get-tuple-element.40), channel_id=1, source_target_pairs={{0,12},{4,0},{8,4},{12,8},{1,13},{5,1},{9,5},{13,9},{2,14},{6,2},{... | collective-permute-start | bytes 307208 | tf_op jit(solution)/shard_map/ppermute | solution.py:90
  34.7 6.6 %collective-permute-start.17 = (bf16[400,128]{1,0:T(8,128)(2,1)S(1)}, bf16[400,128]{1,0:T(8,128)(2,1)S(1)}, u32[]{:S(2)}, u32[]{:S(2)}) collective-permute-start(bf16[400,128]{1,0:T(8,128)(2,1)S(1)} %get-tuple-element.38), channel_id=1, source_target_pairs={{0,4},{4,8},{8,12},{12,0},{1,5},{5,9},{9,13},{13,1},{2,6},{6,10},{... | collective-permute-start | bytes 307208 | tf_op jit(solution)/shard_map/ppermute | solution.py:90
  34.7 9.5 %collective-permute-start.16 = (bf16[400,128]{1,0:T(8,128)(2,1)S(1)}, bf16[400,128]{1,0:T(8,128)(2,1)S(1)}, u32[]{:S(2)}, u32[]{:S(2)}) collective-permute-start(bf16[400,128]{1,0:T(8,128)(2,1)S(1)} %get-tuple-element.37), channel_id=1, source_target_pairs={{0,8},{4,12},{8,0},{12,4},{1,9},{5,13},{9,1},{13,5},{2,10},{6,14},... | collective-permute-start | bytes 307208 | tf_op jit(solution)/shard_map/ppermute | solution.py:90
  35.5 13.7 %collective-permute-start.14 = (bf16[512,128]{1,0:T(8,128)(2,1)S(1)}, bf16[512,128]{1,0:T(8,128)(2,1)S(1)}, u32[]{:S(2)}, u32[]{:S(2)}) collective-permute-start(bf16[512,128]{1,0:T(8,128)(2,1)S(1)} %get-tuple-element.36), channel_id=1, source_target_pairs={{0,1},{1,0},{2,3},{3,2},{4,5},{5,4},{6,7},{7,6},{8,9},{9,8},{10,11... | collective-permute-start | bytes 393224 | tf_op jit(solution)/shard_map/ppermute | solution.py:94
  41.3 6.4 %collective-permute-start.21 = (bf16[768,128]{1,0:T(8,128)(2,1)S(1)}, bf16[768,128]{1,0:T(8,128)(2,1)S(1)}, u32[]{:S(2)}, u32[]{:S(2)}) collective-permute-start(bf16[768,128]{1,0:T(8,128)(2,1)S(1)} %shard_map.79.refs_4_), channel_id=1, source_target_pairs={{0,2},{1,3},{2,0},{3,1},{4,6},{5,7},{6,4},{7,5},{8,10},{9,11},{10,... | collective-permute-start | bytes 589832 | tf_op jit(solution)/shard_map/ppermute | solution.py:94
  44.2 5.0 %collective-permute-start.24 = (bf16[384,128]{1,0:T(8,128)(2,1)S(1)}, bf16[384,128]{1,0:T(8,128)(2,1)S(1)}, u32[]{:S(2)}, u32[]{:S(2)}) collective-permute-start(bf16[384,128]{1,0:T(8,128)(2,1)S(1)} %shard_map.80.refs_8_), channel_id=1, source_target_pairs={{0,2},{1,3},{2,0},{3,1},{4,6},{5,7},{6,4},{7,5},{8,10},{9,11},{10,... | collective-permute-start | bytes 294920 | tf_op jit(solution)/shard_map/ppermute | solution.py:94
  44.8 5.7 %collective-permute-start.20 = (bf16[768,128]{1,0:T(8,128)(2,1)S(1)}, bf16[768,128]{1,0:T(8,128)(2,1)S(1)}, u32[]{:S(2)}, u32[]{:S(2)}) collective-permute-start(bf16[768,128]{1,0:T(8,128)(2,1)S(1)} %shard_map.79.refs_4_), channel_id=1, source_target_pairs={{0,1},{1,0},{2,3},{3,2},{4,5},{5,4},{6,7},{7,6},{8,9},{9,8},{10,11... | collective-permute-start | bytes 589832 | tf_op jit(solution)/shard_map/ppermute | solution.py:94
  47.8 2.9 %collective-permute-start.22 = (bf16[768,128]{1,0:T(8,128)(2,1)S(1)}, bf16[768,128]{1,0:T(8,128)(2,1)S(1)}, u32[]{:S(2)}, u32[]{:S(2)}) collective-permute-start(bf16[768,128]{1,0:T(8,128)(2,1)S(1)} %collective-permute-done.21.refs_6_), channel_id=1, source_target_pairs={{0,1},{1,0},{2,3},{3,2},{4,5},{5,4},{6,7},{7,6},{8,9},{9,8},{10,11... | collective-permute-start | bytes 589832 | tf_op jit(solution)/shard_map/ppermute | solution.py:94
  47.8 2.7 %collective-permute-start.19 = (bf16[640,128]{1,0:T(8,128)(2,1)S(1)}, bf16[640,128]{1,0:T(8,128)(2,1)S(1)}, u32[]{:S(2)}, u32[]{:S(2)}) collective-permute-start(bf16[640,128]{1,0:T(8,128)(2,1)S(1)} %collective-permute-done.15.refs_2_), channel_id=1, source_target_pairs={{0,1},{1,0},{2,3},{3,2},{4,5},{5,4},{6,7},{7,6},{8,9},{9,8},{10,11... | collective-permute-start | bytes 491528 | tf_op jit(solution)/shard_map/ppermute | solution.py:94
  49.2 1.3 %collective-permute-start.23 = (bf16[384,128]{1,0:T(8,128)(2,1)S(1)}, bf16[384,128]{1,0:T(8,128)(2,1)S(1)}, u32[]{:S(2)}, u32[]{:S(2)}) collective-permute-start(bf16[384,128]{1,0:T(8,128)(2,1)S(1)} %shard_map.80.refs_8_), channel_id=1, source_target_pairs={{0,1},{1,0},{2,3},{3,2},{4,5},{5,4},{6,7},{7,6},{8,9},{9,8},{10,11... | collective-permute-start | bytes 294920 | tf_op jit(solution)/shard_map/ppermute | solution.py:94
  49.2 1.5 %collective-permute-start.25 = (bf16[384,128]{1,0:T(8,128)(2,1)S(1)}, bf16[384,128]{1,0:T(8,128)(2,1)S(1)}, u32[]{:S(2)}, u32[]{:S(2)}) collective-permute-start(bf16[384,128]{1,0:T(8,128)(2,1)S(1)} %collective-permute-done.24.refs_10_), channel_id=1, source_target_pairs={{0,1},{1,0},{2,3},{3,2},{4,5},{5,4},{6,7},{7,6},{8,9},{9,8},{10,11... | collective-permute-start | bytes 294920 | tf_op jit(solution)/shard_map/ppermute | solution.py:94

commit v3 on v2

--- a/solution.py
+++ b/solution.py
@@ -7,9 +7,16 @@
 
 LANES = 128
 EXTRA = 32
-SPLIT = 2
-SPACE = 1 << 30
-FAR = 1 << 33
+SPLIT = 1
+SPACE = 1 << 31
+FAR = 1 << 32
+NEAR = (1, 3)
+TIE = 1
+FARD = (2,)
+ORDER = (2, 1, 3)
+BESIDE = 1
+OWNSEP = 1
+SPLIT1 = 2
 COST = pl.CostEstimate(flops=0, bytes_accessed=0, transcendentals=0)
 BACK = 16
 VMEM = pltpu.VMEM
@@ -209,17 +216,20 @@
     return out[:picked], out[picked]
 
 
-def tail_rows(block, cost):
-    def kernel(block_ref, out_ref):
+def tail_rows(block, skip_gain, cost):
+    def kernel(block_ref, skip_ref, out_ref, same_ref):
         out_ref[...] = block_ref[-EXTRA:, :]
-
-    return vmem_call(kernel, [jax.ShapeDtypeStruct((EXTRA, LANES), block.dtype)], [], block, cost=cost)[0]
+        same_ref[...] = skip_ref[...]
+
+    outs = [jax.ShapeDtypeStruct((EXTRA, LANES), block.dtype), jax.ShapeDtypeStruct(skip_gain.shape, skip_gain.dtype)]
+    return vmem_call(kernel, outs, [], block, skip_gain, cost=cost)
 
 
 def long_convolution(chunks, distances, first_tail, short_kernel, skip_gain):
     n = len(chunks)
     block_len = chunks[0].shape[0] - EXTRA
     length = n * block_len
+    half = length // 2
     pieces = block_len // LANES
     f32, bf16 = jnp.float32, jnp.bfloat16
 
@@ -242,7 +252,9 @@
             bands[f * LANES : (f + 1) * LANES, :] = band.astype(bf16)
         short = [[short_ref[j, s : s + 1, :] for j in range(3)] for s in range(3)]
         for q in range(n):
-            source[q * block_len : (q + 1) * block_len, :] = inputs[q, :block_len, :]
+            side, start = divmod(q * block_len, half)
+            columns = slice(side * LANES, (side + 1) * LANES)
+            source[start : start + block_len, columns] = inputs[q, :block_len, :]
             if q == 0:
                 continue
             here = inputs[q, block_len : block_len + EXTRA, :].astype(f32)[4 * pieces :]
@@ -257,19 +269,29 @@
                         k0 * head[1:2] + k1 * head[0:1] + k2 * tail[1:2],
                     )
                 )
-            rows = [fixed[0][t] * fixed[1][t] for t in range(2)]
-            first = source[q * block_len : q * block_len + 16, :].astype(f32)
-            first = jnp.concatenate(rows + [first[2:]], axis=0)
-            source[q * block_len : q * block_len + 16, :] = first.astype(bf16)
-        for p in range(length // LANES):
-            reach = (p + 1) * LANES
-            terms = jnp.dot(bands[:, length + LANES - reach :], source[0:reach, :], preferred_element_type=f32)
+            first = inputs[q, 0:16, :].astype(f32)
+            first = jnp.concatenate([fixed[0][t] * fixed[1][t] for t in range(2)] + [first[2:]], axis=0)
+            source[start : start + 16, columns] = first.astype(bf16)
+
+        def finish(p, terms):
+            side, start = divmod(p * LANES, half)
             total = terms[0:LANES]
             for f in range(1, 4):
                 total = jnp.where(lane >= f * 32, terms[f * LANES : (f + 1) * LANES], total)
-            total = total + skip_ref[...] * source[reach - LANES : reach, :].astype(f32)
+            here = source[start : start + LANES, side * LANES : (side + 1) * LANES]
+            total = total + skip_ref[...] * here.astype(f32)
             q, b = divmod(p, pieces)
             sums[q, b * LANES : (b + 1) * LANES, :] = total.astype(bf16)
+
+        width = length + LANES
+        for p in range(half // LANES):
+            reach = (p + 1) * LANES
+            within = jnp.dot(bands[:, width - reach :], source[0:reach, :], preferred_element_type=f32)
+            across = jnp.dot(
+                bands[:, width - reach - half : width - reach], source[:, 0:LANES], preferred_element_type=f32
+            )
+            finish(p, within[:, 0:LANES])
+            finish(p + half // LANES, within[:, LANES:] + across)
         for q in range(n):
             if q == 0:
                 tail = jnp.zeros((2, LANES), f32)
@@ -282,7 +304,7 @@
     back = jax.ShapeDtypeStruct((block_len + BACK, LANES), bf16)
     scratch = [
         pltpu.VMEM((n, block_len + EXTRA, LANES), bf16),
-        pltpu.VMEM((length, LANES), bf16),
+        pltpu.VMEM((half, 2 * LANES), bf16),
         pltpu.VMEM((4 * LANES, length + LANES), bf16),
         pltpu.VMEM((n, block_len + BACK, LANES), bf16),
     ]
@@ -331,7 +353,8 @@
     groups = len(slabs)
 
     def kernel(*refs):
-        slab_refs, (w_ref, out_ref, w_all) = refs[: 4 * groups], refs[4 * groups :]
+        slab_refs, (w_ref, out_ref, w_all, mixed, sems) = refs[: 4 * groups], refs[4 * groups :]
+        copies = []
         me = lax.axis_index("chan")
         z = lax.axis_index("seq")
         start = len(distances[0]) * block_len
@@ -343,11 +366,27 @@
             for i, k in enumerate(distances[g]):
                 rows = slice(i * block_len, (i + 1) * block_len)
                 lhs = jnp.concatenate([ref[rows, :] for ref in slab_refs[4 * g : 4 * g + 4]], axis=1)
-                out_ref[lax.rem(z + k, count)] = jnp.dot(lhs, w_all[...], preferred_element_type=f32).astype(bf16)
-
-    out = jax.ShapeDtypeStruct((count, block_len, LANES), bf16)
+                n = len(copies)
+                mixed[n] = jnp.dot(lhs, w_all[...], preferred_element_type=f32).astype(bf16)
+                copies.append(pltpu.make_async_copy(mixed.at[n], out_ref.at[lax.rem(z + k, count)], sems.at[n]))
+                copies[n].start()
+        for copy in copies:
+            copy.wait()
+
     operands = [x for slab in slabs for x in slab] + [out_projection]
-    return vmem_call(kernel, [out], [pltpu.VMEM((4 * LANES, LANES), bf16)], *operands)[0]
+    return pl.pallas_call(
+        kernel,
+        out_shape=jax.ShapeDtypeStruct((count, block_len, LANES), bf16),
+        in_specs=[pl.BlockSpec(memory_space=VMEM)] * len(operands),
+        out_specs=pl.BlockSpec(memory_space=pl.ANY),
+        scratch_shapes=[
+            pltpu.VMEM((4 * LANES, LANES), bf16),
+            pltpu.VMEM((count, block_len, LANES), bf16),
+            pltpu.SemaphoreType.DMA((count,)),
+        ],
+        compiler_params=pltpu.CompilerParams(vmem_limit_bytes=40 * 1024 * 1024),
+        cost_estimate=COST,
+    )(*operands)
 
 
 def exchange_body(records, norm_gain, in_projection, short_kernel, long_filter, skip_gain, out_projection):
@@ -359,42 +398,49 @@
     groups = ((2,), (1, 3, 0))
     picked = pick(records, groups)
     across = [exchange(block, "chan", 2) for block in picked]
-    beside = exchange(records, "chan", 1)
-    def projected(g, far):
-        pieces = SPLIT * len(groups[g])
+    beside = exchange(after(records, picked[0]) if BESIDE else records, "chan", 1)
+
+    def projected(offsets, own, far, pieces):
         size = far.shape[0] // pieces
         diagonal = [exchange(far[i * size : (i + 1) * size], "chan", 1) for i in range(pieces)]
-        return project(
-            picked[g], beside, far, diagonal, gain, weights, short_kernel, long_filter, groups[g]
-        )
-
-    (to_two,), query_two = projected(0, across[0])
+        return project(own, beside, far, diagonal, gain, weights, short_kernel, long_filter, offsets)
+
+    query = {}
+    (to_two,), query_two = projected((2,), picked[0], across[0], SPLIT1)
     from_two = rotate(to_two, "seq", 2)
-    (to_one, to_three, kept), query_rest = projected(1, after(across[1], to_two))
+    second = after(across[1], to_two)
+    if OWNSEP:
+        rows = 2 * block_len
+        (to_one, to_three), query_near = projected((1, 3), picked[1][:rows], second[:rows], 2 * SPLIT)
+        last = after(second[rows:], to_one)
+        (kept,), query_own = projected((0,), picked[1][rows:], last, 1)
+        query = {0: (query_own, 0), 1: (query_near, 1), 3: (query_near, 0), 2: (query_two, 0)}
+    else:
+        (to_one, to_three, kept), query_rest = projected((1, 3, 0), picked[1], second, 3 * SPLIT)
+        query = {0: (query_rest, 2), 1: (query_rest, 1), 3: (query_rest, 0), 2: (query_two, 0)}
     from_one = rotate(to_one, "seq", 1)
     from_three = rotate(to_three, "seq", 3)
 
+    tail, skip = tail_rows(from_two, skip, SPACE)
     back_two, back_one, back_three, back_own = long_convolution(
-        (from_two, from_one, from_three, kept),
-        (2, 1, 3, 0),
-        tail_rows(from_two, SPACE),
-        short_kernel,
-        skip,
-    )
-    sums_two = rotate(back_two, "seq", 2)
-    sums_one = rotate(back_one, "seq", 1)
-    sums_three = rotate(back_three, "seq", 3)
-
-    own, own_beside = gate([back_own], [(query_rest, 2)], short_kernel, out_projection)
+        (from_two, from_one, from_three, kept), (2, 1, 3, 0), tail, short_kernel, skip
+    )
+    back = {1: back_one, 2: back_two, 3: back_three}
+    sums = {k: rotate(back[k], "seq", k) for k in ORDER}
+
+    own, own_beside = gate([back_own], [query[0]], short_kernel, out_projection)
     own_over = exchange(own, "chan", 2)
-    (near,) = gate([after(sums_one, own), after(sums_three, own)], [(query_rest, 1), (query_rest, 0)], short_kernel)
-    (far,) = gate([after(sums_two, near, own_over)], [(query_two, 0)], short_kernel, cost=FAR)
+    (near,) = gate([after(sums[k], own) for k in NEAR], [query[k] for k in NEAR], short_kernel)
+    (far,) = gate([after(sums[k], near, own_over) if TIE == 0 else after(sums[k], near) for k in FARD], [query[k] for k in FARD], short_kernel, cost=FAR)
+    if TIE == 1:
+        far = after(far, own_over)
     slabs = []
     for gated, beside, over in ((own, own_beside, own_over), (near, near, None), (far, far, None)):
         if over is None:
             over = exchange(gated, "chan", 2)
         slabs.append((gated, exchange(beside, "chan", 1), over, exchange(after(over, far), "chan", 1)))
-    return mix(slabs, out_projection, ((0,), (3, 1), (2,)), block_len)
+    places = [tuple((4 - k) % 4 for k in group) for group in ((0,), NEAR, FARD)]
+    return mix(slabs, out_projection, places, block_len)
 
 
 def solution(mesh):

time: 52.1 us -> 48.3 us (0.927)
  waiting for transfers between devices: 24.1 us -> 19.4 us
  starting transfers between devices: 19.5 us -> 21.4 us
  local copies, waits for them, and re-layouts: 0.7 us -> 0.09 us
    ppermute x6, waiting for transfers between devices: 13 us -> 9.42 us  [rotate(): lax.ppermute(block, axis, [(i, (i + distance) % n) for i in range(n)])]
    pallas_call x8, Pallas kernels: 6.46 us -> 4.72 us  [vmem_call(): pl.pallas_call(kernel, out_shape=tuple(outs), in_specs=[pl.BlockSpec(memo...]
    pallas_call x0 -> x1, Pallas kernels: none -> 1.3 us  [mix(): pl.pallas_call(kernel, out_shape=jax.ShapeDtypeStruct((count, block_len,...]
    ppermute x20 -> x17, waiting for transfers between devices: 11.2 us -> 9.95 us  [exchange(): lax.ppermute(block, axis, [(i, i ^ mask) for i in range(lax.axis_size(axi...]
    ppermute x6, starting transfers between devices: 10.2 us -> 11.3 us  [rotate(): lax.ppermute(block, axis, [(i, (i + distance) % n) for i in range(n)])]
    ppermute x20 -> x17, starting transfers between devices: 9.26 us -> 10.1 us  [exchange(): lax.ppermute(block, axis, [(i, i ^ mask) for i in range(lax.axis_size(axi...]
    unnamed x12, local copies, waits for them, and re-layouts: 0.68 us -> 0.02 us
  transfers between devices with their start and end apart: 26 -> 23, of which waited for: 17 -> 14; matrix products, arithmetic and copies ran while one was open for 0% -> 0% of each run, Pallas kernels for 6% -> 5%
where the time goes in v3:
time: 48.3 us; the launch traced here: 48.2 us
  starting transfers between devices  21.4 us (44%)
  waiting for transfers between devices  19.4 us (40%)
  Pallas kernels  7.14 us (15%)
    ppermute x6, starting transfers between devices, rotate(): lax.ppermute(block, axis, [(i, (i + distance) % n) for i in range(n)])  11.3 us
    ppermute x17, starting transfers between devices, exchange(): lax.ppermute(block, axis, [(i, i ^ mask) for i in range(lax.axis_size(axi...  10.1 us
    ppermute x17, waiting for transfers between devices, exchange(): lax.ppermute(block, axis, [(i, i ^ mask) for i in range(lax.axis_size(axi...  9.95 us
    ppermute x6, waiting for transfers between devices, rotate(): lax.ppermute(block, axis, [(i, (i + distance) % n) for i in range(n)])  9.42 us
    pallas_call x8, Pallas kernels, vmem_call(): pl.pallas_call(kernel, out_shape=tuple(outs), in_specs=[pl.BlockSpec(memo...  4.72 us
    pallas_call x1, Pallas kernels, mix(): pl.pallas_call(kernel, out_shape=jax.ShapeDtypeStruct((count, block_len,...  1.3 us
    pallas_call x1, Pallas kernels, pick(): pl.pallas_call(kernel, out_shape=tuple(shapes), in_specs=[pl.BlockSpec(me...  1.12 us
  transfers between devices with their start and end apart: 23, of which 14 were waited for; matrix products, arithmetic and copies ran while one was open for 0% of the time, Pallas kernels for 5%

profile of v3, /device:TPU:0, one launch (start us, length us, event | category | flops | bytes accessed | tf_op | source)
XLA Modules:
  0.0 48.2 jit_solution(7581156225716432276)
XLA Ops:
  0.0 0.0 copy-start
  0.0 1.1 %shard_map.73 = (bf16[384,128]{1,0:T(8,128)(2,1)S(1)}, bf16[1152,128]{1,0:T(8,128)(2,1)S(1)}) custom-call(bf16[4,384,128]{2,1,0:T(8,128)(2,1)} %records_ref.1), custom_call_target="tpu_custom_call" | custom-call | tf_op jit(solution)/shard_map/pallas_call | solution.py:140
  1.1 0.5 %collective-permute-start = (bf16[4,384,128]{2,1,0:T(8,128)(2,1)}, bf16[4,384,128]{2,1,0:T(8,128)(2,1)S(1)}, u32[]{:S(2)}, u32[]{:S(2)}) collective-permute-start(bf16[4,384,128]{2,1,0:T(8,128)(2,1)} %records_ref.1), channel_id=1, source_target_pairs={{0,1},{1,0},{2,3},{3,2},{4,5},{5,4},{6,7},{7,6},{8,9},{9,8},{10,11... | collective-permute-start | bytes 1179656 | tf_op jit(solution)/shard_map/ppermute | solution.py:101
  1.6 2.6 %collective-permute-start.1 = (bf16[384,128]{1,0:T(8,128)(2,1)S(1)}, bf16[384,128]{1,0:T(8,128)(2,1)S(1)}, u32[]{:S(2)}, u32[]{:S(2)}) collective-permute-start(bf16[384,128]{1,0:T(8,128)(2,1)S(1)} %get-tuple-element.32.own_ref), channel_id=1, source_target_pairs={{0,2},{1,3},{2,0},{3,1},{4,6},{5,7},{6,4},{7,5},{8,10},{9,11},{10,... | collective-permute-start | bytes 294920 | tf_op jit(solution)/shard_map/ppermute | solution.py:101
  4.2 0.1 collective-permute-start.5
  4.3 3.6 %collective-permute-done.1.across_ref = bf16[384,128]{1,0:T(8,128)(2,1)S(1)} collective-permute-done((bf16[384,128]{1,0:T(8,128)(2,1)S(1)}, bf16[384,128]{1,0:T(8,128)(2,1)S(1)}, u32[]{:S(2)}, u32[]{:S(2)}) %collective-permute-start.1) | collective-permute-done | bytes 98336 | tf_op jit(solution)/shard_map/ppermute | solution.py:101
  7.9 0.0 copy-start.3
  7.9 0.0 copy-start.4
  7.9 0.0 copy-start.2
  7.9 0.1 collective-permute-start.3
  8.0 0.5 %collective-permute-start.2 = (bf16[192,128]{1,0:T(8,128)(2,1)S(1)}, bf16[192,128]{1,0:T(8,128)(2,1)S(1)}, u32[]{:S(2)}, u32[]{:S(2)}) collective-permute-start(bf16[192,128]{1,0:T(8,128)(2,1)S(1)} %get-tuple-element.63), channel_id=1, source_target_pairs={{0,1},{1,0},{2,3},{3,2},{4,5},{5,4},{6,7},{7,6},{8,9},{9,8},{10,11... | collective-permute-start | bytes 147464 | tf_op jit(solution)/shard_map/ppermute | solution.py:101
  8.5 0.7 %collective-permute-done.3.rest_1_ = bf16[192,128]{1,0:T(8,128)(2,1)S(1)} collective-permute-done((bf16[192,128]{1,0:T(8,128)(2,1)S(1)}, bf16[192,128]{1,0:T(8,128)(2,1)S(1)}, u32[]{:S(2)}, u32[]{:S(2)}) %collective-permute-start.3) | collective-permute-done | bytes 49184 | tf_op jit(solution)/shard_map/ppermute | solution.py:101
  9.2 0.2 collective-permute-done.2.rest_0_
  9.3 0.0 collective-permute-done.beside_ref
  9.4 0.0 copy-done
  9.4 0.0 copy-done.3
  9.4 0.0 copy-done.4
  9.4 0.0 copy-done.2
  9.4 0.6 %shard_map.74 = (bf16[416,128]{1,0:T(8,128)(2,1)S(1)}, f32[1,384,128]{2,1,0:T(8,128)S(1)}) custom-call(bf16[384,128]{1,0:T(8,128)(2,1)S(1)} %get-tuple-element.32.own_ref, bf16[4,384,128]{2,1,0:T(8,128)(2,1)S(1)} %collective-permute-done.beside_ref, bf16[384,128]{1,0:T(8,128)(2,1)S(1)} %collective-permute-done.1.across_ref, f32[4,128]{1,0:T(4,128)S(1)} %bitcast.6, ...), custom_call_target="tpu_custom_call" | custom-call | tf_op jit(solution)/shard_map/pallas_call | solution.py:105
  10.0 3.1 %collective-permute-start.4 = (bf16[416,128]{1,0:T(8,128)(2,1)S(1)}, bf16[416,128]{1,0:T(8,128)(2,1)S(1)}, u32[]{:S(2)}, u32[]{:S(2)}) collective-permute-start(bf16[416,128]{1,0:T(8,128)(2,1)S(1)} %get-tuple-element.34), channel_id=1, source_target_pairs={{0,8},{4,12},{8,0},{12,4},{1,9},{5,13},{9,1},{13,5},{2,10},{6,14},... | collective-permute-start | bytes 319496 | tf_op jit(solution)/shard_map/ppermute | solution.py:97
  13.1 0.8 %collective-permute-done.5 = bf16[1152,128]{1,0:T(8,128)(2,1)S(1)} collective-permute-done((bf16[1152,128]{1,0:T(8,128)(2,1)S(1)}, bf16[1152,128]{1,0:T(8,128)(2,1)S(1)}, u32[]{:S(2)}, u32[]{:S(2)}) %collective-permute-start.5) | collective-permute-done | bytes 294944 | tf_op jit(solution)/shard_map/ppermute | solution.py:101
  13.9 0.1 collective-permute-start.7
  14.0 0.5 %collective-permute-start.6 = (bf16[384,128]{1,0:T(8,128)(2,1)S(1)}, bf16[384,128]{1,0:T(8,128)(2,1)S(1)}, u32[]{:S(2)}, u32[]{:S(2)}) collective-permute-start(bf16[384,128]{1,0:T(8,128)(2,1)S(1)} %get-tuple-element.61), channel_id=1, source_target_pairs={{0,1},{1,0},{2,3},{3,2},{4,5},{5,4},{6,7},{7,6},{8,9},{9,8},{10,11... | collective-permute-start | bytes 294920 | tf_op jit(solution)/shard_map/ppermute | solution.py:101
  14.6 0.7 %collective-permute-done.7.rest_1_ = bf16[384,128]{1,0:T(8,128)(2,1)S(1)} collective-permute-done((bf16[384,128]{1,0:T(8,128)(2,1)S(1)}, bf16[384,128]{1,0:T(8,128)(2,1)S(1)}, u32[]{:S(2)}, u32[]{:S(2)}) %collective-permute-start.7) | collective-permute-done | bytes 98336 | tf_op jit(solution)/shard_map/ppermute | solution.py:101
  15.3 0.2 collective-permute-done.6.rest_0_
  15.5 0.9 %shard_map.75 = (bf16[416,128]{1,0:T(8,128)(2,1)S(1)}, bf16[416,128]{1,0:T(8,128)(2,1)S(1)}, f32[2,384,128]{2,1,0:T(8,128)S(1)}) custom-call(bf16[768,128]{1,0:T(8,128)(2,1)S(1)} %slice.28.own_ref, bf16[4,384,128]{2,1,0:T(8,128)(2,1)S(1)} %collective-permute-done.beside_ref, bf16[768,128]{1,0:T(8,128)(2,1)S(1)} %slice.29.across_ref, f32[4,128]{1,0:T(4,128)S(1)} %bitcast.7, ...), custom_call_target="tpu_custom_call" | custom-call | tf_op jit(solution)/shard_map/pallas_call | solution.py:105
  16.3 1.9 %collective-permute-start.8 = (bf16[416,128]{1,0:T(8,128)(2,1)S(1)}, bf16[416,128]{1,0:T(8,128)(2,1)S(1)}, u32[]{:S(2)}, u32[]{:S(2)}) collective-permute-start(bf16[416,128]{1,0:T(8,128)(2,1)S(1)} %get-tuple-element.37), channel_id=1, source_target_pairs={{0,4},{4,8},{8,12},{12,0},{1,5},{5,9},{9,13},{13,1},{2,6},{6,10},{... | collective-permute-start | bytes 319496 | tf_op jit(solution)/shard_map/ppermute | solution.py:97
  18.3 0.1 collective-permute-start.10
  18.3 0.0 copy-start.5
  18.3 2.4 %collective-permute-start.9 = (bf16[416,128]{1,0:T(8,128)(2,1)S(1)}, bf16[416,128]{1,0:T(8,128)(2,1)S(1)}, u32[]{:S(2)}, u32[]{:S(2)}) collective-permute-start(bf16[416,128]{1,0:T(8,128)(2,1)S(1)} %get-tuple-element.38), channel_id=1, source_target_pairs={{0,12},{4,0},{8,4},{12,8},{1,13},{5,1},{9,5},{13,9},{2,14},{6,2},{... | collective-permute-start | bytes 319496 | tf_op jit(solution)/shard_map/ppermute | solution.py:97
  20.7 0.0 collective-permute-done.4.block_ref.refs_0_
  20.7 0.0 copy-done.5
  20.7 0.0 collective-permute-done.10.rest_0_
  20.7 0.6 %shard_map.76 = (bf16[416,128]{1,0:T(8,128)(2,1)S(1)}, f32[1,384,128]{2,1,0:T(8,128)S(1)}) custom-call(bf16[384,128]{1,0:T(8,128)(2,1)S(1)} %slice.32.own_ref, bf16[4,384,128]{2,1,0:T(8,128)(2,1)S(1)} %collective-permute-done.beside_ref, bf16[384,128]{1,0:T(8,128)(2,1)S(1)} %get-tuple-element.39.across_ref, f32[4,128]{1,0:T(4,128)S(1)} %bitcast.8, ...), custom_call_target="tpu_custom_call" | custom-call | tf_op jit(solution)/shard_map/pallas_call | solution.py:105
  21.3 4.6 %collective-permute-done.9.refs_2_ = bf16[416,128]{1,0:T(8,128)(2,1)S(1)} collective-permute-done((bf16[416,128]{1,0:T(8,128)(2,1)S(1)}, bf16[416,128]{1,0:T(8,128)(2,1)S(1)}, u32[]{:S(2)}, u32[]{:S(2)}) %collective-permute-start.9) | collective-permute-done | bytes 106528 | tf_op jit(solution)/shard_map/ppermute | solution.py:97
  25.9 0.0 collective-permute-done.8.refs_1_
  25.9 0.0 copy-start.1
  25.9 2.5 %shard_map.78 = (bf16[400,128]{1,0:T(8,128)(2,1)S(1)}, bf16[400,128]{1,0:T(8,128)(2,1)S(1)}, bf16[400,128]{1,0:T(8,128)(2,1)S(1)}, bf16[400,128]{1,0:T(8,128)(2,1)S(1)}) custom-call(bf16[416,128]{1,0:T(8,128)(2,1)S(1)} %collective-permute-done.4.block_ref.refs_0_, bf16[416,128]{1,0:T(8,128)(2,1)S(1)} %collective-permute-done.8.refs_1_, ...), custom_call_target="tpu_custom_call" | custom-call | tf_op jit(solution)/shard_map/pallas_call | solution.py:105
  28.5 0.8 %collective-permute-start.14 = (bf16[400,128]{1,0:T(8,128)(2,1)S(1)}, bf16[400,128]{1,0:T(8,128)(2,1)S(1)}, u32[]{:S(2)}, u32[]{:S(2)}) collective-permute-start(bf16[400,128]{1,0:T(8,128)(2,1)S(1)} %get-tuple-element.48), channel_id=1, source_target_pairs={{0,4},{4,8},{8,12},{12,0},{1,5},{5,9},{9,13},{13,1},{2,6},{6,10},{... | collective-permute-start | bytes 307208 | tf_op jit(solution)/shard_map/ppermute | solution.py:97
  29.2 3.1 %collective-permute-start.15 = (bf16[400,128]{1,0:T(8,128)(2,1)S(1)}, bf16[400,128]{1,0:T(8,128)(2,1)S(1)}, u32[]{:S(2)}, u32[]{:S(2)}) collective-permute-start(bf16[400,128]{1,0:T(8,128)(2,1)S(1)} %get-tuple-element.50), channel_id=1, source_target_pairs={{0,12},{4,0},{8,4},{12,8},{1,13},{5,1},{9,5},{13,9},{2,14},{6,2},{... | collective-permute-start | bytes 307208 | tf_op jit(solution)/shard_map/ppermute | solution.py:97
  32.3 0.0 collective-permute-start.13
  32.3 0.0 copy-done.1
  32.4 0.1 collective-permute-start.11
  32.5 1.5 %collective-permute-start.12 = (bf16[640,128]{1,0:T(8,128)(2,1)S(1)}, bf16[640,128]{1,0:T(8,128)(2,1)S(1)}, u32[]{:S(2)}, u32[]{:S(2)}) collective-permute-start(bf16[640,128]{1,0:T(8,128)(2,1)S(1)} %get-tuple-element.45.refs_0_), channel_id=1, source_target_pairs={{0,2},{1,3},{2,0},{3,1},{4,6},{5,7},{6,4},{7,5},{8,10},{9,11},{10,... | collective-permute-start | bytes 491528 | tf_op jit(solution)/shard_map/ppermute | solution.py:101
  34.0 2.1 %collective-permute-done.14.refs_0_ = bf16[400,128]{1,0:T(8,128)(2,1)S(1)} collective-permute-done((bf16[400,128]{1,0:T(8,128)(2,1)S(1)}, bf16[400,128]{1,0:T(8,128)(2,1)S(1)}, u32[]{:S(2)}, u32[]{:S(2)}) %collective-permute-start.14) | collective-permute-done | bytes 102432 | tf_op jit(solution)/shard_map/ppermute | solution.py:97
  36.1 0.3 collective-permute-done.15.refs_1_
  36.4 1.6 %collective-permute-start.18 = (bf16[768,128]{1,0:T(8,128)(2,1)S(1)}, bf16[768,128]{1,0:T(8,128)(2,1)S(1)}, u32[]{:S(2)}, u32[]{:S(2)}) collective-permute-start(bf16[768,128]{1,0:T(8,128)(2,1)S(1)} %shard_map.80.refs_4_), channel_id=1, source_target_pairs={{0,2},{1,3},{2,0},{3,1},{4,6},{5,7},{6,4},{7,5},{8,10},{9,11},{10,... | collective-permute-start | bytes 589832 | tf_op jit(solution)/shard_map/ppermute | solution.py:101
  38.0 2.5 %collective-permute-done.13.refs_0_ = bf16[400,128]{1,0:T(8,128)(2,1)S(1)} collective-permute-done((bf16[400,128]{1,0:T(8,128)(2,1)S(1)}, bf16[400,128]{1,0:T(8,128)(2,1)S(1)}, u32[]{:S(2)}, u32[]{:S(2)}) %collective-permute-start.13) | collective-permute-done | bytes 102432 | tf_op jit(solution)/shard_map/ppermute | solution.py:97
  40.5 0.0 collective-permute-done.12.refs_2_
  40.5 1.5 %collective-permute-start.21 = (bf16[384,128]{1,0:T(8,128)(2,1)S(1)}, bf16[384,128]{1,0:T(8,128)(2,1)S(1)}, u32[]{:S(2)}, u32[]{:S(2)}) collective-permute-start(bf16[384,128]{1,0:T(8,128)(2,1)S(1)} %shard_map.81.refs_8_), channel_id=1, source_target_pairs={{0,2},{1,3},{2,0},{3,1},{4,6},{5,7},{6,4},{7,5},{8,10},{9,11},{10,... | collective-permute-start | bytes 294920 | tf_op jit(solution)/shard_map/ppermute | solution.py:101
  42.0 0.0 collective-permute-start.17
  42.0 1.6 %collective-permute-done.18.refs_6_ = bf16[768,128]{1,0:T(8,128)(2,1)S(1)} collective-permute-done((bf16[768,128]{1,0:T(8,128)(2,1)S(1)}, bf16[768,128]{1,0:T(8,128)(2,1)S(1)}, u32[]{:S(2)}, u32[]{:S(2)}) %collective-permute-start.18) | collective-permute-done | bytes 196640 | tf_op jit(solution)/shard_map/ppermute | solution.py:101
  43.6 0.0 collective-permute-start.19
  43.6 0.5 %collective-permute-start.16 = (bf16[640,128]{1,0:T(8,128)(2,1)S(1)}, bf16[640,128]{1,0:T(8,128)(2,1)S(1)}, u32[]{:S(2)}, u32[]{:S(2)}) collective-permute-start(bf16[640,128]{1,0:T(8,128)(2,1)S(1)} %collective-permute-done.12.refs_2_), channel_id=1, source_target_pairs={{0,1},{1,0},{2,3},{3,2},{4,5},{5,4},{6,7},{7,6},{8,9},{9,8},{10,11... | collective-permute-start | bytes 491528 | tf_op jit(solution)/shard_map/ppermute | solution.py:101
  44.2 1.2 %collective-permute-done.21.refs_10_ = bf16[384,128]{1,0:T(8,128)(2,1)S(1)} collective-permute-done((bf16[384,128]{1,0:T(8,128)(2,1)S(1)}, bf16[384,128]{1,0:T(8,128)(2,1)S(1)}, u32[]{:S(2)}, u32[]{:S(2)}) %collective-permute-start.21) | collective-permute-done | bytes 98336 | tf_op jit(solution)/shard_map/ppermute | solution.py:101
  45.4 0.0 collective-permute-start.20
  45.4 0.0 collective-permute-done.11.refs_1_
  45.4 0.5 %collective-permute-start.22 = (bf16[384,128]{1,0:T(8,128)(2,1)S(1)}, bf16[384,128]{1,0:T(8,128)(2,1)S(1)}, u32[]{:S(2)}, u32[]{:S(2)}) collective-permute-start(bf16[384,128]{1,0:T(8,128)(2,1)S(1)} %collective-permute-done.21.refs_10_), channel_id=1, source_target_pairs={{0,1},{1,0},{2,3},{3,2},{4,5},{5,4},{6,7},{7,6},{8,9},{9,8},{10,11... | collective-permute-start | bytes 294920 | tf_op jit(solution)/shard_map/ppermute | solution.py:101
  45.9 0.8 %collective-permute-done.20.refs_9_ = bf16[384,128]{1,0:T(8,128)(2,1)S(1)} collective-permute-done((bf16[384,128]{1,0:T(8,128)(2,1)S(1)}, bf16[384,128]{1,0:T(8,128)(2,1)S(1)}, u32[]{:S(2)}, u32[]{:S(2)}) %collective-permute-start.20) | collective-permute-done | bytes 98336 | tf_op jit(solution)/shard_map/ppermute | solution.py:101
  46.7 0.0 collective-permute-done.17.refs_5_
  46.7 0.0 collective-permute-done.16.refs_3_
  46.7 0.2 collective-permute-done.22.refs_11_
  46.9 0.0 collective-permute-done.19.refs_7_
  46.9 1.3 %shard_map.82 = bf16[4,384,128]{2,1,0:T(8,128)(2,1)} custom-call(bf16[640,128]{1,0:T(8,128)(2,1)S(1)} %get-tuple-element.45.refs_0_, bf16[512,128]{1,0:T(8,128)(2,1)S(1)} %collective-permute-done.11.refs_1_, bf16[640,128]{1,0:T(8,128)(2,1)S(1)} %collective-permute-done.12.refs_2_, bf16[640,128]{1,0:T(8,128)(2,1)S(1)} %collective-permute-done.16.refs_3_, ...), custom_call_target="tpu_custom_call" | custom-call | tf_op jit(solution)/shard_map/pallas_call | solution.py:377
  (9 shorter events, 0.2 us)
Async XLA Ops:
  0.0 9.4 %copy-start = (bf16[512,3,128]{2,0,1:T(8,128)(2,1)S(1)}, bf16[512,3,128]{2,0,1:T(8,128)(2,1)}, u32[]{:S(2)}) copy-start(bf16[512,3,128]{2,0,1:T(8,128)(2,1)} %param.9) | copy-start | bytes 1179652
  1.1 8.2 %collective-permute-start = (bf16[4,384,128]{2,1,0:T(8,128)(2,1)}, bf16[4,384,128]{2,1,0:T(8,128)(2,1)S(1)}, u32[]{:S(2)}, u32[]{:S(2)}) collective-permute-start(bf16[4,384,128]{2,1,0:T(8,128)(2,1)} %records_ref.1), channel_id=1, source_target_pairs={{0,1},{1,0},{2,3},{3,2},{4,5},{5,4},{6,7},{7,6},{8,9},{9,8},{10,11... | collective-permute-start | bytes 1179656 | tf_op jit(solution)/shard_map/ppermute | solution.py:101
  1.6 6.2 %collective-permute-start.1 = (bf16[384,128]{1,0:T(8,128)(2,1)S(1)}, bf16[384,128]{1,0:T(8,128)(2,1)S(1)}, u32[]{:S(2)}, u32[]{:S(2)}) collective-permute-start(bf16[384,128]{1,0:T(8,128)(2,1)S(1)} %get-tuple-element.32.own_ref), channel_id=1, source_target_pairs={{0,2},{1,3},{2,0},{3,1},{4,6},{5,7},{6,4},{7,5},{8,10},{9,11},{10,... | collective-permute-start | bytes 294920 | tf_op jit(solution)/shard_map/ppermute | solution.py:101
  4.2 9.7 %collective-permute-start.5 = (bf16[1152,128]{1,0:T(8,128)(2,1)S(1)}, bf16[1152,128]{1,0:T(8,128)(2,1)S(1)}, u32[]{:S(2)}, u32[]{:S(2)}) collective-permute-start(bf16[1152,128]{1,0:T(8,128)(2,1)S(1)} %get-tuple-element.35), channel_id=1, source_target_pairs={{0,2},{1,3},{2,0},{3,1},{4,6},{5,7},{6,4},{7,5},{8,10},{9,11},{10,... | collective-permute-start | bytes 884744 | tf_op jit(solution)/shard_map/ppermute | solution.py:101
  7.9 1.5 %copy-start.3 = (bf16[4,384]{1,0:T(4,128)(2,1)S(1)}, bf16[4,384]{1,0:T(4,128)(2,1)}, u32[]{:S(2)}) copy-start(bf16[4,384]{1,0:T(4,128)(2,1)} %taps_ref.5) | copy-start | bytes 9220
  7.9 1.5 %copy-start.4 = (f32[512]{0:T(512)S(1)}, f32[512]{0:T(512)}, u32[]{:S(2)}) copy-start(f32[512]{0:T(512)} %param.8) | copy-start | bytes 6148
  7.9 1.5 %copy-start.2 = (f32[3,3,128]{2,1,0:T(4,128)S(1)}, f32[3,3,128]{2,1,0:T(4,128)}, u32[]{:S(2)}) copy-start(f32[3,3,128]{2,1,0:T(4,128)} %refs_2_.3) | copy-start | bytes 13828
  7.9 1.3 %collective-permute-start.3 = (bf16[192,128]{1,0:T(8,128)(2,1)S(1)}, bf16[192,128]{1,0:T(8,128)(2,1)S(1)}, u32[]{:S(2)}, u32[]{:S(2)}) collective-permute-start(bf16[192,128]{1,0:T(8,128)(2,1)S(1)} %get-tuple-element.62), channel_id=1, source_target_pairs={{0,1},{1,0},{2,3},{3,2},{4,5},{5,4},{6,7},{7,6},{8,9},{9,8},{10,11... | collective-permute-start | bytes 147464 | tf_op jit(solution)/shard_map/ppermute | solution.py:101
  8.0 1.4 %collective-permute-start.2 = (bf16[192,128]{1,0:T(8,128)(2,1)S(1)}, bf16[192,128]{1,0:T(8,128)(2,1)S(1)}, u32[]{:S(2)}, u32[]{:S(2)}) collective-permute-start(bf16[192,128]{1,0:T(8,128)(2,1)S(1)} %get-tuple-element.63), channel_id=1, source_target_pairs={{0,1},{1,0},{2,3},{3,2},{4,5},{5,4},{6,7},{7,6},{8,9},{9,8},{10,11... | collective-permute-start | bytes 147464 | tf_op jit(solution)/shard_map/ppermute | solution.py:101
  10.0 10.7 %collective-permute-start.4 = (bf16[416,128]{1,0:T(8,128)(2,1)S(1)}, bf16[416,128]{1,0:T(8,128)(2,1)S(1)}, u32[]{:S(2)}, u32[]{:S(2)}) collective-permute-start(bf16[416,128]{1,0:T(8,128)(2,1)S(1)} %get-tuple-element.34), channel_id=1, source_target_pairs={{0,8},{4,12},{8,0},{12,4},{1,9},{5,13},{9,1},{13,5},{2,10},{6,14},... | collective-permute-start | bytes 319496 | tf_op jit(solution)/shard_map/ppermute | solution.py:97
  13.9 1.4 %collective-permute-start.7 = (bf16[384,128]{1,0:T(8,128)(2,1)S(1)}, bf16[384,128]{1,0:T(8,128)(2,1)S(1)}, u32[]{:S(2)}, u32[]{:S(2)}) collective-permute-start(bf16[384,128]{1,0:T(8,128)(2,1)S(1)} %get-tuple-element.60), channel_id=1, source_target_pairs={{0,1},{1,0},{2,3},{3,2},{4,5},{5,4},{6,7},{7,6},{8,9},{9,8},{10,11... | collective-permute-start | bytes 294920 | tf_op jit(solution)/shard_map/ppermute | solution.py:101
  14.0 1.4 %collective-permute-start.6 = (bf16[384,128]{1,0:T(8,128)(2,1)S(1)}, bf16[384,128]{1,0:T(8,128)(2,1)S(1)}, u32[]{:S(2)}, u32[]{:S(2)}) collective-permute-start(bf16[384,128]{1,0:T(8,128)(2,1)S(1)} %get-tuple-element.61), channel_id=1, source_target_pairs={{0,1},{1,0},{2,3},{3,2},{4,5},{5,4},{6,7},{7,6},{8,9},{9,8},{10,11... | collective-permute-start | bytes 294920 | tf_op jit(solution)/shard_map/ppermute | solution.py:101
  16.3 9.6 %collective-permute-start.8 = (bf16[416,128]{1,0:T(8,128)(2,1)S(1)}, bf16[416,128]{1,0:T(8,128)(2,1)S(1)}, u32[]{:S(2)}, u32[]{:S(2)}) collective-permute-start(bf16[416,128]{1,0:T(8,128)(2,1)S(1)} %get-tuple-element.37), channel_id=1, source_target_pairs={{0,4},{4,8},{8,12},{12,0},{1,5},{5,9},{9,13},{13,1},{2,6},{6,10},{... | collective-permute-start | bytes 319496 | tf_op jit(solution)/shard_map/ppermute | solution.py:97
  18.3 2.5 %collective-permute-start.10 = (bf16[384,128]{1,0:T(8,128)(2,1)S(1)}, bf16[384,128]{1,0:T(8,128)(2,1)S(1)}, u32[]{:S(2)}, u32[]{:S(2)}) collective-permute-start(bf16[384,128]{1,0:T(8,128)(2,1)S(1)} %get-tuple-element.39.across_ref), channel_id=1, source_target_pairs={{0,1},{1,0},{2,3},{3,2},{4,5},{5,4},{6,7},{7,6},{8,9},{9,8},{10,11... | collective-permute-start | bytes 294920 | tf_op jit(solution)/shard_map/ppermute | solution.py:101
  18.3 2.4 %copy-start.5 = (f32[128]{0:T(128)S(1)}, f32[128]{0:T(128)}, u32[]{:S(2)}) copy-start(f32[128]{0:T(128)} %param.12) | copy-start | bytes 1540
  18.3 7.6 %collective-permute-start.9 = (bf16[416,128]{1,0:T(8,128)(2,1)S(1)}, bf16[416,128]{1,0:T(8,128)(2,1)S(1)}, u32[]{:S(2)}, u32[]{:S(2)}) collective-permute-start(bf16[416,128]{1,0:T(8,128)(2,1)S(1)} %get-tuple-element.38), channel_id=1, source_target_pairs={{0,12},{4,0},{8,4},{12,8},{1,13},{5,1},{9,5},{13,9},{2,14},{6,2},{... | collective-permute-start | bytes 319496 | tf_op jit(solution)/shard_map/ppermute | solution.py:97
  25.9 6.4 %copy-start.1 = (bf16[128,512]{1,0:T(8,128)(2,1)S(1)}, bf16[128,512]{1,0:T(8,128)(2,1)}, u32[]{:S(2)}) copy-start(bf16[128,512]{1,0:T(8,128)(2,1)} %refs_12_.1) | copy-start | bytes 393220
  28.5 7.6 %collective-permute-start.14 = (bf16[400,128]{1,0:T(8,128)(2,1)S(1)}, bf16[400,128]{1,0:T(8,128)(2,1)S(1)}, u32[]{:S(2)}, u32[]{:S(2)}) collective-permute-start(bf16[400,128]{1,0:T(8,128)(2,1)S(1)} %get-tuple-element.48), channel_id=1, source_target_pairs={{0,4},{4,8},{8,12},{12,0},{1,5},{5,9},{9,13},{13,1},{2,6},{6,10},{... | collective-permute-start | bytes 307208 | tf_op jit(solution)/shard_map/ppermute | solution.py:97
  29.2 7.1 %collective-permute-start.15 = (bf16[400,128]{1,0:T(8,128)(2,1)S(1)}, bf16[400,128]{1,0:T(8,128)(2,1)S(1)}, u32[]{:S(2)}, u32[]{:S(2)}) collective-permute-start(bf16[400,128]{1,0:T(8,128)(2,1)S(1)} %get-tuple-element.50), channel_id=1, source_target_pairs={{0,12},{4,0},{8,4},{12,8},{1,13},{5,1},{9,5},{13,9},{2,14},{6,2},{... | collective-permute-start | bytes 307208 | tf_op jit(solution)/shard_map/ppermute | solution.py:97
  32.3 8.1 %collective-permute-start.13 = (bf16[400,128]{1,0:T(8,128)(2,1)S(1)}, bf16[400,128]{1,0:T(8,128)(2,1)S(1)}, u32[]{:S(2)}, u32[]{:S(2)}) collective-permute-start(bf16[400,128]{1,0:T(8,128)(2,1)S(1)} %get-tuple-element.47), channel_id=1, source_target_pairs={{0,8},{4,12},{8,0},{12,4},{1,9},{5,13},{9,1},{13,5},{2,10},{6,14},... | collective-permute-start | bytes 307208 | tf_op jit(solution)/shard_map/ppermute | solution.py:97
  32.4 13.0 %collective-permute-start.11 = (bf16[512,128]{1,0:T(8,128)(2,1)S(1)}, bf16[512,128]{1,0:T(8,128)(2,1)S(1)}, u32[]{:S(2)}, u32[]{:S(2)}) collective-permute-start(bf16[512,128]{1,0:T(8,128)(2,1)S(1)} %get-tuple-element.46), channel_id=1, source_target_pairs={{0,1},{1,0},{2,3},{3,2},{4,5},{5,4},{6,7},{7,6},{8,9},{9,8},{10,11... | collective-permute-start | bytes 393224 | tf_op jit(solution)/shard_map/ppermute | solution.py:101
  32.5 8.0 %collective-permute-start.12 = (bf16[640,128]{1,0:T(8,128)(2,1)S(1)}, bf16[640,128]{1,0:T(8,128)(2,1)S(1)}, u32[]{:S(2)}, u32[]{:S(2)}) collective-permute-start(bf16[640,128]{1,0:T(8,128)(2,1)S(1)} %get-tuple-element.45.refs_0_), channel_id=1, source_target_pairs={{0,2},{1,3},{2,0},{3,1},{4,6},{5,7},{6,4},{7,5},{8,10},{9,11},{10,... | collective-permute-start | bytes 491528 | tf_op jit(solution)/shard_map/ppermute | solution.py:101
  36.4 7.3 %collective-permute-start.18 = (bf16[768,128]{1,0:T(8,128)(2,1)S(1)}, bf16[768,128]{1,0:T(8,128)(2,1)S(1)}, u32[]{:S(2)}, u32[]{:S(2)}) collective-permute-start(bf16[768,128]{1,0:T(8,128)(2,1)S(1)} %shard_map.80.refs_4_), channel_id=1, source_target_pairs={{0,2},{1,3},{2,0},{3,1},{4,6},{5,7},{6,4},{7,5},{8,10},{9,11},{10,... | collective-permute-start | bytes 589832 | tf_op jit(solution)/shard_map/ppermute | solution.py:101
  40.5 4.9 %collective-permute-start.21 = (bf16[384,128]{1,0:T(8,128)(2,1)S(1)}, bf16[384,128]{1,0:T(8,128)(2,1)S(1)}, u32[]{:S(2)}, u32[]{:S(2)}) collective-permute-start(bf16[384,128]{1,0:T(8,128)(2,1)S(1)} %shard_map.81.refs_8_), channel_id=1, source_target_pairs={{0,2},{1,3},{2,0},{3,1},{4,6},{5,7},{6,4},{7,5},{8,10},{9,11},{10,... | collective-permute-start | bytes 294920 | tf_op jit(solution)/shard_map/ppermute | solution.py:101
  42.0 4.7 %collective-permute-start.17 = (bf16[768,128]{1,0:T(8,128)(2,1)S(1)}, bf16[768,128]{1,0:T(8,128)(2,1)S(1)}, u32[]{:S(2)}, u32[]{:S(2)}) collective-permute-start(bf16[768,128]{1,0:T(8,128)(2,1)S(1)} %shard_map.80.refs_4_), channel_id=1, source_target_pairs={{0,1},{1,0},{2,3},{3,2},{4,5},{5,4},{6,7},{7,6},{8,9},{9,8},{10,11... | collective-permute-start | bytes 589832 | tf_op jit(solution)/shard_map/ppermute | solution.py:101
  43.6 3.2 %collective-permute-start.19 = (bf16[768,128]{1,0:T(8,128)(2,1)S(1)}, bf16[768,128]{1,0:T(8,128)(2,1)S(1)}, u32[]{:S(2)}, u32[]{:S(2)}) collective-permute-start(bf16[768,128]{1,0:T(8,128)(2,1)S(1)} %collective-permute-done.18.refs_6_), channel_id=1, source_target_pairs={{0,1},{1,0},{2,3},{3,2},{4,5},{5,4},{6,7},{7,6},{8,9},{9,8},{10,11... | collective-permute-start | bytes 589832 | tf_op jit(solution)/shard_map/ppermute | solution.py:101
  43.6 3.1 %collective-permute-start.16 = (bf16[640,128]{1,0:T(8,128)(2,1)S(1)}, bf16[640,128]{1,0:T(8,128)(2,1)S(1)}, u32[]{:S(2)}, u32[]{:S(2)}) collective-permute-start(bf16[640,128]{1,0:T(8,128)(2,1)S(1)} %collective-permute-done.12.refs_2_), channel_id=1, source_target_pairs={{0,1},{1,0},{2,3},{3,2},{4,5},{5,4},{6,7},{7,6},{8,9},{9,8},{10,11... | collective-permute-start | bytes 491528 | tf_op jit(solution)/shard_map/ppermute | solution.py:101
  45.4 1.3 %collective-permute-start.20 = (bf16[384,128]{1,0:T(8,128)(2,1)S(1)}, bf16[384,128]{1,0:T(8,128)(2,1)S(1)}, u32[]{:S(2)}, u32[]{:S(2)}) collective-permute-start(bf16[384,128]{1,0:T(8,128)(2,1)S(1)} %shard_map.81.refs_8_), channel_id=1, source_target_pairs={{0,1},{1,0},{2,3},{3,2},{4,5},{5,4},{6,7},{7,6},{8,9},{9,8},{10,11... | collective-permute-start | bytes 294920 | tf_op jit(solution)/shard_map/ppermute | solution.py:101
  45.4 1.5 %collective-permute-start.22 = (bf16[384,128]{1,0:T(8,128)(2,1)S(1)}, bf16[384,128]{1,0:T(8,128)(2,1)S(1)}, u32[]{:S(2)}, u32[]{:S(2)}) collective-permute-start(bf16[384,128]{1,0:T(8,128)(2,1)S(1)} %collective-permute-done.21.refs_10_), channel_id=1, source_target_pairs={{0,1},{1,0},{2,3},{3,2},{4,5},{5,4},{6,7},{7,6},{8,9},{9,8},{10,11... | collective-permute-start | bytes 294920 | tf_op jit(solution)/shard_map/ppermute | solution.py:101

commit v4 on v3

--- a/solution.py
+++ b/solution.py
@@ -7,17 +7,8 @@
 
 LANES = 128
 EXTRA = 32
-SPLIT = 1
-SPACE = 1 << 31
-FAR = 1 << 32
-NEAR = (1, 3)
-TIE = 1
-FARD = (2,)
-ORDER = (2, 1, 3)
-BESIDE = 1
-OWNSEP = 1
-SPLIT1 = 2
-COST = pl.CostEstimate(flops=0, bytes_accessed=0, transcendentals=0)
+NO_COST = pl.CostEstimate(flops=0, bytes_accessed=0, transcendentals=0)
+EARLY_COST, FAR_COST = 1 << 30, 1 << 33
 BACK = 16
 VMEM = pltpu.VMEM
 
@@ -143,7 +134,7 @@
         in_specs=[pl.BlockSpec(memory_space=pl.ANY)],
         out_specs=tuple(pl.BlockSpec(memory_space=VMEM) for _ in shapes),
         scratch_shapes=[pltpu.SemaphoreType.DMA((count,))],
-        cost_estimate=COST,
+        cost_estimate=NO_COST,
     )(records)
 
 
@@ -347,100 +338,100 @@
     return vmem_call(kernel, outs, [], *sums, *arrays, short_kernel, *extra, cost=cost)
 
 
-def mix(slabs, out_projection, distances, block_len):
+def mix(slabs, out_projection, distances, shape, mixed=None):
     f32, bf16 = jnp.float32, jnp.bfloat16
-    count = sum(len(d) for d in distances)
+    count, block_len, _ = shape
     groups = len(slabs)
+    records = sum(len(d) for d in distances)
+    first = mixed is None
 
     def kernel(*refs):
-        slab_refs, (w_ref, out_ref, w_all, mixed, sems) = refs[: 4 * groups], refs[4 * groups :]
+        slab_refs, w_ref, rest = refs[: 4 * groups], refs[4 * groups], refs[4 * groups + 1 :]
+        if first:
+            out_ref, w_all, results, sems = rest
+            me = lax.axis_index("chan")
+            start = len(distances[0]) * block_len
+            w_all[0:LANES, :] = w_ref[:, pl.ds(pl.multiple_of(me * LANES, LANES), LANES)]
+            w_all[LANES : 2 * LANES, :] = slab_refs[1][start : start + LANES, :]
+            w_all[2 * LANES : 3 * LANES, :] = slab_refs[2][start : start + LANES, :]
+            w_all[3 * LANES :, :] = slab_refs[3][start + LANES : start + 2 * LANES, :]
+        else:
+            w_all, (_, out_ref, results, sems) = w_ref, rest
+        z = lax.axis_index("seq")
         copies = []
-        me = lax.axis_index("chan")
-        z = lax.axis_index("seq")
-        start = len(distances[0]) * block_len
-        w_all[0:LANES, :] = w_ref[:, pl.ds(pl.multiple_of(me * LANES, LANES), LANES)]
-        w_all[LANES : 2 * LANES, :] = slab_refs[1][start : start + LANES, :]
-        w_all[2 * LANES : 3 * LANES, :] = slab_refs[2][start : start + LANES, :]
-        w_all[3 * LANES :, :] = slab_refs[3][start + LANES : start + 2 * LANES, :]
         for g in range(groups):
             for i, k in enumerate(distances[g]):
                 rows = slice(i * block_len, (i + 1) * block_len)
                 lhs = jnp.concatenate([ref[rows, :] for ref in slab_refs[4 * g : 4 * g + 4]], axis=1)
                 n = len(copies)
-                mixed[n] = jnp.dot(lhs, w_all[...], preferred_element_type=f32).astype(bf16)
-                copies.append(pltpu.make_async_copy(mixed.at[n], out_ref.at[lax.rem(z + k, count)], sems.at[n]))
+                results[n] = jnp.dot(lhs, w_all[...], preferred_element_type=f32).astype(bf16)
+                copies.append(pltpu.make_async_copy(results.at[n], out_ref.at[lax.rem(z + k, count)], sems.at[n]))
                 copies[n].start()
         for copy in copies:
             copy.wait()
 
+    whole, anywhere = pl.BlockSpec(memory_space=VMEM), pl.BlockSpec(memory_space=pl.ANY)
     operands = [x for slab in slabs for x in slab] + [out_projection]
+    out_shape, out_specs = [jax.ShapeDtypeStruct(shape, bf16)], [anywhere]
+    if first:
+        out_shape.append(VMEM((4 * LANES, LANES), bf16))
+        out_specs.append(whole)
     return pl.pallas_call(
         kernel,
-        out_shape=jax.ShapeDtypeStruct((count, block_len, LANES), bf16),
-        in_specs=[pl.BlockSpec(memory_space=VMEM)] * len(operands),
-        out_specs=pl.BlockSpec(memory_space=pl.ANY),
-        scratch_shapes=[
-            pltpu.VMEM((4 * LANES, LANES), bf16),
-            pltpu.VMEM((count, block_len, LANES), bf16),
-            pltpu.SemaphoreType.DMA((count,)),
-        ],
+        out_shape=tuple(out_shape),
+        in_specs=[whole] * len(operands) + ([] if first else [anywhere]),
+        out_specs=tuple(out_specs),
+        input_output_aliases={} if first else {len(operands): 0},
+        scratch_shapes=[pltpu.VMEM((records, block_len, LANES), bf16), pltpu.SemaphoreType.DMA((records,))],
         compiler_params=pltpu.CompilerParams(vmem_limit_bytes=40 * 1024 * 1024),
-        cost_estimate=COST,
-    )(*operands)
+        cost_estimate=NO_COST,
+    )(*operands, *([] if first else [mixed]))
 
 
 def exchange_body(records, norm_gain, in_projection, short_kernel, long_filter, skip_gain, out_projection):
-    block_len = records.shape[1]
     weights = jnp.transpose(in_projection, (1, 0, 2))
     gain = norm_gain.reshape(4, LANES)
     skip = skip_gain.reshape(1, LANES)
 
-    groups = ((2,), (1, 3, 0))
-    picked = pick(records, groups)
-    across = [exchange(block, "chan", 2) for block in picked]
-    beside = exchange(after(records, picked[0]) if BESIDE else records, "chan", 1)
+    (first,) = pick(records, ((2,),))
+    second, third = pick(records, ((1, 3), (0,)))
+    across_first, across_second, across_third = (exchange(block, "chan", 2) for block in (first, second, third))
+    beside = exchange(after(records, first), "chan", 1)
 
     def projected(offsets, own, far, pieces):
         size = far.shape[0] // pieces
         diagonal = [exchange(far[i * size : (i + 1) * size], "chan", 1) for i in range(pieces)]
         return project(own, beside, far, diagonal, gain, weights, short_kernel, long_filter, offsets)
 
-    query = {}
-    (to_two,), query_two = projected((2,), picked[0], across[0], SPLIT1)
+    (to_two,), query_two = projected((2,), first, across_first, 2)
     from_two = rotate(to_two, "seq", 2)
-    second = after(across[1], to_two)
-    if OWNSEP:
-        rows = 2 * block_len
-        (to_one, to_three), query_near = projected((1, 3), picked[1][:rows], second[:rows], 2 * SPLIT)
-        last = after(second[rows:], to_one)
-        (kept,), query_own = projected((0,), picked[1][rows:], last, 1)
-        query = {0: (query_own, 0), 1: (query_near, 1), 3: (query_near, 0), 2: (query_two, 0)}
-    else:
-        (to_one, to_three, kept), query_rest = projected((1, 3, 0), picked[1], second, 3 * SPLIT)
-        query = {0: (query_rest, 2), 1: (query_rest, 1), 3: (query_rest, 0), 2: (query_two, 0)}
+    (to_one, to_three), query_near = projected((1, 3), second, after(across_second, to_two), 2)
     from_one = rotate(to_one, "seq", 1)
     from_three = rotate(to_three, "seq", 3)
-
-    tail, skip = tail_rows(from_two, skip, SPACE)
+    (kept,), query_own = projected((0,), third, after(across_third, to_one), 1)
+
+    tail, skip = tail_rows(from_two, skip, EARLY_COST)
     back_two, back_one, back_three, back_own = long_convolution(
         (from_two, from_one, from_three, kept), (2, 1, 3, 0), tail, short_kernel, skip
     )
-    back = {1: back_one, 2: back_two, 3: back_three}
-    sums = {k: rotate(back[k], "seq", k) for k in ORDER}
-
-    own, own_beside = gate([back_own], [query[0]], short_kernel, out_projection)
+    sums_two = rotate(back_two, "seq", 2)
+    sums_one = rotate(back_one, "seq", 1)
+    sums_three = rotate(back_three, "seq", 3)
+
+    own, own_beside = gate([back_own], [(query_own, 0)], short_kernel, out_projection)
     own_over = exchange(own, "chan", 2)
-    (near,) = gate([after(sums[k], own) for k in NEAR], [query[k] for k in NEAR], short_kernel)
-    (far,) = gate([after(sums[k], near, own_over) if TIE == 0 else after(sums[k], near) for k in FARD], [query[k] for k in FARD], short_kernel, cost=FAR)
-    if TIE == 1:
-        far = after(far, own_over)
-    slabs = []
-    for gated, beside, over in ((own, own_beside, own_over), (near, near, None), (far, far, None)):
-        if over is None:
-            over = exchange(gated, "chan", 2)
-        slabs.append((gated, exchange(beside, "chan", 1), over, exchange(after(over, far), "chan", 1)))
-    places = [tuple((4 - k) % 4 for k in group) for group in ((0,), NEAR, FARD)]
-    return mix(slabs, out_projection, places, block_len)
+    (near,) = gate([after(sums_one, own), after(sums_three, own)], [(query_near, 1), (query_near, 0)], short_kernel)
+    near_over = exchange(near, "chan", 2)
+    (far,) = gate([after(sums_two, near)], [(query_two, 0)], short_kernel, cost=FAR_COST)
+    far = after(far, own_over)
+    far_over = exchange(far, "chan", 2)
+
+    def slab(gated, beside, over):
+        return (gated, exchange(beside, "chan", 1), over, exchange(after(over, far), "chan", 1))
+
+    early = [slab(own, own_beside, own_over), slab(near, near, near_over)]
+    mixed, columns = mix(early, out_projection, ((0,), (3, 1)), records.shape)
+    return mix([slab(far, far, far_over)], columns, ((2,),), records.shape, mixed)[0]
 
 
 def solution(mesh):

time: 48.3 us -> 47.2 us (0.977)
  waiting for transfers between devices: 19.4 us -> 13.2 us
  starting transfers between devices: 21.4 us -> 24.8 us
  Pallas kernels: 7.14 us -> 8.87 us
    ppermute x17 -> x18, starting transfers between devices: 10.1 us -> 14.8 us  [exchange(): lax.ppermute(block, axis, [(i, i ^ mask) for i in range(lax.axis_size(axi...]
    ppermute x6, waiting for transfers between devices: 9.42 us -> 5.77 us  [rotate(): lax.ppermute(block, axis, [(i, (i + distance) % n) for i in range(n)])]
    ppermute x17 -> x18, waiting for transfers between devices: 9.95 us -> 7.4 us  [exchange(): lax.ppermute(block, axis, [(i, i ^ mask) for i in range(lax.axis_size(axi...]
    ppermute x6, starting transfers between devices: 11.3 us -> 10 us  [rotate(): lax.ppermute(block, axis, [(i, (i + distance) % n) for i in range(n)])]
    pallas_call x1 -> x2, Pallas kernels: 1.12 us -> 2.02 us  [pick(): pl.pallas_call(kernel, out_shape=tuple(shapes), in_specs=[pl.BlockSpec(me...]
    pallas_call x1 -> x2, Pallas kernels: 1.3 us -> 2.11 us  [mix(): pl.pallas_call(kernel, out_shape=tuple(out_shape), in_specs=[whole] * len...]
  transfers between devices with their start and end apart: 23 -> 24, of which waited for: 14 -> 10; matrix products, arithmetic and copies ran while one was open for 0% -> 0% of each run, Pallas kernels for 5% -> 9%
where the time goes in v4:
time: 47.2 us; the launch traced here: 47 us
  starting transfers between devices  24.8 us (53%)
  waiting for transfers between devices  13.2 us (28%)
  Pallas kernels  8.87 us (19%)
    ppermute x18, starting transfers between devices, exchange(): lax.ppermute(block, axis, [(i, i ^ mask) for i in range(lax.axis_size(axi...  14.8 us
    ppermute x6, starting transfers between devices, rotate(): lax.ppermute(block, axis, [(i, (i + distance) % n) for i in range(n)])  10 us
    ppermute x18, waiting for transfers between devices, exchange(): lax.ppermute(block, axis, [(i, i ^ mask) for i in range(lax.axis_size(axi...  7.4 us
    ppermute x6, waiting for transfers between devices, rotate(): lax.ppermute(block, axis, [(i, (i + distance) % n) for i in range(n)])  5.77 us
    pallas_call x8, Pallas kernels, vmem_call(): pl.pallas_call(kernel, out_shape=tuple(outs), in_specs=[pl.BlockSpec(memo...  4.74 us
    pallas_call x2, Pallas kernels, mix(): pl.pallas_call(kernel, out_shape=tuple(out_shape), in_specs=[whole] * len...  2.11 us
    pallas_call x2, Pallas kernels, pick(): pl.pallas_call(kernel, out_shape=tuple(shapes), in_specs=[pl.BlockSpec(me...  2.02 us
  transfers between devices with their start and end apart: 24, of which 10 were waited for; matrix products, arithmetic and copies ran while one was open for 0% of the time, Pallas kernels for 9%

profile of v4, /device:TPU:0, one launch (start us, length us, event | category | flops | bytes accessed | tf_op | source)
XLA Modules:
  0.0 47.0 jit_solution(10538379240786717092)
XLA Ops:
  0.0 1.0 %shard_map.73.own_ref = bf16[384,128]{1,0:T(8,128)(2,1)S(1)} custom-call(bf16[4,384,128]{2,1,0:T(8,128)(2,1)} %records_ref.3), custom_call_target="tpu_custom_call" | custom-call | tf_op jit(solution)/shard_map/pallas_call | solution.py:131
  1.0 0.0 copy-done.6
  1.0 0.5 %collective-permute-start = (bf16[4,384,128]{2,1,0:T(8,128)(2,1)S(1)}, bf16[4,384,128]{2,1,0:T(8,128)(2,1)S(1)}, u32[]{:S(2)}, u32[]{:S(2)}) collective-permute-start(bf16[4,384,128]{2,1,0:T(8,128)(2,1)S(1)} %copy-done.6), channel_id=1, source_target_pairs={{0,1},{1,0},{2,3},{3,2},{4,5},{5,4},{6,7},{7,6},{8,9},{9,8},{10,11... | collective-permute-start | bytes 1179656 | tf_op jit(solution)/shard_map/ppermute | solution.py:92
  1.6 2.6 %collective-permute-start.1 = (bf16[384,128]{1,0:T(8,128)(2,1)S(1)}, bf16[384,128]{1,0:T(8,128)(2,1)S(1)}, u32[]{:S(2)}, u32[]{:S(2)}) collective-permute-start(bf16[384,128]{1,0:T(8,128)(2,1)S(1)} %shard_map.73.own_ref), channel_id=1, source_target_pairs={{0,2},{1,3},{2,0},{3,1},{4,6},{5,7},{6,4},{7,5},{8,10},{9,11},{10,... | collective-permute-start | bytes 294920 | tf_op jit(solution)/shard_map/ppermute | solution.py:92
  4.1 1.0 %shard_map.75 = (bf16[768,128]{1,0:T(8,128)(2,1)S(1)}, bf16[384,128]{1,0:T(8,128)(2,1)S(1)}) custom-call(bf16[4,384,128]{2,1,0:T(8,128)(2,1)} %records_ref.3), custom_call_target="tpu_custom_call" | custom-call | tf_op jit(solution)/shard_map/pallas_call | solution.py:131
  5.1 0.1 collective-permute-start.5
  5.2 2.3 %collective-permute-done.1.across_ref = bf16[384,128]{1,0:T(8,128)(2,1)S(1)} collective-permute-done((bf16[384,128]{1,0:T(8,128)(2,1)S(1)}, bf16[384,128]{1,0:T(8,128)(2,1)S(1)}, u32[]{:S(2)}, u32[]{:S(2)}) %collective-permute-start.1) | collective-permute-done | bytes 98336 | tf_op jit(solution)/shard_map/ppermute | solution.py:92
  7.5 0.0 copy-start.2
  7.5 0.1 collective-permute-start.2
  7.6 0.5 %collective-permute-start.3 = (bf16[192,128]{1,0:T(8,128)(2,1)S(1)}, bf16[192,128]{1,0:T(8,128)(2,1)S(1)}, u32[]{:S(2)}, u32[]{:S(2)}) collective-permute-start(bf16[192,128]{1,0:T(8,128)(2,1)S(1)} %get-tuple-element.65), channel_id=1, source_target_pairs={{0,1},{1,0},{2,3},{3,2},{4,5},{5,4},{6,7},{7,6},{8,9},{9,8},{10,11... | collective-permute-start | bytes 147464 | tf_op jit(solution)/shard_map/ppermute | solution.py:92
  8.1 0.7 %collective-permute-done.2.rest_0_ = bf16[192,128]{1,0:T(8,128)(2,1)S(1)} collective-permute-done((bf16[192,128]{1,0:T(8,128)(2,1)S(1)}, bf16[192,128]{1,0:T(8,128)(2,1)S(1)}, u32[]{:S(2)}, u32[]{:S(2)}) %collective-permute-start.2) | collective-permute-done | bytes 49184 | tf_op jit(solution)/shard_map/ppermute | solution.py:92
  8.8 0.2 collective-permute-done.3.rest_1_
  9.0 0.0 collective-permute-done.beside_ref
  9.0 0.0 copy-done
  9.0 0.0 copy-done.3
  9.0 0.0 copy-done.4
  9.0 0.0 copy-done.2
  9.0 0.6 %shard_map.74 = (bf16[416,128]{1,0:T(8,128)(2,1)S(1)}, f32[1,384,128]{2,1,0:T(8,128)S(1)}) custom-call(bf16[384,128]{1,0:T(8,128)(2,1)S(1)} %shard_map.73.own_ref, bf16[4,384,128]{2,1,0:T(8,128)(2,1)S(1)} %collective-permute-done.beside_ref, bf16[384,128]{1,0:T(8,128)(2,1)S(1)} %collective-permute-done.1.across_ref, f32[4,128]{1,0:T(4,128)S(1)} %bitcast.6, ...), custom_call_target="tpu_custom_call" | custom-call | tf_op jit(solution)/shard_map/pallas_call | solution.py:96
  9.6 2.9 %collective-permute-start.4 = (bf16[416,128]{1,0:T(8,128)(2,1)S(1)}, bf16[416,128]{1,0:T(8,128)(2,1)S(1)}, u32[]{:S(2)}, u32[]{:S(2)}) collective-permute-start(bf16[416,128]{1,0:T(8,128)(2,1)S(1)} %get-tuple-element.35), channel_id=1, source_target_pairs={{0,8},{4,12},{8,0},{12,4},{1,9},{5,13},{9,1},{13,5},{2,10},{6,14},... | collective-permute-start | bytes 319496 | tf_op jit(solution)/shard_map/ppermute | solution.py:88
  12.5 0.0 collective-permute-done.5.across_ref
  12.6 0.1 collective-permute-start.6
  12.7 0.4 collective-permute-start.7
  13.1 2.0 %collective-permute-start.10 = (bf16[384,128]{1,0:T(8,128)(2,1)S(1)}, bf16[384,128]{1,0:T(8,128)(2,1)S(1)}, u32[]{:S(2)}, u32[]{:S(2)}) collective-permute-start(bf16[384,128]{1,0:T(8,128)(2,1)S(1)} %get-tuple-element.40.own_ref), channel_id=1, source_target_pairs={{0,2},{1,3},{2,0},{3,1},{4,6},{5,7},{6,4},{7,5},{8,10},{9,11},{10,... | collective-permute-start | bytes 294920 | tf_op jit(solution)/shard_map/ppermute | solution.py:92
  15.1 0.0 collective-permute-done.6.rest_0_
  15.1 0.0 collective-permute-done.7.rest_1_
  15.1 0.9 %shard_map.76 = (bf16[416,128]{1,0:T(8,128)(2,1)S(1)}, bf16[416,128]{1,0:T(8,128)(2,1)S(1)}, f32[2,384,128]{2,1,0:T(8,128)S(1)}) custom-call(bf16[768,128]{1,0:T(8,128)(2,1)S(1)} %get-tuple-element.36.own_ref, bf16[4,384,128]{2,1,0:T(8,128)(2,1)S(1)} %collective-permute-done.beside_ref, bf16[768,128]{1,0:T(8,128)(2,1)S(1)} %collective-permute-done.5.across_ref, ...), custom_call_target="tpu_custom_call" | custom-call | tf_op jit(solution)/shard_map/pallas_call | solution.py:96
  16.0 1.6 %collective-permute-start.8 = (bf16[416,128]{1,0:T(8,128)(2,1)S(1)}, bf16[416,128]{1,0:T(8,128)(2,1)S(1)}, u32[]{:S(2)}, u32[]{:S(2)}) collective-permute-start(bf16[416,128]{1,0:T(8,128)(2,1)S(1)} %get-tuple-element.38), channel_id=1, source_target_pairs={{0,4},{4,8},{8,12},{12,0},{1,5},{5,9},{9,13},{13,1},{2,6},{6,10},{... | collective-permute-start | bytes 319496 | tf_op jit(solution)/shard_map/ppermute | solution.py:88
  17.6 2.3 %collective-permute-start.9 = (bf16[416,128]{1,0:T(8,128)(2,1)S(1)}, bf16[416,128]{1,0:T(8,128)(2,1)S(1)}, u32[]{:S(2)}, u32[]{:S(2)}) collective-permute-start(bf16[416,128]{1,0:T(8,128)(2,1)S(1)} %get-tuple-element.39), channel_id=1, source_target_pairs={{0,12},{4,0},{8,4},{12,8},{1,13},{5,1},{9,5},{13,9},{2,14},{6,2},{... | collective-permute-start | bytes 319496 | tf_op jit(solution)/shard_map/ppermute | solution.py:88
  19.9 0.0 collective-permute-done.10.across_ref
  19.9 0.0 collective-permute-start.11
  19.9 0.0 collective-permute-done.4.block_ref.refs_0_
  19.9 0.0 copy-done.5
  19.9 1.3 %collective-permute-done.11.rest_0_ = bf16[384,128]{1,0:T(8,128)(2,1)S(1)} collective-permute-done((bf16[384,128]{1,0:T(8,128)(2,1)S(1)}, bf16[384,128]{1,0:T(8,128)(2,1)S(1)}, u32[]{:S(2)}, u32[]{:S(2)}) %collective-permute-start.11) | collective-permute-done | bytes 98336 | tf_op jit(solution)/shard_map/ppermute | solution.py:92
  21.2 0.6 %shard_map.77 = (bf16[416,128]{1,0:T(8,128)(2,1)S(1)}, f32[1,384,128]{2,1,0:T(8,128)S(1)}) custom-call(bf16[384,128]{1,0:T(8,128)(2,1)S(1)} %get-tuple-element.40.own_ref, bf16[4,384,128]{2,1,0:T(8,128)(2,1)S(1)} %collective-permute-done.beside_ref, bf16[384,128]{1,0:T(8,128)(2,1)S(1)} %collective-permute-done.10.across_ref, f32[4,128]{1,0:T(4,128)S(1)} %bitcast.8, ...), custom_call_target="tpu_custom_call" | custom-call | tf_op jit(solution)/shard_map/pallas_call | solution.py:96
  21.8 1.9 %collective-permute-done.8.refs_1_ = bf16[416,128]{1,0:T(8,128)(2,1)S(1)} collective-permute-done((bf16[416,128]{1,0:T(8,128)(2,1)S(1)}, bf16[416,128]{1,0:T(8,128)(2,1)S(1)}, u32[]{:S(2)}, u32[]{:S(2)}) %collective-permute-start.8) | collective-permute-done | bytes 106528 | tf_op jit(solution)/shard_map/ppermute | solution.py:88
  23.7 0.6 %collective-permute-done.9.refs_2_ = bf16[416,128]{1,0:T(8,128)(2,1)S(1)} collective-permute-done((bf16[416,128]{1,0:T(8,128)(2,1)S(1)}, bf16[416,128]{1,0:T(8,128)(2,1)S(1)}, u32[]{:S(2)}, u32[]{:S(2)}) %collective-permute-start.9) | collective-permute-done | bytes 106528 | tf_op jit(solution)/shard_map/ppermute | solution.py:88
  24.3 2.5 %shard_map.79 = (bf16[400,128]{1,0:T(8,128)(2,1)S(1)}, bf16[400,128]{1,0:T(8,128)(2,1)S(1)}, bf16[400,128]{1,0:T(8,128)(2,1)S(1)}, bf16[400,128]{1,0:T(8,128)(2,1)S(1)}) custom-call(bf16[416,128]{1,0:T(8,128)(2,1)S(1)} %collective-permute-done.4.block_ref.refs_0_, bf16[416,128]{1,0:T(8,128)(2,1)S(1)} %collective-permute-done.8.refs_1_, ...), custom_call_target="tpu_custom_call" | custom-call | tf_op jit(solution)/shard_map/pallas_call | solution.py:96
  26.8 2.2 %collective-permute-start.14 = (bf16[400,128]{1,0:T(8,128)(2,1)S(1)}, bf16[400,128]{1,0:T(8,128)(2,1)S(1)}, u32[]{:S(2)}, u32[]{:S(2)}) collective-permute-start(bf16[400,128]{1,0:T(8,128)(2,1)S(1)} %get-tuple-element.51), channel_id=1, source_target_pairs={{0,12},{4,0},{8,4},{12,8},{1,13},{5,1},{9,5},{13,9},{2,14},{6,2},{... | collective-permute-start | bytes 307208 | tf_op jit(solution)/shard_map/ppermute | solution.py:88
  29.0 0.0 collective-permute-start.13
  29.0 1.0 %collective-permute-start.12 = (bf16[400,128]{1,0:T(8,128)(2,1)S(1)}, bf16[400,128]{1,0:T(8,128)(2,1)S(1)}, u32[]{:S(2)}, u32[]{:S(2)}) collective-permute-start(bf16[400,128]{1,0:T(8,128)(2,1)S(1)} %get-tuple-element.45), channel_id=1, source_target_pairs={{0,8},{4,12},{8,0},{12,4},{1,9},{5,13},{9,1},{13,5},{2,10},{6,14},... | collective-permute-start | bytes 307208 | tf_op jit(solution)/shard_map/ppermute | solution.py:88
  30.0 0.0 copy-done.1
  30.1 2.1 %collective-permute-start.15 = (bf16[640,128]{1,0:T(8,128)(2,1)S(1)}, bf16[640,128]{1,0:T(8,128)(2,1)S(1)}, u32[]{:S(2)}, u32[]{:S(2)}) collective-permute-start(bf16[640,128]{1,0:T(8,128)(2,1)S(1)} %get-tuple-element.49.refs_0_), channel_id=1, source_target_pairs={{0,2},{1,3},{2,0},{3,1},{4,6},{5,7},{6,4},{7,5},{8,10},{9,11},{10,... | collective-permute-start | bytes 491528 | tf_op jit(solution)/shard_map/ppermute | solution.py:92
  32.2 0.0 collective-permute-start.19
  32.2 0.2 collective-permute-done.14.refs_1_
  32.4 3.1 %collective-permute-done.13.refs_0_ = bf16[400,128]{1,0:T(8,128)(2,1)S(1)} collective-permute-done((bf16[400,128]{1,0:T(8,128)(2,1)S(1)}, bf16[400,128]{1,0:T(8,128)(2,1)S(1)}, u32[]{:S(2)}, u32[]{:S(2)}) %collective-permute-start.13) | collective-permute-done | bytes 102432 | tf_op jit(solution)/shard_map/ppermute | solution.py:88
  35.5 3.1 %collective-permute-start.22 = (bf16[768,128]{1,0:T(8,128)(2,1)S(1)}, bf16[768,128]{1,0:T(8,128)(2,1)S(1)}, u32[]{:S(2)}, u32[]{:S(2)}) collective-permute-start(bf16[768,128]{1,0:T(8,128)(2,1)S(1)} %shard_map.81.refs_4_), channel_id=1, source_target_pairs={{0,2},{1,3},{2,0},{3,1},{4,6},{5,7},{6,4},{7,5},{8,10},{9,11},{10,... | collective-permute-start | bytes 589832 | tf_op jit(solution)/shard_map/ppermute | solution.py:92
  38.6 0.0 collective-permute-start.21
  38.6 0.0 collective-permute-done.12.refs_0_
  38.7 0.0 collective-permute-done.15.refs_2_
  38.7 2.2 %collective-permute-start.17 = (bf16[384,128]{1,0:T(8,128)(2,1)S(1)}, bf16[384,128]{1,0:T(8,128)(2,1)S(1)}, u32[]{:S(2)}, u32[]{:S(2)}) collective-permute-start(bf16[384,128]{1,0:T(8,128)(2,1)S(1)} %shard_map.82.refs_0_), channel_id=1, source_target_pairs={{0,2},{1,3},{2,0},{3,1},{4,6},{5,7},{6,4},{7,5},{8,10},{9,11},{10,... | collective-permute-start | bytes 294920 | tf_op jit(solution)/shard_map/ppermute | solution.py:92
  40.9 2.0 %collective-permute-done.22.refs_6_ = bf16[768,128]{1,0:T(8,128)(2,1)S(1)} collective-permute-done((bf16[768,128]{1,0:T(8,128)(2,1)S(1)}, bf16[768,128]{1,0:T(8,128)(2,1)S(1)}, u32[]{:S(2)}, u32[]{:S(2)}) %collective-permute-start.22) | collective-permute-done | bytes 196640 | tf_op jit(solution)/shard_map/ppermute | solution.py:92
  42.9 0.0 collective-permute-start.23
  42.9 0.5 %collective-permute-start.20 = (bf16[640,128]{1,0:T(8,128)(2,1)S(1)}, bf16[640,128]{1,0:T(8,128)(2,1)S(1)}, u32[]{:S(2)}, u32[]{:S(2)}) collective-permute-start(bf16[640,128]{1,0:T(8,128)(2,1)S(1)} %collective-permute-done.15.refs_2_), channel_id=1, source_target_pairs={{0,1},{1,0},{2,3},{3,2},{4,5},{5,4},{6,7},{7,6},{8,9},{9,8},{10,11... | collective-permute-start | bytes 491528 | tf_op jit(solution)/shard_map/ppermute | solution.py:92
  43.4 1.0 %collective-permute-done.17.refs_2_ = bf16[384,128]{1,0:T(8,128)(2,1)S(1)} collective-permute-done((bf16[384,128]{1,0:T(8,128)(2,1)S(1)}, bf16[384,128]{1,0:T(8,128)(2,1)S(1)}, u32[]{:S(2)}, u32[]{:S(2)}) %collective-permute-start.17) | collective-permute-done | bytes 98336 | tf_op jit(solution)/shard_map/ppermute | solution.py:92
  44.4 0.0 collective-permute-start.16
  44.4 0.0 collective-permute-done.19.refs_1_
  44.4 0.5 %collective-permute-start.18 = (bf16[384,128]{1,0:T(8,128)(2,1)S(1)}, bf16[384,128]{1,0:T(8,128)(2,1)S(1)}, u32[]{:S(2)}, u32[]{:S(2)}) collective-permute-start(bf16[384,128]{1,0:T(8,128)(2,1)S(1)} %collective-permute-done.17.refs_2_), channel_id=1, source_target_pairs={{0,1},{1,0},{2,3},{3,2},{4,5},{5,4},{6,7},{7,6},{8,9},{9,8},{10,11... | collective-permute-start | bytes 294920 | tf_op jit(solution)/shard_map/ppermute | solution.py:92
  44.9 0.0 collective-permute-done.21.refs_5_
  44.9 0.0 collective-permute-done.20.refs_3_
  44.9 0.0 collective-permute-done.23.refs_7_
  44.9 1.2 %shard_map.83 = (bf16[4,384,128]{2,1,0:T(8,128)(2,1)}, bf16[512,128]{1,0:T(8,128)(2,1)S(1)}) custom-call(bf16[640,128]{1,0:T(8,128)(2,1)S(1)} %get-tuple-element.49.refs_0_, bf16[512,128]{1,0:T(8,128)(2,1)S(1)} %collective-permute-done.19.refs_1_, bf16[640,128]{1,0:T(8,128)(2,1)S(1)} %collective-permute-done.15.refs_2_, ...), custom_call_target="tpu_custom_call" | custom-call | tf_op jit(solution)/shard_map/pallas_call | solution.py:379
  46.1 0.0 collective-permute-done.16.refs_1_
  46.1 0.0 collective-permute-done.18.refs_3_
  46.1 0.9 %shard_map.84 = bf16[4,384,128]{2,1,0:T(8,128)(2,1)} custom-call(bf16[384,128]{1,0:T(8,128)(2,1)S(1)} %shard_map.82.refs_0_, bf16[384,128]{1,0:T(8,128)(2,1)S(1)} %collective-permute-done.16.refs_1_, bf16[384,128]{1,0:T(8,128)(2,1)S(1)} %collective-permute-done.17.refs_2_, ...), custom_call_target="tpu_custom_call", output_to_operand_aliasing={{}: (5, {})} | custom-call | tf_op jit(solution)/shard_map/pallas_call | solution.py:379
  (12 shorter events, 0.1 us)
Async XLA Ops:
  0.0 1.0 %copy-start.6 = (bf16[4,384,128]{2,1,0:T(8,128)(2,1)S(1)}, bf16[4,384,128]{2,1,0:T(8,128)(2,1)}, u32[]{:S(2)}) copy-start(bf16[4,384,128]{2,1,0:T(8,128)(2,1)} %records_ref.3) | copy-start | bytes 1179652
  1.0 8.0 %copy-start = (bf16[512,3,128]{2,0,1:T(8,128)(2,1)S(1)}, bf16[512,3,128]{2,0,1:T(8,128)(2,1)}, u32[]{:S(2)}) copy-start(bf16[512,3,128]{2,0,1:T(8,128)(2,1)} %param.9) | copy-start | bytes 1179652
  1.0 7.9 %collective-permute-start = (bf16[4,384,128]{2,1,0:T(8,128)(2,1)S(1)}, bf16[4,384,128]{2,1,0:T(8,128)(2,1)S(1)}, u32[]{:S(2)}, u32[]{:S(2)}) collective-permute-start(bf16[4,384,128]{2,1,0:T(8,128)(2,1)S(1)} %copy-done.6), channel_id=1, source_target_pairs={{0,1},{1,0},{2,3},{3,2},{4,5},{5,4},{6,7},{7,6},{8,9},{9,8},{10,11... | collective-permute-start | bytes 1179656 | tf_op jit(solution)/shard_map/ppermute | solution.py:92
  1.6 6.0 %collective-permute-start.1 = (bf16[384,128]{1,0:T(8,128)(2,1)S(1)}, bf16[384,128]{1,0:T(8,128)(2,1)S(1)}, u32[]{:S(2)}, u32[]{:S(2)}) collective-permute-start(bf16[384,128]{1,0:T(8,128)(2,1)S(1)} %shard_map.73.own_ref), channel_id=1, source_target_pairs={{0,2},{1,3},{2,0},{3,1},{4,6},{5,7},{6,4},{7,5},{8,10},{9,11},{10,... | collective-permute-start | bytes 294920 | tf_op jit(solution)/shard_map/ppermute | solution.py:92
  5.1 7.4 %collective-permute-start.5 = (bf16[768,128]{1,0:T(8,128)(2,1)S(1)}, bf16[768,128]{1,0:T(8,128)(2,1)S(1)}, u32[]{:S(2)}, u32[]{:S(2)}) collective-permute-start(bf16[768,128]{1,0:T(8,128)(2,1)S(1)} %get-tuple-element.36.own_ref), channel_id=1, source_target_pairs={{0,2},{1,3},{2,0},{3,1},{4,6},{5,7},{6,4},{7,5},{8,10},{9,11},{10,... | collective-permute-start | bytes 589832 | tf_op jit(solution)/shard_map/ppermute | solution.py:92
  7.5 1.5 %copy-start.3 = (bf16[4,384]{1,0:T(4,128)(2,1)S(1)}, bf16[4,384]{1,0:T(4,128)(2,1)}, u32[]{:S(2)}) copy-start(bf16[4,384]{1,0:T(4,128)(2,1)} %taps_ref.5) | copy-start | bytes 9220
  7.5 1.5 %copy-start.4 = (f32[512]{0:T(512)S(1)}, f32[512]{0:T(512)}, u32[]{:S(2)}) copy-start(f32[512]{0:T(512)} %param.8) | copy-start | bytes 6148
  7.5 1.5 %copy-start.2 = (f32[3,3,128]{2,1,0:T(4,128)S(1)}, f32[3,3,128]{2,1,0:T(4,128)}, u32[]{:S(2)}) copy-start(f32[3,3,128]{2,1,0:T(4,128)} %refs_2_.3) | copy-start | bytes 13828
  7.5 1.3 %collective-permute-start.2 = (bf16[192,128]{1,0:T(8,128)(2,1)S(1)}, bf16[192,128]{1,0:T(8,128)(2,1)S(1)}, u32[]{:S(2)}, u32[]{:S(2)}) collective-permute-start(bf16[192,128]{1,0:T(8,128)(2,1)S(1)} %get-tuple-element.66), channel_id=1, source_target_pairs={{0,1},{1,0},{2,3},{3,2},{4,5},{5,4},{6,7},{7,6},{8,9},{9,8},{10,11... | collective-permute-start | bytes 147464 | tf_op jit(solution)/shard_map/ppermute | solution.py:92
  7.6 1.4 %collective-permute-start.3 = (bf16[192,128]{1,0:T(8,128)(2,1)S(1)}, bf16[192,128]{1,0:T(8,128)(2,1)S(1)}, u32[]{:S(2)}, u32[]{:S(2)}) collective-permute-start(bf16[192,128]{1,0:T(8,128)(2,1)S(1)} %get-tuple-element.65), channel_id=1, source_target_pairs={{0,1},{1,0},{2,3},{3,2},{4,5},{5,4},{6,7},{7,6},{8,9},{9,8},{10,11... | collective-permute-start | bytes 147464 | tf_op jit(solution)/shard_map/ppermute | solution.py:92
  9.6 10.3 %collective-permute-start.4 = (bf16[416,128]{1,0:T(8,128)(2,1)S(1)}, bf16[416,128]{1,0:T(8,128)(2,1)S(1)}, u32[]{:S(2)}, u32[]{:S(2)}) collective-permute-start(bf16[416,128]{1,0:T(8,128)(2,1)S(1)} %get-tuple-element.35), channel_id=1, source_target_pairs={{0,8},{4,12},{8,0},{12,4},{1,9},{5,13},{9,1},{13,5},{2,10},{6,14},... | collective-permute-start | bytes 319496 | tf_op jit(solution)/shard_map/ppermute | solution.py:88
  12.6 2.5 %collective-permute-start.6 = (bf16[384,128]{1,0:T(8,128)(2,1)S(1)}, bf16[384,128]{1,0:T(8,128)(2,1)S(1)}, u32[]{:S(2)}, u32[]{:S(2)}) collective-permute-start(bf16[384,128]{1,0:T(8,128)(2,1)S(1)} %get-tuple-element.64), channel_id=1, source_target_pairs={{0,1},{1,0},{2,3},{3,2},{4,5},{5,4},{6,7},{7,6},{8,9},{9,8},{10,11... | collective-permute-start | bytes 294920 | tf_op jit(solution)/shard_map/ppermute | solution.py:92
  12.7 2.4 %collective-permute-start.7 = (bf16[384,128]{1,0:T(8,128)(2,1)S(1)}, bf16[384,128]{1,0:T(8,128)(2,1)S(1)}, u32[]{:S(2)}, u32[]{:S(2)}) collective-permute-start(bf16[384,128]{1,0:T(8,128)(2,1)S(1)} %get-tuple-element.63), channel_id=1, source_target_pairs={{0,1},{1,0},{2,3},{3,2},{4,5},{5,4},{6,7},{7,6},{8,9},{9,8},{10,11... | collective-permute-start | bytes 294920 | tf_op jit(solution)/shard_map/ppermute | solution.py:92
  13.1 6.7 %collective-permute-start.10 = (bf16[384,128]{1,0:T(8,128)(2,1)S(1)}, bf16[384,128]{1,0:T(8,128)(2,1)S(1)}, u32[]{:S(2)}, u32[]{:S(2)}) collective-permute-start(bf16[384,128]{1,0:T(8,128)(2,1)S(1)} %get-tuple-element.40.own_ref), channel_id=1, source_target_pairs={{0,2},{1,3},{2,0},{3,1},{4,6},{5,7},{6,4},{7,5},{8,10},{9,11},{10,... | collective-permute-start | bytes 294920 | tf_op jit(solution)/shard_map/ppermute | solution.py:92
  16.0 7.7 %collective-permute-start.8 = (bf16[416,128]{1,0:T(8,128)(2,1)S(1)}, bf16[416,128]{1,0:T(8,128)(2,1)S(1)}, u32[]{:S(2)}, u32[]{:S(2)}) collective-permute-start(bf16[416,128]{1,0:T(8,128)(2,1)S(1)} %get-tuple-element.38), channel_id=1, source_target_pairs={{0,4},{4,8},{8,12},{12,0},{1,5},{5,9},{9,13},{13,1},{2,6},{6,10},{... | collective-permute-start | bytes 319496 | tf_op jit(solution)/shard_map/ppermute | solution.py:88
  17.6 2.3 %copy-start.5 = (f32[128]{0:T(128)S(1)}, f32[128]{0:T(128)}, u32[]{:S(2)}) copy-start(f32[128]{0:T(128)} %param.12) | copy-start | bytes 1540
  17.6 6.7 %collective-permute-start.9 = (bf16[416,128]{1,0:T(8,128)(2,1)S(1)}, bf16[416,128]{1,0:T(8,128)(2,1)S(1)}, u32[]{:S(2)}, u32[]{:S(2)}) collective-permute-start(bf16[416,128]{1,0:T(8,128)(2,1)S(1)} %get-tuple-element.39), channel_id=1, source_target_pairs={{0,12},{4,0},{8,4},{12,8},{1,13},{5,1},{9,5},{13,9},{2,14},{6,2},{... | collective-permute-start | bytes 319496 | tf_op jit(solution)/shard_map/ppermute | solution.py:88
  19.9 1.3 %collective-permute-start.11 = (bf16[384,128]{1,0:T(8,128)(2,1)S(1)}, bf16[384,128]{1,0:T(8,128)(2,1)S(1)}, u32[]{:S(2)}, u32[]{:S(2)}) collective-permute-start(bf16[384,128]{1,0:T(8,128)(2,1)S(1)} %collective-permute-done.10.across_ref), channel_id=1, source_target_pairs={{0,1},{1,0},{2,3},{3,2},{4,5},{5,4},{6,7},{7,6},{8,9},{9,8},{10,11... | collective-permute-start | bytes 294920 | tf_op jit(solution)/shard_map/ppermute | solution.py:92
  24.3 5.7 %copy-start.1 = (bf16[128,512]{1,0:T(8,128)(2,1)S(1)}, bf16[128,512]{1,0:T(8,128)(2,1)}, u32[]{:S(2)}) copy-start(bf16[128,512]{1,0:T(8,128)(2,1)} %refs_8_.1) | copy-start | bytes 393220
  26.8 5.5 %collective-permute-start.14 = (bf16[400,128]{1,0:T(8,128)(2,1)S(1)}, bf16[400,128]{1,0:T(8,128)(2,1)S(1)}, u32[]{:S(2)}, u32[]{:S(2)}) collective-permute-start(bf16[400,128]{1,0:T(8,128)(2,1)S(1)} %get-tuple-element.51), channel_id=1, source_target_pairs={{0,12},{4,0},{8,4},{12,8},{1,13},{5,1},{9,5},{13,9},{2,14},{6,2},{... | collective-permute-start | bytes 307208 | tf_op jit(solution)/shard_map/ppermute | solution.py:88
  29.0 6.5 %collective-permute-start.13 = (bf16[400,128]{1,0:T(8,128)(2,1)S(1)}, bf16[400,128]{1,0:T(8,128)(2,1)S(1)}, u32[]{:S(2)}, u32[]{:S(2)}) collective-permute-start(bf16[400,128]{1,0:T(8,128)(2,1)S(1)} %get-tuple-element.46), channel_id=1, source_target_pairs={{0,4},{4,8},{8,12},{12,0},{1,5},{5,9},{9,13},{13,1},{2,6},{6,10},{... | collective-permute-start | bytes 307208 | tf_op jit(solution)/shard_map/ppermute | solution.py:88
  29.0 9.6 %collective-permute-start.12 = (bf16[400,128]{1,0:T(8,128)(2,1)S(1)}, bf16[400,128]{1,0:T(8,128)(2,1)S(1)}, u32[]{:S(2)}, u32[]{:S(2)}) collective-permute-start(bf16[400,128]{1,0:T(8,128)(2,1)S(1)} %get-tuple-element.45), channel_id=1, source_target_pairs={{0,8},{4,12},{8,0},{12,4},{1,9},{5,13},{9,1},{13,5},{2,10},{6,14},... | collective-permute-start | bytes 307208 | tf_op jit(solution)/shard_map/ppermute | solution.py:88
  30.1 8.6 %collective-permute-start.15 = (bf16[640,128]{1,0:T(8,128)(2,1)S(1)}, bf16[640,128]{1,0:T(8,128)(2,1)S(1)}, u32[]{:S(2)}, u32[]{:S(2)}) collective-permute-start(bf16[640,128]{1,0:T(8,128)(2,1)S(1)} %get-tuple-element.49.refs_0_), channel_id=1, source_target_pairs={{0,2},{1,3},{2,0},{3,1},{4,6},{5,7},{6,4},{7,5},{8,10},{9,11},{10,... | collective-permute-start | bytes 491528 | tf_op jit(solution)/shard_map/ppermute | solution.py:92
  32.2 12.2 %collective-permute-start.19 = (bf16[512,128]{1,0:T(8,128)(2,1)S(1)}, bf16[512,128]{1,0:T(8,128)(2,1)S(1)}, u32[]{:S(2)}, u32[]{:S(2)}) collective-permute-start(bf16[512,128]{1,0:T(8,128)(2,1)S(1)} %get-tuple-element.58), channel_id=1, source_target_pairs={{0,1},{1,0},{2,3},{3,2},{4,5},{5,4},{6,7},{7,6},{8,9},{9,8},{10,11... | collective-permute-start | bytes 393224 | tf_op jit(solution)/shard_map/ppermute | solution.py:92
  35.5 7.3 %collective-permute-start.22 = (bf16[768,128]{1,0:T(8,128)(2,1)S(1)}, bf16[768,128]{1,0:T(8,128)(2,1)S(1)}, u32[]{:S(2)}, u32[]{:S(2)}) collective-permute-start(bf16[768,128]{1,0:T(8,128)(2,1)S(1)} %shard_map.81.refs_4_), channel_id=1, source_target_pairs={{0,2},{1,3},{2,0},{3,1},{4,6},{5,7},{6,4},{7,5},{8,10},{9,11},{10,... | collective-permute-start | bytes 589832 | tf_op jit(solution)/shard_map/ppermute | solution.py:92
  38.6 6.3 %collective-permute-start.21 = (bf16[768,128]{1,0:T(8,128)(2,1)S(1)}, bf16[768,128]{1,0:T(8,128)(2,1)S(1)}, u32[]{:S(2)}, u32[]{:S(2)}) collective-permute-start(bf16[768,128]{1,0:T(8,128)(2,1)S(1)} %shard_map.81.refs_4_), channel_id=1, source_target_pairs={{0,1},{1,0},{2,3},{3,2},{4,5},{5,4},{6,7},{7,6},{8,9},{9,8},{10,11... | collective-permute-start | bytes 589832 | tf_op jit(solution)/shard_map/ppermute | solution.py:92
  38.7 5.7 %collective-permute-start.17 = (bf16[384,128]{1,0:T(8,128)(2,1)S(1)}, bf16[384,128]{1,0:T(8,128)(2,1)S(1)}, u32[]{:S(2)}, u32[]{:S(2)}) collective-permute-start(bf16[384,128]{1,0:T(8,128)(2,1)S(1)} %shard_map.82.refs_0_), channel_id=1, source_target_pairs={{0,2},{1,3},{2,0},{3,1},{4,6},{5,7},{6,4},{7,5},{8,10},{9,11},{10,... | collective-permute-start | bytes 294920 | tf_op jit(solution)/shard_map/ppermute | solution.py:92
  42.9 2.0 %collective-permute-start.23 = (bf16[768,128]{1,0:T(8,128)(2,1)S(1)}, bf16[768,128]{1,0:T(8,128)(2,1)S(1)}, u32[]{:S(2)}, u32[]{:S(2)}) collective-permute-start(bf16[768,128]{1,0:T(8,128)(2,1)S(1)} %collective-permute-done.22.refs_6_), channel_id=1, source_target_pairs={{0,1},{1,0},{2,3},{3,2},{4,5},{5,4},{6,7},{7,6},{8,9},{9,8},{10,11... | collective-permute-start | bytes 589832 | tf_op jit(solution)/shard_map/ppermute | solution.py:92
  42.9 2.0 %collective-permute-start.20 = (bf16[640,128]{1,0:T(8,128)(2,1)S(1)}, bf16[640,128]{1,0:T(8,128)(2,1)S(1)}, u32[]{:S(2)}, u32[]{:S(2)}) collective-permute-start(bf16[640,128]{1,0:T(8,128)(2,1)S(1)} %collective-permute-done.15.refs_2_), channel_id=1, source_target_pairs={{0,1},{1,0},{2,3},{3,2},{4,5},{5,4},{6,7},{7,6},{8,9},{9,8},{10,11... | collective-permute-start | bytes 491528 | tf_op jit(solution)/shard_map/ppermute | solution.py:92
  44.4 1.7 %collective-permute-start.16 = (bf16[384,128]{1,0:T(8,128)(2,1)S(1)}, bf16[384,128]{1,0:T(8,128)(2,1)S(1)}, u32[]{:S(2)}, u32[]{:S(2)}) collective-permute-start(bf16[384,128]{1,0:T(8,128)(2,1)S(1)} %shard_map.82.refs_0_), channel_id=1, source_target_pairs={{0,1},{1,0},{2,3},{3,2},{4,5},{5,4},{6,7},{7,6},{8,9},{9,8},{10,11... | collective-permute-start | bytes 294920 | tf_op jit(solution)/shard_map/ppermute | solution.py:92
  44.4 1.7 %collective-permute-start.18 = (bf16[384,128]{1,0:T(8,128)(2,1)S(1)}, bf16[384,128]{1,0:T(8,128)(2,1)S(1)}, u32[]{:S(2)}, u32[]{:S(2)}) collective-permute-start(bf16[384,128]{1,0:T(8,128)(2,1)S(1)} %collective-permute-done.17.refs_2_), channel_id=1, source_target_pairs={{0,1},{1,0},{2,3},{3,2},{4,5},{5,4},{6,7},{7,6},{8,9},{9,8},{10,11... | collective-permute-start | bytes 294920 | tf_op jit(solution)/shard_map/ppermute | solution.py:92

commit v5 on v4

--- a/solution.py
+++ b/solution.py
@@ -9,6 +9,7 @@
 EXTRA = 32
 NO_COST = pl.CostEstimate(flops=0, bytes_accessed=0, transcendentals=0)
 EARLY_COST, FAR_COST = 1 << 30, 1 << 33
+GRANT = 40 * 1024 * 1024
 BACK = 16
 VMEM = pltpu.VMEM
 
@@ -99,7 +100,7 @@
         in_specs=[pl.BlockSpec(memory_space=VMEM)] * len(operands),
         out_specs=tuple(pl.BlockSpec(memory_space=VMEM) for _ in outs),
         scratch_shapes=scratch,
-        compiler_params=pltpu.CompilerParams(vmem_limit_bytes=40 * 1024 * 1024),
+        compiler_params=pltpu.CompilerParams(vmem_limit_bytes=GRANT),
         cost_estimate=pl.CostEstimate(flops=cost, bytes_accessed=0, transcendentals=0),
     )(*operands)
 
@@ -338,57 +339,63 @@
     return vmem_call(kernel, outs, [], *sums, *arrays, short_kernel, *extra, cost=cost)
 
 
-def mix(slabs, out_projection, distances, shape, mixed=None):
+def mix_early(slabs, out_projection, block_len):
     f32, bf16 = jnp.float32, jnp.bfloat16
-    count, block_len, _ = shape
     groups = len(slabs)
-    records = sum(len(d) for d in distances)
-    first = mixed is None
+    counts = [slab[0].shape[0] // block_len for slab in slabs]
+    counts[0] = 1
 
     def kernel(*refs):
-        slab_refs, w_ref, rest = refs[: 4 * groups], refs[4 * groups], refs[4 * groups + 1 :]
-        if first:
-            out_ref, w_all, results, sems = rest
-            me = lax.axis_index("chan")
-            start = len(distances[0]) * block_len
-            w_all[0:LANES, :] = w_ref[:, pl.ds(pl.multiple_of(me * LANES, LANES), LANES)]
-            w_all[LANES : 2 * LANES, :] = slab_refs[1][start : start + LANES, :]
-            w_all[2 * LANES : 3 * LANES, :] = slab_refs[2][start : start + LANES, :]
-            w_all[3 * LANES :, :] = slab_refs[3][start + LANES : start + 2 * LANES, :]
-        else:
-            w_all, (_, out_ref, results, sems) = w_ref, rest
+        slab_refs, (w_ref, out_ref, w_all) = refs[: 4 * groups], refs[4 * groups :]
+        me = lax.axis_index("chan")
+        w_all[0:LANES, :] = w_ref[:, pl.ds(pl.multiple_of(me * LANES, LANES), LANES)]
+        w_all[LANES : 2 * LANES, :] = slab_refs[1][block_len : block_len + LANES, :]
+        w_all[2 * LANES : 3 * LANES, :] = slab_refs[2][block_len : block_len + LANES, :]
+        w_all[3 * LANES :, :] = slab_refs[3][block_len + LANES : block_len + 2 * LANES, :]
+        n = 0
+        for g in range(groups):
+            for i in range(counts[g]):
+                rows = slice(i * block_len, (i + 1) * block_len)
+                lhs = jnp.concatenate([ref[rows, :] for ref in slab_refs[4 * g : 4 * g + 4]], axis=1)
+                out_ref[n] = jnp.dot(lhs, w_all[...], preferred_element_type=f32).astype(bf16)
+                n += 1
+
+    operands = [x for slab in slabs for x in slab] + [out_projection]
+    outs = [VMEM((sum(counts), block_len, LANES), bf16), VMEM((4 * LANES, LANES), bf16)]
+    return vmem_call(kernel, outs, [], *operands)
+
+
+def mix_last(slab, columns, early, places, count):
+    block_len = slab[0].shape[0]
+
+    def kernel(*refs):
+        slab_refs, (w_ref, early_ref, out_ref, last, sems) = refs[:4], refs[4:]
         z = lax.axis_index("seq")
         copies = []
-        for g in range(groups):
-            for i, k in enumerate(distances[g]):
-                rows = slice(i * block_len, (i + 1) * block_len)
-                lhs = jnp.concatenate([ref[rows, :] for ref in slab_refs[4 * g : 4 * g + 4]], axis=1)
-                n = len(copies)
-                results[n] = jnp.dot(lhs, w_all[...], preferred_element_type=f32).astype(bf16)
-                copies.append(pltpu.make_async_copy(results.at[n], out_ref.at[lax.rem(z + k, count)], sems.at[n]))
-                copies[n].start()
+        for i, k in enumerate(places):
+            source = early_ref.at[i] if i < count - 1 else last
+            copies.append(pltpu.make_async_copy(source, out_ref.at[lax.rem(z + k, count)], sems.at[i]))
+        for copy in copies[:-1]:
+            copy.start()
+        lhs = jnp.concatenate([ref[...] for ref in slab_refs], axis=1)
+        last[...] = jnp.dot(lhs, w_ref[...], preferred_element_type=jnp.float32).astype(jnp.bfloat16)
+        copies[-1].start()
         for copy in copies:
             copy.wait()
 
-    whole, anywhere = pl.BlockSpec(memory_space=VMEM), pl.BlockSpec(memory_space=pl.ANY)
-    operands = [x for slab in slabs for x in slab] + [out_projection]
-    out_shape, out_specs = [jax.ShapeDtypeStruct(shape, bf16)], [anywhere]
-    if first:
-        out_shape.append(VMEM((4 * LANES, LANES), bf16))
-        out_specs.append(whole)
     return pl.pallas_call(
         kernel,
-        out_shape=tuple(out_shape),
-        in_specs=[whole] * len(operands) + ([] if first else [anywhere]),
-        out_specs=tuple(out_specs),
-        input_output_aliases={} if first else {len(operands): 0},
-        scratch_shapes=[pltpu.VMEM((records, block_len, LANES), bf16), pltpu.SemaphoreType.DMA((records,))],
-        compiler_params=pltpu.CompilerParams(vmem_limit_bytes=40 * 1024 * 1024),
+        out_shape=jax.ShapeDtypeStruct((count, block_len, LANES), jnp.bfloat16),
+        in_specs=[pl.BlockSpec(memory_space=VMEM)] * 6,
+        out_specs=pl.BlockSpec(memory_space=pl.ANY),
+        scratch_shapes=[pltpu.VMEM((block_len, LANES), jnp.bfloat16), pltpu.SemaphoreType.DMA((count,))],
+        compiler_params=pltpu.CompilerParams(vmem_limit_bytes=GRANT),
         cost_estimate=NO_COST,
-    )(*operands, *([] if first else [mixed]))
+    )(*slab, columns, early)
 
 
 def exchange_body(records, norm_gain, in_projection, short_kernel, long_filter, skip_gain, out_projection):
+    block_len = records.shape[1]
     weights = jnp.transpose(in_projection, (1, 0, 2))
     gain = norm_gain.reshape(4, LANES)
     skip = skip_gain.reshape(1, LANES)
@@ -403,7 +410,7 @@
         diagonal = [exchange(far[i * size : (i + 1) * size], "chan", 1) for i in range(pieces)]
         return project(own, beside, far, diagonal, gain, weights, short_kernel, long_filter, offsets)
 
-    (to_two,), query_two = projected((2,), first, across_first, 2)
+    (to_two,), query_two = projected((2,), first, across_first, 1)
     from_two = rotate(to_two, "seq", 2)
     (to_one, to_three), query_near = projected((1, 3), second, after(across_second, to_two), 2)
     from_one = rotate(to_one, "seq", 1)
@@ -429,9 +436,9 @@
     def slab(gated, beside, over):
         return (gated, exchange(beside, "chan", 1), over, exchange(after(over, far), "chan", 1))
 
-    early = [slab(own, own_beside, own_over), slab(near, near, near_over)]
-    mixed, columns = mix(early, out_projection, ((0,), (3, 1)), records.shape)
-    return mix([slab(far, far, far_over)], columns, ((2,),), records.shape, mixed)[0]
+    early_slabs = [slab(own, own_beside, own_over), slab(near, near, near_over)]
+    early, columns = mix_early(early_slabs, out_projection, block_len)
+    return mix_last(slab(far, far, far_over), columns, early, (0, 3, 1, 2), records.shape[0])
 
 
 def solution(mesh):

time: 47.2 us -> 46.5 us (0.985)
  waiting for transfers between devices: 13.2 us -> 14.4 us
  starting transfers between devices: 24.8 us -> 23.6 us
  Pallas kernels: 8.87 us -> 8.18 us
    pallas_call x2 -> x1, Pallas kernels: 2.11 us -> 0.93 us  [mix_last(): pl.pallas_call(kernel, out_shape=jax.ShapeDtypeStruct((count, block_len,...]
    ppermute x18 -> x17, starting transfers between devices: 14.8 us -> 13.6 us  [exchange(): lax.ppermute(block, axis, [(i, i ^ mask) for i in range(lax.axis_size(axi...]
    ppermute x18 -> x17, waiting for transfers between devices: 7.4 us -> 8.21 us  [exchange(): lax.ppermute(block, axis, [(i, i ^ mask) for i in range(lax.axis_size(axi...]
    pallas_call x8 -> x9, Pallas kernels: 4.74 us -> 5.22 us  [vmem_call(): pl.pallas_call(kernel, out_shape=tuple(outs), in_specs=[pl.BlockSpec(memo...]
  transfers between devices with their start and end apart: 24 -> 23, of which waited for: 10 -> 12; matrix products, arithmetic and copies ran while one was open for 0% -> 0% of each run, Pallas kernels for 9% -> 8%
where the time goes in v5:
time: 46.5 us; the launch traced here: 46.4 us
  starting transfers between devices  23.6 us (51%)
  waiting for transfers between devices  14.4 us (31%)
  Pallas kernels  8.18 us (18%)
    ppermute x17, starting transfers between devices, exchange(): lax.ppermute(block, axis, [(i, i ^ mask) for i in range(lax.axis_size(axi...  13.6 us
    ppermute x6, starting transfers between devices, rotate(): lax.ppermute(block, axis, [(i, (i + distance) % n) for i in range(n)])  10 us
    ppermute x17, waiting for transfers between devices, exchange(): lax.ppermute(block, axis, [(i, i ^ mask) for i in range(lax.axis_size(axi...  8.21 us
    ppermute x6, waiting for transfers between devices, rotate(): lax.ppermute(block, axis, [(i, (i + distance) % n) for i in range(n)])  6.16 us
    pallas_call x9, Pallas kernels, vmem_call(): pl.pallas_call(kernel, out_shape=tuple(outs), in_specs=[pl.BlockSpec(memo...  5.22 us
    pallas_call x2, Pallas kernels, pick(): pl.pallas_call(kernel, out_shape=tuple(shapes), in_specs=[pl.BlockSpec(me...  2.04 us
    pallas_call x1, Pallas kernels, mix_last(): pl.pallas_call(kernel, out_shape=jax.ShapeDtypeStruct((count, block_len,...  0.93 us
  transfers between devices with their start and end apart: 23, of which 12 were waited for; matrix products, arithmetic and copies ran while one was open for 0% of the time, Pallas kernels for 8%

profile of v5, /device:TPU:0, one launch (start us, length us, event | category | flops | bytes accessed | tf_op | source)
XLA Modules:
  0.0 46.4 jit_solution(155141378892765324)
XLA Ops:
  0.0 0.0 copy-start.6
  0.0 1.0 %shard_map.73.own_ref = bf16[384,128]{1,0:T(8,128)(2,1)S(1)} custom-call(bf16[4,384,128]{2,1,0:T(8,128)(2,1)} %records_ref.3), custom_call_target="tpu_custom_call" | custom-call | tf_op jit(solution)/shard_map/pallas_call | solution.py:132
  1.0 0.0 copy-done.6
  1.0 0.5 %collective-permute-start = (bf16[4,384,128]{2,1,0:T(8,128)(2,1)S(1)}, bf16[4,384,128]{2,1,0:T(8,128)(2,1)S(1)}, u32[]{:S(2)}, u32[]{:S(2)}) collective-permute-start(bf16[4,384,128]{2,1,0:T(8,128)(2,1)S(1)} %copy-done.6), channel_id=1, source_target_pairs={{0,1},{1,0},{2,3},{3,2},{4,5},{5,4},{6,7},{7,6},{8,9},{9,8},{10,11... | collective-permute-start | bytes 1179656 | tf_op jit(solution)/shard_map/ppermute | solution.py:93
  1.5 2.6 %collective-permute-start.1 = (bf16[384,128]{1,0:T(8,128)(2,1)S(1)}, bf16[384,128]{1,0:T(8,128)(2,1)S(1)}, u32[]{:S(2)}, u32[]{:S(2)}) collective-permute-start(bf16[384,128]{1,0:T(8,128)(2,1)S(1)} %shard_map.73.own_ref), channel_id=1, source_target_pairs={{0,2},{1,3},{2,0},{3,1},{4,6},{5,7},{6,4},{7,5},{8,10},{9,11},{10,... | collective-permute-start | bytes 294920 | tf_op jit(solution)/shard_map/ppermute | solution.py:93
  4.1 1.0 %shard_map.75 = (bf16[768,128]{1,0:T(8,128)(2,1)S(1)}, bf16[384,128]{1,0:T(8,128)(2,1)S(1)}) custom-call(bf16[4,384,128]{2,1,0:T(8,128)(2,1)} %records_ref.3), custom_call_target="tpu_custom_call" | custom-call | tf_op jit(solution)/shard_map/pallas_call | solution.py:132
  5.2 0.0 copy-start.3
  5.2 0.0 copy-start.4
  5.2 0.1 collective-permute-start.4
  5.3 2.2 %collective-permute-done.1.across_ref = bf16[384,128]{1,0:T(8,128)(2,1)S(1)} collective-permute-done((bf16[384,128]{1,0:T(8,128)(2,1)S(1)}, bf16[384,128]{1,0:T(8,128)(2,1)S(1)}, u32[]{:S(2)}, u32[]{:S(2)}) %collective-permute-start.1) | collective-permute-done | bytes 98336 | tf_op jit(solution)/shard_map/ppermute | solution.py:93
  7.5 0.0 collective-permute-start.2
  7.5 1.3 %collective-permute-done.2.rest_0_ = bf16[384,128]{1,0:T(8,128)(2,1)S(1)} collective-permute-done((bf16[384,128]{1,0:T(8,128)(2,1)S(1)}, bf16[384,128]{1,0:T(8,128)(2,1)S(1)}, u32[]{:S(2)}, u32[]{:S(2)}) %collective-permute-start.2) | collective-permute-done | bytes 98336 | tf_op jit(solution)/shard_map/ppermute | solution.py:93
  8.8 0.0 collective-permute-done.beside_ref
  8.8 0.0 copy-done
  8.8 0.0 copy-done.2
  8.8 0.0 copy-done.3
  8.8 0.0 copy-done.4
  8.8 0.6 %shard_map.74 = (bf16[416,128]{1,0:T(8,128)(2,1)S(1)}, f32[1,384,128]{2,1,0:T(8,128)S(1)}) custom-call(bf16[384,128]{1,0:T(8,128)(2,1)S(1)} %shard_map.73.own_ref, bf16[4,384,128]{2,1,0:T(8,128)(2,1)S(1)} %collective-permute-done.beside_ref, bf16[384,128]{1,0:T(8,128)(2,1)S(1)} %collective-permute-done.1.across_ref, f32[4,128]{1,0:T(4,128)S(1)} %bitcast.6, ...), custom_call_target="tpu_custom_call" | custom-call | tf_op jit(solution)/shard_map/pallas_call | solution.py:97
  9.4 2.9 %collective-permute-start.3 = (bf16[416,128]{1,0:T(8,128)(2,1)S(1)}, bf16[416,128]{1,0:T(8,128)(2,1)S(1)}, u32[]{:S(2)}, u32[]{:S(2)}) collective-permute-start(bf16[416,128]{1,0:T(8,128)(2,1)S(1)} %get-tuple-element.35), channel_id=1, source_target_pairs={{0,8},{4,12},{8,0},{12,4},{1,9},{5,13},{9,1},{13,5},{2,10},{6,14},... | collective-permute-start | bytes 319496 | tf_op jit(solution)/shard_map/ppermute | solution.py:89
  12.4 0.0 collective-permute-done.4.across_ref
  12.4 0.1 collective-permute-start.5
  12.5 0.5 %collective-permute-start.6 = (bf16[384,128]{1,0:T(8,128)(2,1)S(1)}, bf16[384,128]{1,0:T(8,128)(2,1)S(1)}, u32[]{:S(2)}, u32[]{:S(2)}) collective-permute-start(bf16[384,128]{1,0:T(8,128)(2,1)S(1)} %get-tuple-element.63), channel_id=1, source_target_pairs={{0,1},{1,0},{2,3},{3,2},{4,5},{5,4},{6,7},{7,6},{8,9},{9,8},{10,11... | collective-permute-start | bytes 294920 | tf_op jit(solution)/shard_map/ppermute | solution.py:93
  13.0 1.9 %collective-permute-start.9 = (bf16[384,128]{1,0:T(8,128)(2,1)S(1)}, bf16[384,128]{1,0:T(8,128)(2,1)S(1)}, u32[]{:S(2)}, u32[]{:S(2)}) collective-permute-start(bf16[384,128]{1,0:T(8,128)(2,1)S(1)} %get-tuple-element.40.own_ref), channel_id=1, source_target_pairs={{0,2},{1,3},{2,0},{3,1},{4,6},{5,7},{6,4},{7,5},{8,10},{9,11},{10,... | collective-permute-start | bytes 294920 | tf_op jit(solution)/shard_map/ppermute | solution.py:93
  14.9 0.0 collective-permute-done.5.rest_0_
  14.9 0.0 collective-permute-done.6.rest_1_
  14.9 0.9 %shard_map.76 = (bf16[416,128]{1,0:T(8,128)(2,1)S(1)}, bf16[416,128]{1,0:T(8,128)(2,1)S(1)}, f32[2,384,128]{2,1,0:T(8,128)S(1)}) custom-call(bf16[768,128]{1,0:T(8,128)(2,1)S(1)} %get-tuple-element.36.own_ref, bf16[4,384,128]{2,1,0:T(8,128)(2,1)S(1)} %collective-permute-done.beside_ref, bf16[768,128]{1,0:T(8,128)(2,1)S(1)} %collective-permute-done.4.across_ref, ...), custom_call_target="tpu_custom_call" | custom-call | tf_op jit(solution)/shard_map/pallas_call | solution.py:97
  15.8 1.6 %collective-permute-start.7 = (bf16[416,128]{1,0:T(8,128)(2,1)S(1)}, bf16[416,128]{1,0:T(8,128)(2,1)S(1)}, u32[]{:S(2)}, u32[]{:S(2)}) collective-permute-start(bf16[416,128]{1,0:T(8,128)(2,1)S(1)} %get-tuple-element.38), channel_id=1, source_target_pairs={{0,4},{4,8},{8,12},{12,0},{1,5},{5,9},{9,13},{13,1},{2,6},{6,10},{... | collective-permute-start | bytes 319496 | tf_op jit(solution)/shard_map/ppermute | solution.py:89
  17.4 2.2 %collective-permute-start.8 = (bf16[416,128]{1,0:T(8,128)(2,1)S(1)}, bf16[416,128]{1,0:T(8,128)(2,1)S(1)}, u32[]{:S(2)}, u32[]{:S(2)}) collective-permute-start(bf16[416,128]{1,0:T(8,128)(2,1)S(1)} %get-tuple-element.39), channel_id=1, source_target_pairs={{0,12},{4,0},{8,4},{12,8},{1,13},{5,1},{9,5},{13,9},{2,14},{6,2},{... | collective-permute-start | bytes 319496 | tf_op jit(solution)/shard_map/ppermute | solution.py:89
  19.7 0.0 collective-permute-done.9.across_ref
  19.7 0.0 collective-permute-start.10
  19.7 0.0 collective-permute-done.3.block_ref.refs_0_
  19.7 0.0 copy-done.5
  19.7 1.3 %collective-permute-done.10.rest_0_ = bf16[384,128]{1,0:T(8,128)(2,1)S(1)} collective-permute-done((bf16[384,128]{1,0:T(8,128)(2,1)S(1)}, bf16[384,128]{1,0:T(8,128)(2,1)S(1)}, u32[]{:S(2)}, u32[]{:S(2)}) %collective-permute-start.10) | collective-permute-done | bytes 98336 | tf_op jit(solution)/shard_map/ppermute | solution.py:93
  21.0 0.6 %shard_map.77 = (bf16[416,128]{1,0:T(8,128)(2,1)S(1)}, f32[1,384,128]{2,1,0:T(8,128)S(1)}) custom-call(bf16[384,128]{1,0:T(8,128)(2,1)S(1)} %get-tuple-element.40.own_ref, bf16[4,384,128]{2,1,0:T(8,128)(2,1)S(1)} %collective-permute-done.beside_ref, bf16[384,128]{1,0:T(8,128)(2,1)S(1)} %collective-permute-done.9.across_ref, f32[4,128]{1,0:T(4,128)S(1)} %bitcast.8, ...), custom_call_target="tpu_custom_call" | custom-call | tf_op jit(solution)/shard_map/pallas_call | solution.py:97
  21.6 1.9 %collective-permute-done.7.refs_1_ = bf16[416,128]{1,0:T(8,128)(2,1)S(1)} collective-permute-done((bf16[416,128]{1,0:T(8,128)(2,1)S(1)}, bf16[416,128]{1,0:T(8,128)(2,1)S(1)}, u32[]{:S(2)}, u32[]{:S(2)}) %collective-permute-start.7) | collective-permute-done | bytes 106528 | tf_op jit(solution)/shard_map/ppermute | solution.py:89
  23.5 0.6 %collective-permute-done.8.refs_2_ = bf16[416,128]{1,0:T(8,128)(2,1)S(1)} collective-permute-done((bf16[416,128]{1,0:T(8,128)(2,1)S(1)}, bf16[416,128]{1,0:T(8,128)(2,1)S(1)}, u32[]{:S(2)}, u32[]{:S(2)}) %collective-permute-start.8) | collective-permute-done | bytes 106528 | tf_op jit(solution)/shard_map/ppermute | solution.py:89
  24.1 2.5 %shard_map.79 = (bf16[400,128]{1,0:T(8,128)(2,1)S(1)}, bf16[400,128]{1,0:T(8,128)(2,1)S(1)}, bf16[400,128]{1,0:T(8,128)(2,1)S(1)}, bf16[400,128]{1,0:T(8,128)(2,1)S(1)}) custom-call(bf16[416,128]{1,0:T(8,128)(2,1)S(1)} %collective-permute-done.3.block_ref.refs_0_, bf16[416,128]{1,0:T(8,128)(2,1)S(1)} %collective-permute-done.7.refs_1_, ...), custom_call_target="tpu_custom_call" | custom-call | tf_op jit(solution)/shard_map/pallas_call | solution.py:97
  26.6 2.2 %collective-permute-start.13 = (bf16[400,128]{1,0:T(8,128)(2,1)S(1)}, bf16[400,128]{1,0:T(8,128)(2,1)S(1)}, u32[]{:S(2)}, u32[]{:S(2)}) collective-permute-start(bf16[400,128]{1,0:T(8,128)(2,1)S(1)} %get-tuple-element.51), channel_id=1, source_target_pairs={{0,12},{4,0},{8,4},{12,8},{1,13},{5,1},{9,5},{13,9},{2,14},{6,2},{... | collective-permute-start | bytes 307208 | tf_op jit(solution)/shard_map/ppermute | solution.py:89
  28.8 0.0 collective-permute-start.12
  28.8 1.0 %collective-permute-start.11 = (bf16[400,128]{1,0:T(8,128)(2,1)S(1)}, bf16[400,128]{1,0:T(8,128)(2,1)S(1)}, u32[]{:S(2)}, u32[]{:S(2)}) collective-permute-start(bf16[400,128]{1,0:T(8,128)(2,1)S(1)} %get-tuple-element.45), channel_id=1, source_target_pairs={{0,8},{4,12},{8,0},{12,4},{1,9},{5,13},{9,1},{13,5},{2,10},{6,14},... | collective-permute-start | bytes 307208 | tf_op jit(solution)/shard_map/ppermute | solution.py:89
  29.8 0.0 copy-done.1
  29.9 1.9 %collective-permute-start.14 = (bf16[640,128]{1,0:T(8,128)(2,1)S(1)}, bf16[640,128]{1,0:T(8,128)(2,1)S(1)}, u32[]{:S(2)}, u32[]{:S(2)}) collective-permute-start(bf16[640,128]{1,0:T(8,128)(2,1)S(1)} %get-tuple-element.49.refs_0_), channel_id=1, source_target_pairs={{0,2},{1,3},{2,0},{3,1},{4,6},{5,7},{6,4},{7,5},{8,10},{9,11},{10,... | collective-permute-start | bytes 491528 | tf_op jit(solution)/shard_map/ppermute | solution.py:93
  31.8 0.0 collective-permute-start.18
  31.8 0.2 collective-permute-done.13.refs_1_
  32.0 3.2 %collective-permute-done.12.refs_0_ = bf16[400,128]{1,0:T(8,128)(2,1)S(1)} collective-permute-done((bf16[400,128]{1,0:T(8,128)(2,1)S(1)}, bf16[400,128]{1,0:T(8,128)(2,1)S(1)}, u32[]{:S(2)}, u32[]{:S(2)}) %collective-permute-start.12) | collective-permute-done | bytes 102432 | tf_op jit(solution)/shard_map/ppermute | solution.py:89
  35.3 2.9 %collective-permute-start.21 = (bf16[768,128]{1,0:T(8,128)(2,1)S(1)}, bf16[768,128]{1,0:T(8,128)(2,1)S(1)}, u32[]{:S(2)}, u32[]{:S(2)}) collective-permute-start(bf16[768,128]{1,0:T(8,128)(2,1)S(1)} %shard_map.81.refs_4_), channel_id=1, source_target_pairs={{0,2},{1,3},{2,0},{3,1},{4,6},{5,7},{6,4},{7,5},{8,10},{9,11},{10,... | collective-permute-start | bytes 589832 | tf_op jit(solution)/shard_map/ppermute | solution.py:93
  38.2 0.0 collective-permute-start.20
  38.2 0.2 collective-permute-done.11.refs_0_
  38.5 0.0 collective-permute-done.14.refs_2_
  38.5 2.0 %collective-permute-start.16 = (bf16[384,128]{1,0:T(8,128)(2,1)S(1)}, bf16[384,128]{1,0:T(8,128)(2,1)S(1)}, u32[]{:S(2)}, u32[]{:S(2)}) collective-permute-start(bf16[384,128]{1,0:T(8,128)(2,1)S(1)} %shard_map.82.refs_0_), channel_id=1, source_target_pairs={{0,2},{1,3},{2,0},{3,1},{4,6},{5,7},{6,4},{7,5},{8,10},{9,11},{10,... | collective-permute-start | bytes 294920 | tf_op jit(solution)/shard_map/ppermute | solution.py:93
  40.5 2.0 %collective-permute-done.21.refs_6_ = bf16[768,128]{1,0:T(8,128)(2,1)S(1)} collective-permute-done((bf16[768,128]{1,0:T(8,128)(2,1)S(1)}, bf16[768,128]{1,0:T(8,128)(2,1)S(1)}, u32[]{:S(2)}, u32[]{:S(2)}) %collective-permute-start.21) | collective-permute-done | bytes 196640 | tf_op jit(solution)/shard_map/ppermute | solution.py:93
  42.5 0.0 collective-permute-start.22
  42.5 0.5 %collective-permute-start.19 = (bf16[640,128]{1,0:T(8,128)(2,1)S(1)}, bf16[640,128]{1,0:T(8,128)(2,1)S(1)}, u32[]{:S(2)}, u32[]{:S(2)}) collective-permute-start(bf16[640,128]{1,0:T(8,128)(2,1)S(1)} %collective-permute-done.14.refs_2_), channel_id=1, source_target_pairs={{0,1},{1,0},{2,3},{3,2},{4,5},{5,4},{6,7},{7,6},{8,9},{9,8},{10,11... | collective-permute-start | bytes 491528 | tf_op jit(solution)/shard_map/ppermute | solution.py:93
  43.0 1.0 %collective-permute-done.16.refs_2_ = bf16[384,128]{1,0:T(8,128)(2,1)S(1)} collective-permute-done((bf16[384,128]{1,0:T(8,128)(2,1)S(1)}, bf16[384,128]{1,0:T(8,128)(2,1)S(1)}, u32[]{:S(2)}, u32[]{:S(2)}) %collective-permute-start.16) | collective-permute-done | bytes 98336 | tf_op jit(solution)/shard_map/ppermute | solution.py:93
  44.0 0.0 collective-permute-start.15
  44.0 0.0 collective-permute-done.18.refs_1_
  44.0 0.5 %collective-permute-start.17 = (bf16[384,128]{1,0:T(8,128)(2,1)S(1)}, bf16[384,128]{1,0:T(8,128)(2,1)S(1)}, u32[]{:S(2)}, u32[]{:S(2)}) collective-permute-start(bf16[384,128]{1,0:T(8,128)(2,1)S(1)} %collective-permute-done.16.refs_2_), channel_id=1, source_target_pairs={{0,1},{1,0},{2,3},{3,2},{4,5},{5,4},{6,7},{7,6},{8,9},{9,8},{10,11... | collective-permute-start | bytes 294920 | tf_op jit(solution)/shard_map/ppermute | solution.py:93
  44.5 0.0 collective-permute-done.20.refs_5_
  44.5 0.0 collective-permute-done.19.refs_3_
  44.5 0.0 collective-permute-done.22.refs_7_
  44.5 0.5 %shard_map.83 = (bf16[3,384,128]{2,1,0:T(8,128)(2,1)S(1)}, bf16[512,128]{1,0:T(8,128)(2,1)S(1)}) custom-call(bf16[640,128]{1,0:T(8,128)(2,1)S(1)} %get-tuple-element.49.refs_0_, bf16[512,128]{1,0:T(8,128)(2,1)S(1)} %collective-permute-done.18.refs_1_, bf16[640,128]{1,0:T(8,128)(2,1)S(1)} %collective-permute-done.14.refs_2_, ...), custom_call_target="tpu_custom_call" | custom-call | tf_op jit(solution)/shard_map/pallas_call | solution.py:97
  45.0 0.3 collective-permute-done.15.refs_1_
  45.3 0.2 collective-permute-done.17.refs_3_
  45.4 0.9 %shard_map.84 = bf16[4,384,128]{2,1,0:T(8,128)(2,1)} custom-call(bf16[384,128]{1,0:T(8,128)(2,1)S(1)} %shard_map.82.refs_0_, bf16[384,128]{1,0:T(8,128)(2,1)S(1)} %collective-permute-done.15.refs_1_, bf16[384,128]{1,0:T(8,128)(2,1)S(1)} %collective-permute-done.16.refs_2_, bf16[384,128]{1,0:T(8,128)(2,1)S(1)} %collective-permute-done.17.refs_3_, ...), custom_call_target="tpu_custom_call" | custom-call | tf_op jit(solution)/shard_map/pallas_call | solution.py:386
  (9 shorter events, 0.1 us)
Async XLA Ops:
  0.0 1.0 %copy-start.6 = (bf16[4,384,128]{2,1,0:T(8,128)(2,1)S(1)}, bf16[4,384,128]{2,1,0:T(8,128)(2,1)}, u32[]{:S(2)}) copy-start(bf16[4,384,128]{2,1,0:T(8,128)(2,1)} %records_ref.3) | copy-start | bytes 1179652
  0.0 8.8 %copy-start = (bf16[512,3,128]{2,0,1:T(8,128)(2,1)S(1)}, bf16[512,3,128]{2,0,1:T(8,128)(2,1)}, u32[]{:S(2)}) copy-start(bf16[512,3,128]{2,0,1:T(8,128)(2,1)} %param.9) | copy-start | bytes 1179652
  1.0 7.8 %collective-permute-start = (bf16[4,384,128]{2,1,0:T(8,128)(2,1)S(1)}, bf16[4,384,128]{2,1,0:T(8,128)(2,1)S(1)}, u32[]{:S(2)}, u32[]{:S(2)}) collective-permute-start(bf16[4,384,128]{2,1,0:T(8,128)(2,1)S(1)} %copy-done.6), channel_id=1, source_target_pairs={{0,1},{1,0},{2,3},{3,2},{4,5},{5,4},{6,7},{7,6},{8,9},{9,8},{10,11... | collective-permute-start | bytes 1179656 | tf_op jit(solution)/shard_map/ppermute | solution.py:93
  1.5 6.0 %collective-permute-start.1 = (bf16[384,128]{1,0:T(8,128)(2,1)S(1)}, bf16[384,128]{1,0:T(8,128)(2,1)S(1)}, u32[]{:S(2)}, u32[]{:S(2)}) collective-permute-start(bf16[384,128]{1,0:T(8,128)(2,1)S(1)} %shard_map.73.own_ref), channel_id=1, source_target_pairs={{0,2},{1,3},{2,0},{3,1},{4,6},{5,7},{6,4},{7,5},{8,10},{9,11},{10,... | collective-permute-start | bytes 294920 | tf_op jit(solution)/shard_map/ppermute | solution.py:93
  4.1 4.7 %copy-start.2 = (f32[3,3,128]{2,1,0:T(4,128)S(1)}, f32[3,3,128]{2,1,0:T(4,128)}, u32[]{:S(2)}) copy-start(f32[3,3,128]{2,1,0:T(4,128)} %refs_2_.3) | copy-start | bytes 13828
  5.2 3.7 %copy-start.3 = (bf16[4,384]{1,0:T(4,128)(2,1)S(1)}, bf16[4,384]{1,0:T(4,128)(2,1)}, u32[]{:S(2)}) copy-start(bf16[4,384]{1,0:T(4,128)(2,1)} %taps_ref.5) | copy-start | bytes 9220
  5.2 3.7 %copy-start.4 = (f32[512]{0:T(512)S(1)}, f32[512]{0:T(512)}, u32[]{:S(2)}) copy-start(f32[512]{0:T(512)} %param.8) | copy-start | bytes 6148
  5.2 7.2 %collective-permute-start.4 = (bf16[768,128]{1,0:T(8,128)(2,1)S(1)}, bf16[768,128]{1,0:T(8,128)(2,1)S(1)}, u32[]{:S(2)}, u32[]{:S(2)}) collective-permute-start(bf16[768,128]{1,0:T(8,128)(2,1)S(1)} %get-tuple-element.36.own_ref), channel_id=1, source_target_pairs={{0,2},{1,3},{2,0},{3,1},{4,6},{5,7},{6,4},{7,5},{8,10},{9,11},{10,... | collective-permute-start | bytes 589832 | tf_op jit(solution)/shard_map/ppermute | solution.py:93
  7.5 1.3 %collective-permute-start.2 = (bf16[384,128]{1,0:T(8,128)(2,1)S(1)}, bf16[384,128]{1,0:T(8,128)(2,1)S(1)}, u32[]{:S(2)}, u32[]{:S(2)}) collective-permute-start(bf16[384,128]{1,0:T(8,128)(2,1)S(1)} %collective-permute-done.1.across_ref), channel_id=1, source_target_pairs={{0,1},{1,0},{2,3},{3,2},{4,5},{5,4},{6,7},{7,6},{8,9},{9,8},{10,11... | collective-permute-start | bytes 294920 | tf_op jit(solution)/shard_map/ppermute | solution.py:93
  9.4 10.2 %collective-permute-start.3 = (bf16[416,128]{1,0:T(8,128)(2,1)S(1)}, bf16[416,128]{1,0:T(8,128)(2,1)S(1)}, u32[]{:S(2)}, u32[]{:S(2)}) collective-permute-start(bf16[416,128]{1,0:T(8,128)(2,1)S(1)} %get-tuple-element.35), channel_id=1, source_target_pairs={{0,8},{4,12},{8,0},{12,4},{1,9},{5,13},{9,1},{13,5},{2,10},{6,14},... | collective-permute-start | bytes 319496 | tf_op jit(solution)/shard_map/ppermute | solution.py:89
  12.4 2.5 %collective-permute-start.5 = (bf16[384,128]{1,0:T(8,128)(2,1)S(1)}, bf16[384,128]{1,0:T(8,128)(2,1)S(1)}, u32[]{:S(2)}, u32[]{:S(2)}) collective-permute-start(bf16[384,128]{1,0:T(8,128)(2,1)S(1)} %get-tuple-element.64), channel_id=1, source_target_pairs={{0,1},{1,0},{2,3},{3,2},{4,5},{5,4},{6,7},{7,6},{8,9},{9,8},{10,11... | collective-permute-start | bytes 294920 | tf_op jit(solution)/shard_map/ppermute | solution.py:93
  12.5 2.4 %collective-permute-start.6 = (bf16[384,128]{1,0:T(8,128)(2,1)S(1)}, bf16[384,128]{1,0:T(8,128)(2,1)S(1)}, u32[]{:S(2)}, u32[]{:S(2)}) collective-permute-start(bf16[384,128]{1,0:T(8,128)(2,1)S(1)} %get-tuple-element.63), channel_id=1, source_target_pairs={{0,1},{1,0},{2,3},{3,2},{4,5},{5,4},{6,7},{7,6},{8,9},{9,8},{10,11... | collective-permute-start | bytes 294920 | tf_op jit(solution)/shard_map/ppermute | solution.py:93
  13.0 6.7 %collective-permute-start.9 = (bf16[384,128]{1,0:T(8,128)(2,1)S(1)}, bf16[384,128]{1,0:T(8,128)(2,1)S(1)}, u32[]{:S(2)}, u32[]{:S(2)}) collective-permute-start(bf16[384,128]{1,0:T(8,128)(2,1)S(1)} %get-tuple-element.40.own_ref), channel_id=1, source_target_pairs={{0,2},{1,3},{2,0},{3,1},{4,6},{5,7},{6,4},{7,5},{8,10},{9,11},{10,... | collective-permute-start | bytes 294920 | tf_op jit(solution)/shard_map/ppermute | solution.py:93
  15.8 7.7 %collective-permute-start.7 = (bf16[416,128]{1,0:T(8,128)(2,1)S(1)}, bf16[416,128]{1,0:T(8,128)(2,1)S(1)}, u32[]{:S(2)}, u32[]{:S(2)}) collective-permute-start(bf16[416,128]{1,0:T(8,128)(2,1)S(1)} %get-tuple-element.38), channel_id=1, source_target_pairs={{0,4},{4,8},{8,12},{12,0},{1,5},{5,9},{9,13},{13,1},{2,6},{6,10},{... | collective-permute-start | bytes 319496 | tf_op jit(solution)/shard_map/ppermute | solution.py:89
  17.4 2.3 %copy-start.5 = (f32[128]{0:T(128)S(1)}, f32[128]{0:T(128)}, u32[]{:S(2)}) copy-start(f32[128]{0:T(128)} %param.12) | copy-start | bytes 1540
  17.4 6.7 %collective-permute-start.8 = (bf16[416,128]{1,0:T(8,128)(2,1)S(1)}, bf16[416,128]{1,0:T(8,128)(2,1)S(1)}, u32[]{:S(2)}, u32[]{:S(2)}) collective-permute-start(bf16[416,128]{1,0:T(8,128)(2,1)S(1)} %get-tuple-element.39), channel_id=1, source_target_pairs={{0,12},{4,0},{8,4},{12,8},{1,13},{5,1},{9,5},{13,9},{2,14},{6,2},{... | collective-permute-start | bytes 319496 | tf_op jit(solution)/shard_map/ppermute | solution.py:89
  19.7 1.3 %collective-permute-start.10 = (bf16[384,128]{1,0:T(8,128)(2,1)S(1)}, bf16[384,128]{1,0:T(8,128)(2,1)S(1)}, u32[]{:S(2)}, u32[]{:S(2)}) collective-permute-start(bf16[384,128]{1,0:T(8,128)(2,1)S(1)} %collective-permute-done.9.across_ref), channel_id=1, source_target_pairs={{0,1},{1,0},{2,3},{3,2},{4,5},{5,4},{6,7},{7,6},{8,9},{9,8},{10,11... | collective-permute-start | bytes 294920 | tf_op jit(solution)/shard_map/ppermute | solution.py:93
  24.1 5.7 %copy-start.1 = (bf16[128,512]{1,0:T(8,128)(2,1)S(1)}, bf16[128,512]{1,0:T(8,128)(2,1)}, u32[]{:S(2)}) copy-start(bf16[128,512]{1,0:T(8,128)(2,1)} %refs_8_.1) | copy-start | bytes 393220
  26.6 5.4 %collective-permute-start.13 = (bf16[400,128]{1,0:T(8,128)(2,1)S(1)}, bf16[400,128]{1,0:T(8,128)(2,1)S(1)}, u32[]{:S(2)}, u32[]{:S(2)}) collective-permute-start(bf16[400,128]{1,0:T(8,128)(2,1)S(1)} %get-tuple-element.51), channel_id=1, source_target_pairs={{0,12},{4,0},{8,4},{12,8},{1,13},{5,1},{9,5},{13,9},{2,14},{6,2},{... | collective-permute-start | bytes 307208 | tf_op jit(solution)/shard_map/ppermute | solution.py:89
  28.8 6.5 %collective-permute-start.12 = (bf16[400,128]{1,0:T(8,128)(2,1)S(1)}, bf16[400,128]{1,0:T(8,128)(2,1)S(1)}, u32[]{:S(2)}, u32[]{:S(2)}) collective-permute-start(bf16[400,128]{1,0:T(8,128)(2,1)S(1)} %get-tuple-element.46), channel_id=1, source_target_pairs={{0,4},{4,8},{8,12},{12,0},{1,5},{5,9},{9,13},{13,1},{2,6},{6,10},{... | collective-permute-start | bytes 307208 | tf_op jit(solution)/shard_map/ppermute | solution.py:89
  28.8 9.6 %collective-permute-start.11 = (bf16[400,128]{1,0:T(8,128)(2,1)S(1)}, bf16[400,128]{1,0:T(8,128)(2,1)S(1)}, u32[]{:S(2)}, u32[]{:S(2)}) collective-permute-start(bf16[400,128]{1,0:T(8,128)(2,1)S(1)} %get-tuple-element.45), channel_id=1, source_target_pairs={{0,8},{4,12},{8,0},{12,4},{1,9},{5,13},{9,1},{13,5},{2,10},{6,14},... | collective-permute-start | bytes 307208 | tf_op jit(solution)/shard_map/ppermute | solution.py:89
  29.9 8.6 %collective-permute-start.14 = (bf16[640,128]{1,0:T(8,128)(2,1)S(1)}, bf16[640,128]{1,0:T(8,128)(2,1)S(1)}, u32[]{:S(2)}, u32[]{:S(2)}) collective-permute-start(bf16[640,128]{1,0:T(8,128)(2,1)S(1)} %get-tuple-element.49.refs_0_), channel_id=1, source_target_pairs={{0,2},{1,3},{2,0},{3,1},{4,6},{5,7},{6,4},{7,5},{8,10},{9,11},{10,... | collective-permute-start | bytes 491528 | tf_op jit(solution)/shard_map/ppermute | solution.py:93
  31.8 12.2 %collective-permute-start.18 = (bf16[512,128]{1,0:T(8,128)(2,1)S(1)}, bf16[512,128]{1,0:T(8,128)(2,1)S(1)}, u32[]{:S(2)}, u32[]{:S(2)}) collective-permute-start(bf16[512,128]{1,0:T(8,128)(2,1)S(1)} %get-tuple-element.58), channel_id=1, source_target_pairs={{0,1},{1,0},{2,3},{3,2},{4,5},{5,4},{6,7},{7,6},{8,9},{9,8},{10,11... | collective-permute-start | bytes 393224 | tf_op jit(solution)/shard_map/ppermute | solution.py:93
  35.3 7.2 %collective-permute-start.21 = (bf16[768,128]{1,0:T(8,128)(2,1)S(1)}, bf16[768,128]{1,0:T(8,128)(2,1)S(1)}, u32[]{:S(2)}, u32[]{:S(2)}) collective-permute-start(bf16[768,128]{1,0:T(8,128)(2,1)S(1)} %shard_map.81.refs_4_), channel_id=1, source_target_pairs={{0,2},{1,3},{2,0},{3,1},{4,6},{5,7},{6,4},{7,5},{8,10},{9,11},{10,... | collective-permute-start | bytes 589832 | tf_op jit(solution)/shard_map/ppermute | solution.py:93
  38.2 6.3 %collective-permute-start.20 = (bf16[768,128]{1,0:T(8,128)(2,1)S(1)}, bf16[768,128]{1,0:T(8,128)(2,1)S(1)}, u32[]{:S(2)}, u32[]{:S(2)}) collective-permute-start(bf16[768,128]{1,0:T(8,128)(2,1)S(1)} %shard_map.81.refs_4_), channel_id=1, source_target_pairs={{0,1},{1,0},{2,3},{3,2},{4,5},{5,4},{6,7},{7,6},{8,9},{9,8},{10,11... | collective-permute-start | bytes 589832 | tf_op jit(solution)/shard_map/ppermute | solution.py:93
  38.5 5.5 %collective-permute-start.16 = (bf16[384,128]{1,0:T(8,128)(2,1)S(1)}, bf16[384,128]{1,0:T(8,128)(2,1)S(1)}, u32[]{:S(2)}, u32[]{:S(2)}) collective-permute-start(bf16[384,128]{1,0:T(8,128)(2,1)S(1)} %shard_map.82.refs_0_), channel_id=1, source_target_pairs={{0,2},{1,3},{2,0},{3,1},{4,6},{5,7},{6,4},{7,5},{8,10},{9,11},{10,... | collective-permute-start | bytes 294920 | tf_op jit(solution)/shard_map/ppermute | solution.py:93
  42.5 2.0 %collective-permute-start.22 = (bf16[768,128]{1,0:T(8,128)(2,1)S(1)}, bf16[768,128]{1,0:T(8,128)(2,1)S(1)}, u32[]{:S(2)}, u32[]{:S(2)}) collective-permute-start(bf16[768,128]{1,0:T(8,128)(2,1)S(1)} %collective-permute-done.21.refs_6_), channel_id=1, source_target_pairs={{0,1},{1,0},{2,3},{3,2},{4,5},{5,4},{6,7},{7,6},{8,9},{9,8},{10,11... | collective-permute-start | bytes 589832 | tf_op jit(solution)/shard_map/ppermute | solution.py:93
  42.5 2.0 %collective-permute-start.19 = (bf16[640,128]{1,0:T(8,128)(2,1)S(1)}, bf16[640,128]{1,0:T(8,128)(2,1)S(1)}, u32[]{:S(2)}, u32[]{:S(2)}) collective-permute-start(bf16[640,128]{1,0:T(8,128)(2,1)S(1)} %collective-permute-done.14.refs_2_), channel_id=1, source_target_pairs={{0,1},{1,0},{2,3},{3,2},{4,5},{5,4},{6,7},{7,6},{8,9},{9,8},{10,11... | collective-permute-start | bytes 491528 | tf_op jit(solution)/shard_map/ppermute | solution.py:93
  44.0 1.3 %collective-permute-start.15 = (bf16[384,128]{1,0:T(8,128)(2,1)S(1)}, bf16[384,128]{1,0:T(8,128)(2,1)S(1)}, u32[]{:S(2)}, u32[]{:S(2)}) collective-permute-start(bf16[384,128]{1,0:T(8,128)(2,1)S(1)} %shard_map.82.refs_0_), channel_id=1, source_target_pairs={{0,1},{1,0},{2,3},{3,2},{4,5},{5,4},{6,7},{7,6},{8,9},{9,8},{10,11... | collective-permute-start | bytes 294920 | tf_op jit(solution)/shard_map/ppermute | solution.py:93
  44.0 1.5 %collective-permute-start.17 = (bf16[384,128]{1,0:T(8,128)(2,1)S(1)}, bf16[384,128]{1,0:T(8,128)(2,1)S(1)}, u32[]{:S(2)}, u32[]{:S(2)}) collective-permute-start(bf16[384,128]{1,0:T(8,128)(2,1)S(1)} %collective-permute-done.16.refs_2_), channel_id=1, source_target_pairs={{0,1},{1,0},{2,3},{3,2},{4,5},{5,4},{6,7},{7,6},{8,9},{9,8},{10,11... | collective-permute-start | bytes 294920 | tf_op jit(solution)/shard_map/ppermute | solution.py:93

commit v6 on v5

--- a/solution.py
+++ b/solution.py
@@ -276,14 +276,23 @@
             sums[q, b * LANES : (b + 1) * LANES, :] = total.astype(bf16)
 
         width = length + LANES
+        pair = 2 * LANES
+        pairs = half // pair
+        crossed = [[None, None] for _ in range(pairs)]
+        for lag in range(1, 2 * pairs):
+            blocks = [q for q in range(pairs) if 0 <= lag - pairs + q < pairs]
+            side = jnp.concatenate([source[q * pair : (q + 1) * pair, 0:LANES] for q in blocks], axis=1)
+            for h in range(2):
+                start = length - lag * pair - h * LANES
+                terms = jnp.dot(bands[:, start : start + pair], side, preferred_element_type=f32)
+                for i, q in enumerate(blocks):
+                    part, place = terms[:, i * LANES : (i + 1) * LANES], crossed[lag - pairs + q]
+                    place[h] = part if place[h] is None else place[h] + part
         for p in range(half // LANES):
             reach = (p + 1) * LANES
             within = jnp.dot(bands[:, width - reach :], source[0:reach, :], preferred_element_type=f32)
-            across = jnp.dot(
-                bands[:, width - reach - half : width - reach], source[:, 0:LANES], preferred_element_type=f32
-            )
             finish(p, within[:, 0:LANES])
-            finish(p + half // LANES, within[:, LANES:] + across)
+            finish(p + half // LANES, within[:, LANES:] + crossed[p // 2][p % 2])
         for q in range(n):
             if q == 0:
                 tail = jnp.zeros((2, LANES), f32)

time: 46.5 us -> 46.1 us (level)
  no operation moved by 1% of the time
where the time goes in v6:
time: 46.1 us; the launch traced here: 46 us
  starting transfers between devices  23.6 us (51%)
  waiting for transfers between devices  14.4 us (31%)
  Pallas kernels  7.77 us (17%)
    ppermute x17, starting transfers between devices, exchange(): lax.ppermute(block, axis, [(i, i ^ mask) for i in range(lax.axis_size(axi...  13.6 us
    ppermute x6, starting transfers between devices, rotate(): lax.ppermute(block, axis, [(i, (i + distance) % n) for i in range(n)])  9.99 us
    ppermute x17, waiting for transfers between devices, exchange(): lax.ppermute(block, axis, [(i, i ^ mask) for i in range(lax.axis_size(axi...  8.21 us
    ppermute x6, waiting for transfers between devices, rotate(): lax.ppermute(block, axis, [(i, (i + distance) % n) for i in range(n)])  6.15 us
    pallas_call x9, Pallas kernels, vmem_call(): pl.pallas_call(kernel, out_shape=tuple(outs), in_specs=[pl.BlockSpec(memo...  4.79 us
    pallas_call x2, Pallas kernels, pick(): pl.pallas_call(kernel, out_shape=tuple(shapes), in_specs=[pl.BlockSpec(me...  2.04 us
    pallas_call x1, Pallas kernels, mix_last(): pl.pallas_call(kernel, out_shape=jax.ShapeDtypeStruct((count, block_len,...  0.94 us
  transfers between devices with their start and end apart: 23, of which 12 were waited for; matrix products, arithmetic and copies ran while one was open for 0% of the time, Pallas kernels for 8%

profile of v6, /device:TPU:0, one launch (start us, length us, event | category | flops | bytes accessed | tf_op | source)
XLA Modules:
  0.0 46.0 jit_solution(5840786440122851961)
XLA Ops:
  0.0 0.0 copy-start.6
  0.0 1.0 %shard_map.73.own_ref = bf16[384,128]{1,0:T(8,128)(2,1)S(1)} custom-call(bf16[4,384,128]{2,1,0:T(8,128)(2,1)} %records_ref.3), custom_call_target="tpu_custom_call" | custom-call | tf_op jit(solution)/shard_map/pallas_call | solution.py:132
  1.0 0.0 copy-done.6
  1.0 0.5 %collective-permute-start = (bf16[4,384,128]{2,1,0:T(8,128)(2,1)S(1)}, bf16[4,384,128]{2,1,0:T(8,128)(2,1)S(1)}, u32[]{:S(2)}, u32[]{:S(2)}) collective-permute-start(bf16[4,384,128]{2,1,0:T(8,128)(2,1)S(1)} %copy-done.6), channel_id=1, source_target_pairs={{0,1},{1,0},{2,3},{3,2},{4,5},{5,4},{6,7},{7,6},{8,9},{9,8},{10,11... | collective-permute-start | bytes 1179656 | tf_op jit(solution)/shard_map/ppermute | solution.py:93
  1.5 2.6 %collective-permute-start.1 = (bf16[384,128]{1,0:T(8,128)(2,1)S(1)}, bf16[384,128]{1,0:T(8,128)(2,1)S(1)}, u32[]{:S(2)}, u32[]{:S(2)}) collective-permute-start(bf16[384,128]{1,0:T(8,128)(2,1)S(1)} %shard_map.73.own_ref), channel_id=1, source_target_pairs={{0,2},{1,3},{2,0},{3,1},{4,6},{5,7},{6,4},{7,5},{8,10},{9,11},{10,... | collective-permute-start | bytes 294920 | tf_op jit(solution)/shard_map/ppermute | solution.py:93
  4.1 1.0 %shard_map.75 = (bf16[768,128]{1,0:T(8,128)(2,1)S(1)}, bf16[384,128]{1,0:T(8,128)(2,1)S(1)}) custom-call(bf16[4,384,128]{2,1,0:T(8,128)(2,1)} %records_ref.3), custom_call_target="tpu_custom_call" | custom-call | tf_op jit(solution)/shard_map/pallas_call | solution.py:132
  5.2 0.0 copy-start.3
  5.2 0.0 copy-start.4
  5.2 0.1 collective-permute-start.4
  5.3 2.2 %collective-permute-done.1.across_ref = bf16[384,128]{1,0:T(8,128)(2,1)S(1)} collective-permute-done((bf16[384,128]{1,0:T(8,128)(2,1)S(1)}, bf16[384,128]{1,0:T(8,128)(2,1)S(1)}, u32[]{:S(2)}, u32[]{:S(2)}) %collective-permute-start.1) | collective-permute-done | bytes 98336 | tf_op jit(solution)/shard_map/ppermute | solution.py:93
  7.5 0.0 collective-permute-start.2
  7.5 1.3 %collective-permute-done.2.rest_0_ = bf16[384,128]{1,0:T(8,128)(2,1)S(1)} collective-permute-done((bf16[384,128]{1,0:T(8,128)(2,1)S(1)}, bf16[384,128]{1,0:T(8,128)(2,1)S(1)}, u32[]{:S(2)}, u32[]{:S(2)}) %collective-permute-start.2) | collective-permute-done | bytes 98336 | tf_op jit(solution)/shard_map/ppermute | solution.py:93
  8.8 0.0 collective-permute-done.beside_ref
  8.8 0.0 copy-done
  8.8 0.0 copy-done.2
  8.8 0.0 copy-done.3
  8.8 0.0 copy-done.4
  8.8 0.6 %shard_map.74 = (bf16[416,128]{1,0:T(8,128)(2,1)S(1)}, f32[1,384,128]{2,1,0:T(8,128)S(1)}) custom-call(bf16[384,128]{1,0:T(8,128)(2,1)S(1)} %shard_map.73.own_ref, bf16[4,384,128]{2,1,0:T(8,128)(2,1)S(1)} %collective-permute-done.beside_ref, bf16[384,128]{1,0:T(8,128)(2,1)S(1)} %collective-permute-done.1.across_ref, f32[4,128]{1,0:T(4,128)S(1)} %bitcast.6, ...), custom_call_target="tpu_custom_call" | custom-call | tf_op jit(solution)/shard_map/pallas_call | solution.py:97
  9.4 2.9 %collective-permute-start.3 = (bf16[416,128]{1,0:T(8,128)(2,1)S(1)}, bf16[416,128]{1,0:T(8,128)(2,1)S(1)}, u32[]{:S(2)}, u32[]{:S(2)}) collective-permute-start(bf16[416,128]{1,0:T(8,128)(2,1)S(1)} %get-tuple-element.35), channel_id=1, source_target_pairs={{0,8},{4,12},{8,0},{12,4},{1,9},{5,13},{9,1},{13,5},{2,10},{6,14},... | collective-permute-start | bytes 319496 | tf_op jit(solution)/shard_map/ppermute | solution.py:89
  12.4 0.0 collective-permute-done.4.across_ref
  12.4 0.1 collective-permute-start.5
  12.5 0.5 %collective-permute-start.6 = (bf16[384,128]{1,0:T(8,128)(2,1)S(1)}, bf16[384,128]{1,0:T(8,128)(2,1)S(1)}, u32[]{:S(2)}, u32[]{:S(2)}) collective-permute-start(bf16[384,128]{1,0:T(8,128)(2,1)S(1)} %get-tuple-element.63), channel_id=1, source_target_pairs={{0,1},{1,0},{2,3},{3,2},{4,5},{5,4},{6,7},{7,6},{8,9},{9,8},{10,11... | collective-permute-start | bytes 294920 | tf_op jit(solution)/shard_map/ppermute | solution.py:93
  13.0 1.9 %collective-permute-start.9 = (bf16[384,128]{1,0:T(8,128)(2,1)S(1)}, bf16[384,128]{1,0:T(8,128)(2,1)S(1)}, u32[]{:S(2)}, u32[]{:S(2)}) collective-permute-start(bf16[384,128]{1,0:T(8,128)(2,1)S(1)} %get-tuple-element.40.own_ref), channel_id=1, source_target_pairs={{0,2},{1,3},{2,0},{3,1},{4,6},{5,7},{6,4},{7,5},{8,10},{9,11},{10,... | collective-permute-start | bytes 294920 | tf_op jit(solution)/shard_map/ppermute | solution.py:93
  14.9 0.0 collective-permute-done.5.rest_0_
  14.9 0.0 collective-permute-done.6.rest_1_
  14.9 0.9 %shard_map.76 = (bf16[416,128]{1,0:T(8,128)(2,1)S(1)}, bf16[416,128]{1,0:T(8,128)(2,1)S(1)}, f32[2,384,128]{2,1,0:T(8,128)S(1)}) custom-call(bf16[768,128]{1,0:T(8,128)(2,1)S(1)} %get-tuple-element.36.own_ref, bf16[4,384,128]{2,1,0:T(8,128)(2,1)S(1)} %collective-permute-done.beside_ref, bf16[768,128]{1,0:T(8,128)(2,1)S(1)} %collective-permute-done.4.across_ref, ...), custom_call_target="tpu_custom_call" | custom-call | tf_op jit(solution)/shard_map/pallas_call | solution.py:97
  15.8 1.6 %collective-permute-start.7 = (bf16[416,128]{1,0:T(8,128)(2,1)S(1)}, bf16[416,128]{1,0:T(8,128)(2,1)S(1)}, u32[]{:S(2)}, u32[]{:S(2)}) collective-permute-start(bf16[416,128]{1,0:T(8,128)(2,1)S(1)} %get-tuple-element.38), channel_id=1, source_target_pairs={{0,4},{4,8},{8,12},{12,0},{1,5},{5,9},{9,13},{13,1},{2,6},{6,10},{... | collective-permute-start | bytes 319496 | tf_op jit(solution)/shard_map/ppermute | solution.py:89
  17.4 2.2 %collective-permute-start.8 = (bf16[416,128]{1,0:T(8,128)(2,1)S(1)}, bf16[416,128]{1,0:T(8,128)(2,1)S(1)}, u32[]{:S(2)}, u32[]{:S(2)}) collective-permute-start(bf16[416,128]{1,0:T(8,128)(2,1)S(1)} %get-tuple-element.39), channel_id=1, source_target_pairs={{0,12},{4,0},{8,4},{12,8},{1,13},{5,1},{9,5},{13,9},{2,14},{6,2},{... | collective-permute-start | bytes 319496 | tf_op jit(solution)/shard_map/ppermute | solution.py:89
  19.7 0.0 collective-permute-done.9.across_ref
  19.7 0.0 collective-permute-start.10
  19.7 0.0 collective-permute-done.3.block_ref.refs_0_
  19.7 0.0 copy-done.5
  19.7 1.3 %collective-permute-done.10.rest_0_ = bf16[384,128]{1,0:T(8,128)(2,1)S(1)} collective-permute-done((bf16[384,128]{1,0:T(8,128)(2,1)S(1)}, bf16[384,128]{1,0:T(8,128)(2,1)S(1)}, u32[]{:S(2)}, u32[]{:S(2)}) %collective-permute-start.10) | collective-permute-done | bytes 98336 | tf_op jit(solution)/shard_map/ppermute | solution.py:93
  21.0 0.6 %shard_map.77 = (bf16[416,128]{1,0:T(8,128)(2,1)S(1)}, f32[1,384,128]{2,1,0:T(8,128)S(1)}) custom-call(bf16[384,128]{1,0:T(8,128)(2,1)S(1)} %get-tuple-element.40.own_ref, bf16[4,384,128]{2,1,0:T(8,128)(2,1)S(1)} %collective-permute-done.beside_ref, bf16[384,128]{1,0:T(8,128)(2,1)S(1)} %collective-permute-done.9.across_ref, f32[4,128]{1,0:T(4,128)S(1)} %bitcast.8, ...), custom_call_target="tpu_custom_call" | custom-call | tf_op jit(solution)/shard_map/pallas_call | solution.py:97
  21.6 1.9 %collective-permute-done.7.refs_1_ = bf16[416,128]{1,0:T(8,128)(2,1)S(1)} collective-permute-done((bf16[416,128]{1,0:T(8,128)(2,1)S(1)}, bf16[416,128]{1,0:T(8,128)(2,1)S(1)}, u32[]{:S(2)}, u32[]{:S(2)}) %collective-permute-start.7) | collective-permute-done | bytes 106528 | tf_op jit(solution)/shard_map/ppermute | solution.py:89
  23.5 0.6 %collective-permute-done.8.refs_2_ = bf16[416,128]{1,0:T(8,128)(2,1)S(1)} collective-permute-done((bf16[416,128]{1,0:T(8,128)(2,1)S(1)}, bf16[416,128]{1,0:T(8,128)(2,1)S(1)}, u32[]{:S(2)}, u32[]{:S(2)}) %collective-permute-start.8) | collective-permute-done | bytes 106528 | tf_op jit(solution)/shard_map/ppermute | solution.py:89
  24.1 2.1 %shard_map.79 = (bf16[400,128]{1,0:T(8,128)(2,1)S(1)}, bf16[400,128]{1,0:T(8,128)(2,1)S(1)}, bf16[400,128]{1,0:T(8,128)(2,1)S(1)}, bf16[400,128]{1,0:T(8,128)(2,1)S(1)}) custom-call(bf16[416,128]{1,0:T(8,128)(2,1)S(1)} %collective-permute-done.3.block_ref.refs_0_, bf16[416,128]{1,0:T(8,128)(2,1)S(1)} %collective-permute-done.7.refs_1_, ...), custom_call_target="tpu_custom_call" | custom-call | tf_op jit(solution)/shard_map/pallas_call | solution.py:97
  26.2 2.2 %collective-permute-start.13 = (bf16[400,128]{1,0:T(8,128)(2,1)S(1)}, bf16[400,128]{1,0:T(8,128)(2,1)S(1)}, u32[]{:S(2)}, u32[]{:S(2)}) collective-permute-start(bf16[400,128]{1,0:T(8,128)(2,1)S(1)} %get-tuple-element.51), channel_id=1, source_target_pairs={{0,12},{4,0},{8,4},{12,8},{1,13},{5,1},{9,5},{13,9},{2,14},{6,2},{... | collective-permute-start | bytes 307208 | tf_op jit(solution)/shard_map/ppermute | solution.py:89
  28.4 0.0 collective-permute-start.12
  28.4 1.0 %collective-permute-start.11 = (bf16[400,128]{1,0:T(8,128)(2,1)S(1)}, bf16[400,128]{1,0:T(8,128)(2,1)S(1)}, u32[]{:S(2)}, u32[]{:S(2)}) collective-permute-start(bf16[400,128]{1,0:T(8,128)(2,1)S(1)} %get-tuple-element.45), channel_id=1, source_target_pairs={{0,8},{4,12},{8,0},{12,4},{1,9},{5,13},{9,1},{13,5},{2,10},{6,14},... | collective-permute-start | bytes 307208 | tf_op jit(solution)/shard_map/ppermute | solution.py:89
  29.4 0.0 copy-done.1
  29.4 1.9 %collective-permute-start.14 = (bf16[640,128]{1,0:T(8,128)(2,1)S(1)}, bf16[640,128]{1,0:T(8,128)(2,1)S(1)}, u32[]{:S(2)}, u32[]{:S(2)}) collective-permute-start(bf16[640,128]{1,0:T(8,128)(2,1)S(1)} %get-tuple-element.49.refs_0_), channel_id=1, source_target_pairs={{0,2},{1,3},{2,0},{3,1},{4,6},{5,7},{6,4},{7,5},{8,10},{9,11},{10,... | collective-permute-start | bytes 491528 | tf_op jit(solution)/shard_map/ppermute | solution.py:93
  31.4 0.0 collective-permute-start.18
  31.4 0.2 collective-permute-done.13.refs_1_
  31.6 3.2 %collective-permute-done.12.refs_0_ = bf16[400,128]{1,0:T(8,128)(2,1)S(1)} collective-permute-done((bf16[400,128]{1,0:T(8,128)(2,1)S(1)}, bf16[400,128]{1,0:T(8,128)(2,1)S(1)}, u32[]{:S(2)}, u32[]{:S(2)}) %collective-permute-start.12) | collective-permute-done | bytes 102432 | tf_op jit(solution)/shard_map/ppermute | solution.py:89
  34.9 2.9 %collective-permute-start.21 = (bf16[768,128]{1,0:T(8,128)(2,1)S(1)}, bf16[768,128]{1,0:T(8,128)(2,1)S(1)}, u32[]{:S(2)}, u32[]{:S(2)}) collective-permute-start(bf16[768,128]{1,0:T(8,128)(2,1)S(1)} %shard_map.81.refs_4_), channel_id=1, source_target_pairs={{0,2},{1,3},{2,0},{3,1},{4,6},{5,7},{6,4},{7,5},{8,10},{9,11},{10,... | collective-permute-start | bytes 589832 | tf_op jit(solution)/shard_map/ppermute | solution.py:93
  37.8 0.0 collective-permute-start.20
  37.8 0.2 collective-permute-done.11.refs_0_
  38.0 0.0 collective-permute-done.14.refs_2_
  38.0 2.1 %collective-permute-start.16 = (bf16[384,128]{1,0:T(8,128)(2,1)S(1)}, bf16[384,128]{1,0:T(8,128)(2,1)S(1)}, u32[]{:S(2)}, u32[]{:S(2)}) collective-permute-start(bf16[384,128]{1,0:T(8,128)(2,1)S(1)} %shard_map.82.refs_0_), channel_id=1, source_target_pairs={{0,2},{1,3},{2,0},{3,1},{4,6},{5,7},{6,4},{7,5},{8,10},{9,11},{10,... | collective-permute-start | bytes 294920 | tf_op jit(solution)/shard_map/ppermute | solution.py:93
  40.1 2.0 %collective-permute-done.21.refs_6_ = bf16[768,128]{1,0:T(8,128)(2,1)S(1)} collective-permute-done((bf16[768,128]{1,0:T(8,128)(2,1)S(1)}, bf16[768,128]{1,0:T(8,128)(2,1)S(1)}, u32[]{:S(2)}, u32[]{:S(2)}) %collective-permute-start.21) | collective-permute-done | bytes 196640 | tf_op jit(solution)/shard_map/ppermute | solution.py:93
  42.0 0.0 collective-permute-start.22
  42.0 0.5 %collective-permute-start.19 = (bf16[640,128]{1,0:T(8,128)(2,1)S(1)}, bf16[640,128]{1,0:T(8,128)(2,1)S(1)}, u32[]{:S(2)}, u32[]{:S(2)}) collective-permute-start(bf16[640,128]{1,0:T(8,128)(2,1)S(1)} %collective-permute-done.14.refs_2_), channel_id=1, source_target_pairs={{0,1},{1,0},{2,3},{3,2},{4,5},{5,4},{6,7},{7,6},{8,9},{9,8},{10,11... | collective-permute-start | bytes 491528 | tf_op jit(solution)/shard_map/ppermute | solution.py:93
  42.6 1.0 %collective-permute-done.16.refs_2_ = bf16[384,128]{1,0:T(8,128)(2,1)S(1)} collective-permute-done((bf16[384,128]{1,0:T(8,128)(2,1)S(1)}, bf16[384,128]{1,0:T(8,128)(2,1)S(1)}, u32[]{:S(2)}, u32[]{:S(2)}) %collective-permute-start.16) | collective-permute-done | bytes 98336 | tf_op jit(solution)/shard_map/ppermute | solution.py:93
  43.6 0.0 collective-permute-start.15
  43.6 0.0 collective-permute-done.18.refs_1_
  43.6 0.5 %collective-permute-start.17 = (bf16[384,128]{1,0:T(8,128)(2,1)S(1)}, bf16[384,128]{1,0:T(8,128)(2,1)S(1)}, u32[]{:S(2)}, u32[]{:S(2)}) collective-permute-start(bf16[384,128]{1,0:T(8,128)(2,1)S(1)} %collective-permute-done.16.refs_2_), channel_id=1, source_target_pairs={{0,1},{1,0},{2,3},{3,2},{4,5},{5,4},{6,7},{7,6},{8,9},{9,8},{10,11... | collective-permute-start | bytes 294920 | tf_op jit(solution)/shard_map/ppermute | solution.py:93
  44.1 0.0 collective-permute-done.20.refs_5_
  44.1 0.0 collective-permute-done.19.refs_3_
  44.1 0.0 collective-permute-done.22.refs_7_
  44.1 0.5 %shard_map.83 = (bf16[3,384,128]{2,1,0:T(8,128)(2,1)S(1)}, bf16[512,128]{1,0:T(8,128)(2,1)S(1)}) custom-call(bf16[640,128]{1,0:T(8,128)(2,1)S(1)} %get-tuple-element.49.refs_0_, bf16[512,128]{1,0:T(8,128)(2,1)S(1)} %collective-permute-done.18.refs_1_, bf16[640,128]{1,0:T(8,128)(2,1)S(1)} %collective-permute-done.14.refs_2_, ...), custom_call_target="tpu_custom_call" | custom-call | tf_op jit(solution)/shard_map/pallas_call | solution.py:97
  44.6 0.3 collective-permute-done.15.refs_1_
  44.9 0.2 collective-permute-done.17.refs_3_
  45.0 0.9 %shard_map.84 = bf16[4,384,128]{2,1,0:T(8,128)(2,1)} custom-call(bf16[384,128]{1,0:T(8,128)(2,1)S(1)} %shard_map.82.refs_0_, bf16[384,128]{1,0:T(8,128)(2,1)S(1)} %collective-permute-done.15.refs_1_, bf16[384,128]{1,0:T(8,128)(2,1)S(1)} %collective-permute-done.16.refs_2_, bf16[384,128]{1,0:T(8,128)(2,1)S(1)} %collective-permute-done.17.refs_3_, ...), custom_call_target="tpu_custom_call" | custom-call | tf_op jit(solution)/shard_map/pallas_call | solution.py:395
  (9 shorter events, 0.1 us)
Async XLA Ops:
  0.0 1.0 %copy-start.6 = (bf16[4,384,128]{2,1,0:T(8,128)(2,1)S(1)}, bf16[4,384,128]{2,1,0:T(8,128)(2,1)}, u32[]{:S(2)}) copy-start(bf16[4,384,128]{2,1,0:T(8,128)(2,1)} %records_ref.3) | copy-start | bytes 1179652
  0.0 8.8 %copy-start = (bf16[512,3,128]{2,0,1:T(8,128)(2,1)S(1)}, bf16[512,3,128]{2,0,1:T(8,128)(2,1)}, u32[]{:S(2)}) copy-start(bf16[512,3,128]{2,0,1:T(8,128)(2,1)} %param.9) | copy-start | bytes 1179652
  1.0 7.8 %collective-permute-start = (bf16[4,384,128]{2,1,0:T(8,128)(2,1)S(1)}, bf16[4,384,128]{2,1,0:T(8,128)(2,1)S(1)}, u32[]{:S(2)}, u32[]{:S(2)}) collective-permute-start(bf16[4,384,128]{2,1,0:T(8,128)(2,1)S(1)} %copy-done.6), channel_id=1, source_target_pairs={{0,1},{1,0},{2,3},{3,2},{4,5},{5,4},{6,7},{7,6},{8,9},{9,8},{10,11... | collective-permute-start | bytes 1179656 | tf_op jit(solution)/shard_map/ppermute | solution.py:93
  1.5 6.0 %collective-permute-start.1 = (bf16[384,128]{1,0:T(8,128)(2,1)S(1)}, bf16[384,128]{1,0:T(8,128)(2,1)S(1)}, u32[]{:S(2)}, u32[]{:S(2)}) collective-permute-start(bf16[384,128]{1,0:T(8,128)(2,1)S(1)} %shard_map.73.own_ref), channel_id=1, source_target_pairs={{0,2},{1,3},{2,0},{3,1},{4,6},{5,7},{6,4},{7,5},{8,10},{9,11},{10,... | collective-permute-start | bytes 294920 | tf_op jit(solution)/shard_map/ppermute | solution.py:93
  4.1 4.7 %copy-start.2 = (f32[3,3,128]{2,1,0:T(4,128)S(1)}, f32[3,3,128]{2,1,0:T(4,128)}, u32[]{:S(2)}) copy-start(f32[3,3,128]{2,1,0:T(4,128)} %refs_2_.3) | copy-start | bytes 13828
  5.2 3.7 %copy-start.3 = (bf16[4,384]{1,0:T(4,128)(2,1)S(1)}, bf16[4,384]{1,0:T(4,128)(2,1)}, u32[]{:S(2)}) copy-start(bf16[4,384]{1,0:T(4,128)(2,1)} %taps_ref.5) | copy-start | bytes 9220
  5.2 3.7 %copy-start.4 = (f32[512]{0:T(512)S(1)}, f32[512]{0:T(512)}, u32[]{:S(2)}) copy-start(f32[512]{0:T(512)} %param.8) | copy-start | bytes 6148
  5.2 7.2 %collective-permute-start.4 = (bf16[768,128]{1,0:T(8,128)(2,1)S(1)}, bf16[768,128]{1,0:T(8,128)(2,1)S(1)}, u32[]{:S(2)}, u32[]{:S(2)}) collective-permute-start(bf16[768,128]{1,0:T(8,128)(2,1)S(1)} %get-tuple-element.36.own_ref), channel_id=1, source_target_pairs={{0,2},{1,3},{2,0},{3,1},{4,6},{5,7},{6,4},{7,5},{8,10},{9,11},{10,... | collective-permute-start | bytes 589832 | tf_op jit(solution)/shard_map/ppermute | solution.py:93
  7.5 1.3 %collective-permute-start.2 = (bf16[384,128]{1,0:T(8,128)(2,1)S(1)}, bf16[384,128]{1,0:T(8,128)(2,1)S(1)}, u32[]{:S(2)}, u32[]{:S(2)}) collective-permute-start(bf16[384,128]{1,0:T(8,128)(2,1)S(1)} %collective-permute-done.1.across_ref), channel_id=1, source_target_pairs={{0,1},{1,0},{2,3},{3,2},{4,5},{5,4},{6,7},{7,6},{8,9},{9,8},{10,11... | collective-permute-start | bytes 294920 | tf_op jit(solution)/shard_map/ppermute | solution.py:93
  9.4 10.2 %collective-permute-start.3 = (bf16[416,128]{1,0:T(8,128)(2,1)S(1)}, bf16[416,128]{1,0:T(8,128)(2,1)S(1)}, u32[]{:S(2)}, u32[]{:S(2)}) collective-permute-start(bf16[416,128]{1,0:T(8,128)(2,1)S(1)} %get-tuple-element.35), channel_id=1, source_target_pairs={{0,8},{4,12},{8,0},{12,4},{1,9},{5,13},{9,1},{13,5},{2,10},{6,14},... | collective-permute-start | bytes 319496 | tf_op jit(solution)/shard_map/ppermute | solution.py:89
  12.4 2.5 %collective-permute-start.5 = (bf16[384,128]{1,0:T(8,128)(2,1)S(1)}, bf16[384,128]{1,0:T(8,128)(2,1)S(1)}, u32[]{:S(2)}, u32[]{:S(2)}) collective-permute-start(bf16[384,128]{1,0:T(8,128)(2,1)S(1)} %get-tuple-element.64), channel_id=1, source_target_pairs={{0,1},{1,0},{2,3},{3,2},{4,5},{5,4},{6,7},{7,6},{8,9},{9,8},{10,11... | collective-permute-start | bytes 294920 | tf_op jit(solution)/shard_map/ppermute | solution.py:93
  12.5 2.4 %collective-permute-start.6 = (bf16[384,128]{1,0:T(8,128)(2,1)S(1)}, bf16[384,128]{1,0:T(8,128)(2,1)S(1)}, u32[]{:S(2)}, u32[]{:S(2)}) collective-permute-start(bf16[384,128]{1,0:T(8,128)(2,1)S(1)} %get-tuple-element.63), channel_id=1, source_target_pairs={{0,1},{1,0},{2,3},{3,2},{4,5},{5,4},{6,7},{7,6},{8,9},{9,8},{10,11... | collective-permute-start | bytes 294920 | tf_op jit(solution)/shard_map/ppermute | solution.py:93
  13.0 6.7 %collective-permute-start.9 = (bf16[384,128]{1,0:T(8,128)(2,1)S(1)}, bf16[384,128]{1,0:T(8,128)(2,1)S(1)}, u32[]{:S(2)}, u32[]{:S(2)}) collective-permute-start(bf16[384,128]{1,0:T(8,128)(2,1)S(1)} %get-tuple-element.40.own_ref), channel_id=1, source_target_pairs={{0,2},{1,3},{2,0},{3,1},{4,6},{5,7},{6,4},{7,5},{8,10},{9,11},{10,... | collective-permute-start | bytes 294920 | tf_op jit(solution)/shard_map/ppermute | solution.py:93
  15.8 7.7 %collective-permute-start.7 = (bf16[416,128]{1,0:T(8,128)(2,1)S(1)}, bf16[416,128]{1,0:T(8,128)(2,1)S(1)}, u32[]{:S(2)}, u32[]{:S(2)}) collective-permute-start(bf16[416,128]{1,0:T(8,128)(2,1)S(1)} %get-tuple-element.38), channel_id=1, source_target_pairs={{0,4},{4,8},{8,12},{12,0},{1,5},{5,9},{9,13},{13,1},{2,6},{6,10},{... | collective-permute-start | bytes 319496 | tf_op jit(solution)/shard_map/ppermute | solution.py:89
  17.4 2.3 %copy-start.5 = (f32[128]{0:T(128)S(1)}, f32[128]{0:T(128)}, u32[]{:S(2)}) copy-start(f32[128]{0:T(128)} %param.12) | copy-start | bytes 1540
  17.4 6.7 %collective-permute-start.8 = (bf16[416,128]{1,0:T(8,128)(2,1)S(1)}, bf16[416,128]{1,0:T(8,128)(2,1)S(1)}, u32[]{:S(2)}, u32[]{:S(2)}) collective-permute-start(bf16[416,128]{1,0:T(8,128)(2,1)S(1)} %get-tuple-element.39), channel_id=1, source_target_pairs={{0,12},{4,0},{8,4},{12,8},{1,13},{5,1},{9,5},{13,9},{2,14},{6,2},{... | collective-permute-start | bytes 319496 | tf_op jit(solution)/shard_map/ppermute | solution.py:89
  19.7 1.3 %collective-permute-start.10 = (bf16[384,128]{1,0:T(8,128)(2,1)S(1)}, bf16[384,128]{1,0:T(8,128)(2,1)S(1)}, u32[]{:S(2)}, u32[]{:S(2)}) collective-permute-start(bf16[384,128]{1,0:T(8,128)(2,1)S(1)} %collective-permute-done.9.across_ref), channel_id=1, source_target_pairs={{0,1},{1,0},{2,3},{3,2},{4,5},{5,4},{6,7},{7,6},{8,9},{9,8},{10,11... | collective-permute-start | bytes 294920 | tf_op jit(solution)/shard_map/ppermute | solution.py:93
  24.1 5.3 %copy-start.1 = (bf16[128,512]{1,0:T(8,128)(2,1)S(1)}, bf16[128,512]{1,0:T(8,128)(2,1)}, u32[]{:S(2)}) copy-start(bf16[128,512]{1,0:T(8,128)(2,1)} %refs_8_.1) | copy-start | bytes 393220
  26.2 5.4 %collective-permute-start.13 = (bf16[400,128]{1,0:T(8,128)(2,1)S(1)}, bf16[400,128]{1,0:T(8,128)(2,1)S(1)}, u32[]{:S(2)}, u32[]{:S(2)}) collective-permute-start(bf16[400,128]{1,0:T(8,128)(2,1)S(1)} %get-tuple-element.51), channel_id=1, source_target_pairs={{0,12},{4,0},{8,4},{12,8},{1,13},{5,1},{9,5},{13,9},{2,14},{6,2},{... | collective-permute-start | bytes 307208 | tf_op jit(solution)/shard_map/ppermute | solution.py:89
  28.4 6.5 %collective-permute-start.12 = (bf16[400,128]{1,0:T(8,128)(2,1)S(1)}, bf16[400,128]{1,0:T(8,128)(2,1)S(1)}, u32[]{:S(2)}, u32[]{:S(2)}) collective-permute-start(bf16[400,128]{1,0:T(8,128)(2,1)S(1)} %get-tuple-element.46), channel_id=1, source_target_pairs={{0,4},{4,8},{8,12},{12,0},{1,5},{5,9},{9,13},{13,1},{2,6},{6,10},{... | collective-permute-start | bytes 307208 | tf_op jit(solution)/shard_map/ppermute | solution.py:89
  28.4 9.6 %collective-permute-start.11 = (bf16[400,128]{1,0:T(8,128)(2,1)S(1)}, bf16[400,128]{1,0:T(8,128)(2,1)S(1)}, u32[]{:S(2)}, u32[]{:S(2)}) collective-permute-start(bf16[400,128]{1,0:T(8,128)(2,1)S(1)} %get-tuple-element.45), channel_id=1, source_target_pairs={{0,8},{4,12},{8,0},{12,4},{1,9},{5,13},{9,1},{13,5},{2,10},{6,14},... | collective-permute-start | bytes 307208 | tf_op jit(solution)/shard_map/ppermute | solution.py:89
  29.4 8.6 %collective-permute-start.14 = (bf16[640,128]{1,0:T(8,128)(2,1)S(1)}, bf16[640,128]{1,0:T(8,128)(2,1)S(1)}, u32[]{:S(2)}, u32[]{:S(2)}) collective-permute-start(bf16[640,128]{1,0:T(8,128)(2,1)S(1)} %get-tuple-element.49.refs_0_), channel_id=1, source_target_pairs={{0,2},{1,3},{2,0},{3,1},{4,6},{5,7},{6,4},{7,5},{8,10},{9,11},{10,... | collective-permute-start | bytes 491528 | tf_op jit(solution)/shard_map/ppermute | solution.py:93
  31.4 12.2 %collective-permute-start.18 = (bf16[512,128]{1,0:T(8,128)(2,1)S(1)}, bf16[512,128]{1,0:T(8,128)(2,1)S(1)}, u32[]{:S(2)}, u32[]{:S(2)}) collective-permute-start(bf16[512,128]{1,0:T(8,128)(2,1)S(1)} %get-tuple-element.58), channel_id=1, source_target_pairs={{0,1},{1,0},{2,3},{3,2},{4,5},{5,4},{6,7},{7,6},{8,9},{9,8},{10,11... | collective-permute-start | bytes 393224 | tf_op jit(solution)/shard_map/ppermute | solution.py:93
  34.9 7.2 %collective-permute-start.21 = (bf16[768,128]{1,0:T(8,128)(2,1)S(1)}, bf16[768,128]{1,0:T(8,128)(2,1)S(1)}, u32[]{:S(2)}, u32[]{:S(2)}) collective-permute-start(bf16[768,128]{1,0:T(8,128)(2,1)S(1)} %shard_map.81.refs_4_), channel_id=1, source_target_pairs={{0,2},{1,3},{2,0},{3,1},{4,6},{5,7},{6,4},{7,5},{8,10},{9,11},{10,... | collective-permute-start | bytes 589832 | tf_op jit(solution)/shard_map/ppermute | solution.py:93
  37.8 6.3 %collective-permute-start.20 = (bf16[768,128]{1,0:T(8,128)(2,1)S(1)}, bf16[768,128]{1,0:T(8,128)(2,1)S(1)}, u32[]{:S(2)}, u32[]{:S(2)}) collective-permute-start(bf16[768,128]{1,0:T(8,128)(2,1)S(1)} %shard_map.81.refs_4_), channel_id=1, source_target_pairs={{0,1},{1,0},{2,3},{3,2},{4,5},{5,4},{6,7},{7,6},{8,9},{9,8},{10,11... | collective-permute-start | bytes 589832 | tf_op jit(solution)/shard_map/ppermute | solution.py:93
  38.0 5.5 %collective-permute-start.16 = (bf16[384,128]{1,0:T(8,128)(2,1)S(1)}, bf16[384,128]{1,0:T(8,128)(2,1)S(1)}, u32[]{:S(2)}, u32[]{:S(2)}) collective-permute-start(bf16[384,128]{1,0:T(8,128)(2,1)S(1)} %shard_map.82.refs_0_), channel_id=1, source_target_pairs={{0,2},{1,3},{2,0},{3,1},{4,6},{5,7},{6,4},{7,5},{8,10},{9,11},{10,... | collective-permute-start | bytes 294920 | tf_op jit(solution)/shard_map/ppermute | solution.py:93
  42.0 2.0 %collective-permute-start.22 = (bf16[768,128]{1,0:T(8,128)(2,1)S(1)}, bf16[768,128]{1,0:T(8,128)(2,1)S(1)}, u32[]{:S(2)}, u32[]{:S(2)}) collective-permute-start(bf16[768,128]{1,0:T(8,128)(2,1)S(1)} %collective-permute-done.21.refs_6_), channel_id=1, source_target_pairs={{0,1},{1,0},{2,3},{3,2},{4,5},{5,4},{6,7},{7,6},{8,9},{9,8},{10,11... | collective-permute-start | bytes 589832 | tf_op jit(solution)/shard_map/ppermute | solution.py:93
  42.0 2.0 %collective-permute-start.19 = (bf16[640,128]{1,0:T(8,128)(2,1)S(1)}, bf16[640,128]{1,0:T(8,128)(2,1)S(1)}, u32[]{:S(2)}, u32[]{:S(2)}) collective-permute-start(bf16[640,128]{1,0:T(8,128)(2,1)S(1)} %collective-permute-done.14.refs_2_), channel_id=1, source_target_pairs={{0,1},{1,0},{2,3},{3,2},{4,5},{5,4},{6,7},{7,6},{8,9},{9,8},{10,11... | collective-permute-start | bytes 491528 | tf_op jit(solution)/shard_map/ppermute | solution.py:93
  43.6 1.3 %collective-permute-start.15 = (bf16[384,128]{1,0:T(8,128)(2,1)S(1)}, bf16[384,128]{1,0:T(8,128)(2,1)S(1)}, u32[]{:S(2)}, u32[]{:S(2)}) collective-permute-start(bf16[384,128]{1,0:T(8,128)(2,1)S(1)} %shard_map.82.refs_0_), channel_id=1, source_target_pairs={{0,1},{1,0},{2,3},{3,2},{4,5},{5,4},{6,7},{7,6},{8,9},{9,8},{10,11... | collective-permute-start | bytes 294920 | tf_op jit(solution)/shard_map/ppermute | solution.py:93
  43.6 1.5 %collective-permute-start.17 = (bf16[384,128]{1,0:T(8,128)(2,1)S(1)}, bf16[384,128]{1,0:T(8,128)(2,1)S(1)}, u32[]{:S(2)}, u32[]{:S(2)}) collective-permute-start(bf16[384,128]{1,0:T(8,128)(2,1)S(1)} %collective-permute-done.16.refs_2_), channel_id=1, source_target_pairs={{0,1},{1,0},{2,3},{3,2},{4,5},{5,4},{6,7},{7,6},{8,9},{9,8},{10,11... | collective-permute-start | bytes 294920 | tf_op jit(solution)/shard_map/ppermute | solution.py:93

commit v7 on v6

--- a/solution.py
+++ b/solution.py
@@ -109,12 +109,24 @@
     return lax.optimization_barrier((value, *done))[0]
 
 
-def pick(records, groups):
+def reversed_rows(taps):
+    row = lax.broadcasted_iota(jnp.int32, (LANES, LANES), 0)
+    column = lax.broadcasted_iota(jnp.int32, (LANES, LANES), 1)
+    flip = (row + column == LANES - 1).astype(taps.dtype)
+    return [
+        jnp.dot(taps[:, b * LANES : (b + 1) * LANES], flip, preferred_element_type=jnp.float32)
+        for b in range(taps.shape[1] // LANES)
+    ]
+
+
+def pick(records, groups, taps=None):
     count, block_len, _ = records.shape
-    flat = [len(group) * block_len for group in groups]
+    with_taps = taps is not None
 
     def kernel(records_ref, *rest):
-        out_refs, sems = rest[:-1], rest[-1]
+        taps_ref, rest = (rest[0], rest[1:]) if with_taps else (None, rest)
+        out_refs, rest = rest[: len(groups)], rest[len(groups) :]
+        sems = rest[-1]
         z = lax.axis_index("seq")
         copies = []
         for ref, group in zip(out_refs, groups):
@@ -125,18 +137,30 @@
                 )
         for copy in copies:
             copy.start()
+        if with_taps:
+            rows_ref, held = rest[0], rest[1]
+            fetch = pltpu.make_async_copy(taps_ref, held, sems.at[len(copies)])
+            fetch.start()
+            fetch.wait()
+            rows_ref[...] = jnp.concatenate(reversed_rows(held[...]), axis=0)
         for copy in copies:
             copy.wait()
 
-    shapes = [VMEM((n, LANES), records.dtype) for n in flat]
+    shapes = [VMEM((len(group) * block_len, LANES), records.dtype) for group in groups]
+    scratch = [pltpu.SemaphoreType.DMA((count + 1,))]
+    operands = [records]
+    if with_taps:
+        shapes.append(VMEM((taps.size // LANES, LANES), jnp.float32))
+        scratch.insert(0, pltpu.VMEM(taps.shape, taps.dtype))
+        operands.append(taps)
     return pl.pallas_call(
         kernel,
         out_shape=tuple(shapes),
-        in_specs=[pl.BlockSpec(memory_space=pl.ANY)],
+        in_specs=[pl.BlockSpec(memory_space=pl.ANY)] * len(operands),
         out_specs=tuple(pl.BlockSpec(memory_space=VMEM) for _ in shapes),
-        scratch_shapes=[pltpu.SemaphoreType.DMA((count,))],
+        scratch_shapes=scratch,
         cost_estimate=NO_COST,
-    )(records)
+    )(*operands)
 
 
 def project(own, beside, across, diagonal, norm_gain, weights, short_kernel, taps, offsets):
@@ -156,16 +180,7 @@
             for s in range(3):
                 w_all[j * LANES : (j + 1) * LANES, s * LANES : (s + 1) * LANES] = w_ref[s, pl.ds(first, LANES), :]
         shifted[0:8, :] = jnp.zeros((8, 3 * LANES), f32)
-        taps_block = taps_ref[...]
-        flip = (
-            lax.broadcasted_iota(jnp.int32, (LANES, LANES), 0)
-            + lax.broadcasted_iota(jnp.int32, (LANES, LANES), 1)
-            == LANES - 1
-        ).astype(bf16)
-        tap_rows = [
-            jnp.dot(taps_block[:, b * LANES : (b + 1) * LANES], flip, preferred_element_type=f32)
-            for b in range(block_len // LANES)
-        ]
+        tap_rows = [taps_ref[...]]
         for i, k in enumerate(offsets):
             rec = lax.rem(z + k, count)
             rows = slice(i * block_len, (i + 1) * block_len)
@@ -410,9 +425,9 @@
     skip = skip_gain.reshape(1, LANES)
 
     (first,) = pick(records, ((2,),))
-    second, third = pick(records, ((1, 3), (0,)))
+    second, third, long_filter = pick(records, ((1, 3), (0,)), long_filter)
     across_first, across_second, across_third = (exchange(block, "chan", 2) for block in (first, second, third))
-    beside = exchange(after(records, first), "chan", 1)
+    beside = exchange(records, "chan", 1)
 
     def projected(offsets, own, far, pieces):
         size = far.shape[0] // pieces
@@ -439,7 +454,6 @@
     (near,) = gate([after(sums_one, own), after(sums_three, own)], [(query_near, 1), (query_near, 0)], short_kernel)
     near_over = exchange(near, "chan", 2)
     (far,) = gate([after(sums_two, near)], [(query_two, 0)], short_kernel, cost=FAR_COST)
-    far = after(far, own_over)
     far_over = exchange(far, "chan", 2)
 
     def slab(gated, beside, over):

time: 46.1 us -> 46 us (level)
  transfers between devices with their start and end apart: 23 -> 23, of which waited for: 12 -> 12; matrix products, arithmetic and copies ran while one was open for 0% -> 0% of each run, Pallas kernels for 8% -> 10%
where the time goes in v7:
time: 46 us; the launch traced here: 45.9 us
  starting transfers between devices  23.5 us (51%)
  waiting for transfers between devices  14.4 us (31%)
  Pallas kernels  7.75 us (17%)
    ppermute x17, starting transfers between devices, exchange(): lax.ppermute(block, axis, [(i, i ^ mask) for i in range(lax.axis_size(axi...  13.5 us
    ppermute x6, starting transfers between devices, rotate(): lax.ppermute(block, axis, [(i, (i + distance) % n) for i in range(n)])  9.97 us
    ppermute x17, waiting for transfers between devices, exchange(): lax.ppermute(block, axis, [(i, i ^ mask) for i in range(lax.axis_size(axi...  8.25 us
    ppermute x6, waiting for transfers between devices, rotate(): lax.ppermute(block, axis, [(i, (i + distance) % n) for i in range(n)])  6.18 us
    pallas_call x9, Pallas kernels, vmem_call(): pl.pallas_call(kernel, out_shape=tuple(outs), in_specs=[pl.BlockSpec(memo...  4.83 us
    pallas_call x2, Pallas kernels, pick(): pl.pallas_call(kernel, out_shape=tuple(shapes), in_specs=[pl.BlockSpec(me...  1.98 us
    pallas_call x1, Pallas kernels, mix_last(): pl.pallas_call(kernel, out_shape=jax.ShapeDtypeStruct((count, block_len,...  0.94 us
  transfers between devices with their start and end apart: 23, of which 12 were waited for; matrix products, arithmetic and copies ran while one was open for 0% of the time, Pallas kernels for 10%

profile of v7, /device:TPU:0, one launch (start us, length us, event | category | flops | bytes accessed | tf_op | source)
XLA Modules:
  0.0 45.9 jit_solution(10284506708657936046)
XLA Ops:
  0.0 0.0 copy-start
  0.0 0.5 collective-permute-start
  0.5 0.9 %shard_map.73.own_ref = bf16[384,128]{1,0:T(8,128)(2,1)S(1)} custom-call(bf16[4,384,128]{2,1,0:T(8,128)(2,1)} %records_ref.3), custom_call_target="tpu_custom_call" | custom-call | tf_op jit(solution)/shard_map/pallas_call | solution.py:156
  1.4 2.6 %collective-permute-start.1 = (bf16[384,128]{1,0:T(8,128)(2,1)S(1)}, bf16[384,128]{1,0:T(8,128)(2,1)S(1)}, u32[]{:S(2)}, u32[]{:S(2)}) collective-permute-start(bf16[384,128]{1,0:T(8,128)(2,1)S(1)} %shard_map.73.own_ref), channel_id=1, source_target_pairs={{0,2},{1,3},{2,0},{3,1},{4,6},{5,7},{6,4},{7,5},{8,10},{9,11},{10,... | collective-permute-start | bytes 294920 | tf_op jit(solution)/shard_map/ppermute | solution.py:93
  4.0 0.0 copy-start.3
  4.0 1.0 %shard_map.74 = (bf16[768,128]{1,0:T(8,128)(2,1)S(1)}, bf16[384,128]{1,0:T(8,128)(2,1)S(1)}, f32[12,128]{1,0:T(8,128)S(1)}) custom-call(bf16[4,384,128]{2,1,0:T(8,128)(2,1)} %records_ref.3, bf16[4,384]{1,0:T(4,128)(2,1)} %rest_0_.1), custom_call_target="tpu_custom_call" | custom-call | tf_op jit(solution)/shard_map/pallas_call | solution.py:156
  5.1 0.0 copy-start.2
  5.1 0.1 collective-permute-start.4
  5.2 2.3 %collective-permute-done.1.across_ref = bf16[384,128]{1,0:T(8,128)(2,1)S(1)} collective-permute-done((bf16[384,128]{1,0:T(8,128)(2,1)S(1)}, bf16[384,128]{1,0:T(8,128)(2,1)S(1)}, u32[]{:S(2)}, u32[]{:S(2)}) %collective-permute-start.1) | collective-permute-done | bytes 98336 | tf_op jit(solution)/shard_map/ppermute | solution.py:93
  7.4 0.0 collective-permute-start.2
  7.4 1.3 %collective-permute-done.2.rest_0_ = bf16[384,128]{1,0:T(8,128)(2,1)S(1)} collective-permute-done((bf16[384,128]{1,0:T(8,128)(2,1)S(1)}, bf16[384,128]{1,0:T(8,128)(2,1)S(1)}, u32[]{:S(2)}, u32[]{:S(2)}) %collective-permute-start.2) | collective-permute-done | bytes 98336 | tf_op jit(solution)/shard_map/ppermute | solution.py:93
  8.7 0.0 collective-permute-done.beside_ref
  8.7 0.0 copy-done
  8.7 0.0 copy-done.3
  8.7 0.0 copy-done.2
  8.7 0.6 %shard_map.75 = (bf16[416,128]{1,0:T(8,128)(2,1)S(1)}, f32[1,384,128]{2,1,0:T(8,128)S(1)}) custom-call(bf16[384,128]{1,0:T(8,128)(2,1)S(1)} %shard_map.73.own_ref, bf16[4,384,128]{2,1,0:T(8,128)(2,1)S(1)} %collective-permute-done.beside_ref, bf16[384,128]{1,0:T(8,128)(2,1)S(1)} %collective-permute-done.1.across_ref, f32[4,128]{1,0:T(4,128)S(1)} %bitcast.6, ...), custom_call_target="tpu_custom_call" | custom-call | tf_op jit(solution)/shard_map/pallas_call | solution.py:97
  9.4 2.9 %collective-permute-start.3 = (bf16[416,128]{1,0:T(8,128)(2,1)S(1)}, bf16[416,128]{1,0:T(8,128)(2,1)S(1)}, u32[]{:S(2)}, u32[]{:S(2)}) collective-permute-start(bf16[416,128]{1,0:T(8,128)(2,1)S(1)} %get-tuple-element.34), channel_id=1, source_target_pairs={{0,8},{4,12},{8,0},{12,4},{1,9},{5,13},{9,1},{13,5},{2,10},{6,14},... | collective-permute-start | bytes 319496 | tf_op jit(solution)/shard_map/ppermute | solution.py:89
  12.3 0.0 collective-permute-done.4.across_ref
  12.3 0.1 collective-permute-start.5
  12.4 0.5 %collective-permute-start.6 = (bf16[384,128]{1,0:T(8,128)(2,1)S(1)}, bf16[384,128]{1,0:T(8,128)(2,1)S(1)}, u32[]{:S(2)}, u32[]{:S(2)}) collective-permute-start(bf16[384,128]{1,0:T(8,128)(2,1)S(1)} %get-tuple-element.61), channel_id=1, source_target_pairs={{0,1},{1,0},{2,3},{3,2},{4,5},{5,4},{6,7},{7,6},{8,9},{9,8},{10,11... | collective-permute-start | bytes 294920 | tf_op jit(solution)/shard_map/ppermute | solution.py:93
  12.9 1.9 %collective-permute-start.9 = (bf16[384,128]{1,0:T(8,128)(2,1)S(1)}, bf16[384,128]{1,0:T(8,128)(2,1)S(1)}, u32[]{:S(2)}, u32[]{:S(2)}) collective-permute-start(bf16[384,128]{1,0:T(8,128)(2,1)S(1)} %get-tuple-element.39.own_ref), channel_id=1, source_target_pairs={{0,2},{1,3},{2,0},{3,1},{4,6},{5,7},{6,4},{7,5},{8,10},{9,11},{10,... | collective-permute-start | bytes 294920 | tf_op jit(solution)/shard_map/ppermute | solution.py:93
  14.8 0.0 collective-permute-done.5.rest_0_
  14.8 0.0 collective-permute-done.6.rest_1_
  14.8 0.9 %shard_map.76 = (bf16[416,128]{1,0:T(8,128)(2,1)S(1)}, bf16[416,128]{1,0:T(8,128)(2,1)S(1)}, f32[2,384,128]{2,1,0:T(8,128)S(1)}) custom-call(bf16[768,128]{1,0:T(8,128)(2,1)S(1)} %get-tuple-element.35.own_ref, bf16[4,384,128]{2,1,0:T(8,128)(2,1)S(1)} %collective-permute-done.beside_ref, bf16[768,128]{1,0:T(8,128)(2,1)S(1)} %collective-permute-done.4.across_ref, ...), custom_call_target="tpu_custom_call" | custom-call | tf_op jit(solution)/shard_map/pallas_call | solution.py:97
  15.7 1.6 %collective-permute-start.7 = (bf16[416,128]{1,0:T(8,128)(2,1)S(1)}, bf16[416,128]{1,0:T(8,128)(2,1)S(1)}, u32[]{:S(2)}, u32[]{:S(2)}) collective-permute-start(bf16[416,128]{1,0:T(8,128)(2,1)S(1)} %get-tuple-element.37), channel_id=1, source_target_pairs={{0,4},{4,8},{8,12},{12,0},{1,5},{5,9},{9,13},{13,1},{2,6},{6,10},{... | collective-permute-start | bytes 319496 | tf_op jit(solution)/shard_map/ppermute | solution.py:89
  17.4 0.0 copy-start.4
  17.4 2.2 %collective-permute-start.8 = (bf16[416,128]{1,0:T(8,128)(2,1)S(1)}, bf16[416,128]{1,0:T(8,128)(2,1)S(1)}, u32[]{:S(2)}, u32[]{:S(2)}) collective-permute-start(bf16[416,128]{1,0:T(8,128)(2,1)S(1)} %get-tuple-element.38), channel_id=1, source_target_pairs={{0,12},{4,0},{8,4},{12,8},{1,13},{5,1},{9,5},{13,9},{2,14},{6,2},{... | collective-permute-start | bytes 319496 | tf_op jit(solution)/shard_map/ppermute | solution.py:89
  19.6 0.0 collective-permute-done.9.across_ref
  19.6 0.0 collective-permute-start.10
  19.6 0.0 collective-permute-done.3.block_ref.refs_0_
  19.6 0.0 copy-done.4
  19.6 1.3 %collective-permute-done.10.rest_0_ = bf16[384,128]{1,0:T(8,128)(2,1)S(1)} collective-permute-done((bf16[384,128]{1,0:T(8,128)(2,1)S(1)}, bf16[384,128]{1,0:T(8,128)(2,1)S(1)}, u32[]{:S(2)}, u32[]{:S(2)}) %collective-permute-start.10) | collective-permute-done | bytes 98336 | tf_op jit(solution)/shard_map/ppermute | solution.py:93
  20.9 0.6 %shard_map.77 = (bf16[416,128]{1,0:T(8,128)(2,1)S(1)}, f32[1,384,128]{2,1,0:T(8,128)S(1)}) custom-call(bf16[384,128]{1,0:T(8,128)(2,1)S(1)} %get-tuple-element.39.own_ref, bf16[4,384,128]{2,1,0:T(8,128)(2,1)S(1)} %collective-permute-done.beside_ref, bf16[384,128]{1,0:T(8,128)(2,1)S(1)} %collective-permute-done.9.across_ref, f32[4,128]{1,0:T(4,128)S(1)} %bitcast.8, ...), custom_call_target="tpu_custom_call" | custom-call | tf_op jit(solution)/shard_map/pallas_call | solution.py:97
  21.5 1.9 %collective-permute-done.7.refs_1_ = bf16[416,128]{1,0:T(8,128)(2,1)S(1)} collective-permute-done((bf16[416,128]{1,0:T(8,128)(2,1)S(1)}, bf16[416,128]{1,0:T(8,128)(2,1)S(1)}, u32[]{:S(2)}, u32[]{:S(2)}) %collective-permute-start.7) | collective-permute-done | bytes 106528 | tf_op jit(solution)/shard_map/ppermute | solution.py:89
  23.5 0.6 %collective-permute-done.8.refs_2_ = bf16[416,128]{1,0:T(8,128)(2,1)S(1)} collective-permute-done((bf16[416,128]{1,0:T(8,128)(2,1)S(1)}, bf16[416,128]{1,0:T(8,128)(2,1)S(1)}, u32[]{:S(2)}, u32[]{:S(2)}) %collective-permute-start.8) | collective-permute-done | bytes 106528 | tf_op jit(solution)/shard_map/ppermute | solution.py:89
  24.0 0.0 copy-start.1
  24.0 2.1 %shard_map.79 = (bf16[400,128]{1,0:T(8,128)(2,1)S(1)}, bf16[400,128]{1,0:T(8,128)(2,1)S(1)}, bf16[400,128]{1,0:T(8,128)(2,1)S(1)}, bf16[400,128]{1,0:T(8,128)(2,1)S(1)}) custom-call(bf16[416,128]{1,0:T(8,128)(2,1)S(1)} %collective-permute-done.3.block_ref.refs_0_, bf16[416,128]{1,0:T(8,128)(2,1)S(1)} %collective-permute-done.7.refs_1_, ...), custom_call_target="tpu_custom_call" | custom-call | tf_op jit(solution)/shard_map/pallas_call | solution.py:97
  26.1 2.2 %collective-permute-start.13 = (bf16[400,128]{1,0:T(8,128)(2,1)S(1)}, bf16[400,128]{1,0:T(8,128)(2,1)S(1)}, u32[]{:S(2)}, u32[]{:S(2)}) collective-permute-start(bf16[400,128]{1,0:T(8,128)(2,1)S(1)} %get-tuple-element.50), channel_id=1, source_target_pairs={{0,12},{4,0},{8,4},{12,8},{1,13},{5,1},{9,5},{13,9},{2,14},{6,2},{... | collective-permute-start | bytes 307208 | tf_op jit(solution)/shard_map/ppermute | solution.py:89
  28.3 0.0 collective-permute-start.12
  28.3 1.0 %collective-permute-start.11 = (bf16[400,128]{1,0:T(8,128)(2,1)S(1)}, bf16[400,128]{1,0:T(8,128)(2,1)S(1)}, u32[]{:S(2)}, u32[]{:S(2)}) collective-permute-start(bf16[400,128]{1,0:T(8,128)(2,1)S(1)} %get-tuple-element.44), channel_id=1, source_target_pairs={{0,8},{4,12},{8,0},{12,4},{1,9},{5,13},{9,1},{13,5},{2,10},{6,14},... | collective-permute-start | bytes 307208 | tf_op jit(solution)/shard_map/ppermute | solution.py:89
  29.3 0.0 copy-done.1
  29.4 1.9 %collective-permute-start.18 = (bf16[640,128]{1,0:T(8,128)(2,1)S(1)}, bf16[640,128]{1,0:T(8,128)(2,1)S(1)}, u32[]{:S(2)}, u32[]{:S(2)}) collective-permute-start(bf16[640,128]{1,0:T(8,128)(2,1)S(1)} %get-tuple-element.48.refs_0_), channel_id=1, source_target_pairs={{0,2},{1,3},{2,0},{3,1},{4,6},{5,7},{6,4},{7,5},{8,10},{9,11},{10,... | collective-permute-start | bytes 491528 | tf_op jit(solution)/shard_map/ppermute | solution.py:93
  31.3 0.0 collective-permute-start.17
  31.3 0.2 collective-permute-done.13.refs_1_
  31.5 3.2 %collective-permute-done.12.refs_0_ = bf16[400,128]{1,0:T(8,128)(2,1)S(1)} collective-permute-done((bf16[400,128]{1,0:T(8,128)(2,1)S(1)}, bf16[400,128]{1,0:T(8,128)(2,1)S(1)}, u32[]{:S(2)}, u32[]{:S(2)}) %collective-permute-start.12) | collective-permute-done | bytes 102432 | tf_op jit(solution)/shard_map/ppermute | solution.py:89
  34.8 2.9 %collective-permute-start.21 = (bf16[768,128]{1,0:T(8,128)(2,1)S(1)}, bf16[768,128]{1,0:T(8,128)(2,1)S(1)}, u32[]{:S(2)}, u32[]{:S(2)}) collective-permute-start(bf16[768,128]{1,0:T(8,128)(2,1)S(1)} %shard_map.81.refs_4_), channel_id=1, source_target_pairs={{0,2},{1,3},{2,0},{3,1},{4,6},{5,7},{6,4},{7,5},{8,10},{9,11},{10,... | collective-permute-start | bytes 589832 | tf_op jit(solution)/shard_map/ppermute | solution.py:93
  37.7 0.0 collective-permute-start.20
  37.7 0.2 collective-permute-done.11.refs_0_
  37.9 2.1 %collective-permute-start.15 = (bf16[384,128]{1,0:T(8,128)(2,1)S(1)}, bf16[384,128]{1,0:T(8,128)(2,1)S(1)}, u32[]{:S(2)}, u32[]{:S(2)}) collective-permute-start(bf16[384,128]{1,0:T(8,128)(2,1)S(1)} %shard_map.82.refs_0_), channel_id=1, source_target_pairs={{0,2},{1,3},{2,0},{3,1},{4,6},{5,7},{6,4},{7,5},{8,10},{9,11},{10,... | collective-permute-start | bytes 294920 | tf_op jit(solution)/shard_map/ppermute | solution.py:93
  40.0 2.0 %collective-permute-done.21.refs_6_ = bf16[768,128]{1,0:T(8,128)(2,1)S(1)} collective-permute-done((bf16[768,128]{1,0:T(8,128)(2,1)S(1)}, bf16[768,128]{1,0:T(8,128)(2,1)S(1)}, u32[]{:S(2)}, u32[]{:S(2)}) %collective-permute-start.21) | collective-permute-done | bytes 196640 | tf_op jit(solution)/shard_map/ppermute | solution.py:93
  41.9 0.0 collective-permute-start.22
  42.0 0.0 collective-permute-done.18.refs_2_
  42.0 0.5 %collective-permute-start.19 = (bf16[640,128]{1,0:T(8,128)(2,1)S(1)}, bf16[640,128]{1,0:T(8,128)(2,1)S(1)}, u32[]{:S(2)}, u32[]{:S(2)}) collective-permute-start(bf16[640,128]{1,0:T(8,128)(2,1)S(1)} %collective-permute-done.18.refs_2_), channel_id=1, source_target_pairs={{0,1},{1,0},{2,3},{3,2},{4,5},{5,4},{6,7},{7,6},{8,9},{9,8},{10,11... | collective-permute-start | bytes 491528 | tf_op jit(solution)/shard_map/ppermute | solution.py:93
  42.5 1.0 %collective-permute-done.15.refs_2_ = bf16[384,128]{1,0:T(8,128)(2,1)S(1)} collective-permute-done((bf16[384,128]{1,0:T(8,128)(2,1)S(1)}, bf16[384,128]{1,0:T(8,128)(2,1)S(1)}, u32[]{:S(2)}, u32[]{:S(2)}) %collective-permute-start.15) | collective-permute-done | bytes 98336 | tf_op jit(solution)/shard_map/ppermute | solution.py:93
  43.5 0.0 collective-permute-start.14
  43.5 0.0 collective-permute-done.17.refs_1_
  43.5 0.5 %collective-permute-start.16 = (bf16[384,128]{1,0:T(8,128)(2,1)S(1)}, bf16[384,128]{1,0:T(8,128)(2,1)S(1)}, u32[]{:S(2)}, u32[]{:S(2)}) collective-permute-start(bf16[384,128]{1,0:T(8,128)(2,1)S(1)} %collective-permute-done.15.refs_2_), channel_id=1, source_target_pairs={{0,1},{1,0},{2,3},{3,2},{4,5},{5,4},{6,7},{7,6},{8,9},{9,8},{10,11... | collective-permute-start | bytes 294920 | tf_op jit(solution)/shard_map/ppermute | solution.py:93
  44.0 0.0 collective-permute-done.20.refs_5_
  44.0 0.0 collective-permute-done.19.refs_3_
  44.0 0.0 collective-permute-done.22.refs_7_
  44.0 0.5 %shard_map.83 = (bf16[3,384,128]{2,1,0:T(8,128)(2,1)S(1)}, bf16[512,128]{1,0:T(8,128)(2,1)S(1)}) custom-call(bf16[640,128]{1,0:T(8,128)(2,1)S(1)} %get-tuple-element.48.refs_0_, bf16[512,128]{1,0:T(8,128)(2,1)S(1)} %collective-permute-done.17.refs_1_, bf16[640,128]{1,0:T(8,128)(2,1)S(1)} %collective-permute-done.18.refs_2_, ...), custom_call_target="tpu_custom_call" | custom-call | tf_op jit(solution)/shard_map/pallas_call | solution.py:97
  44.5 0.3 collective-permute-done.14.refs_1_
  44.8 0.2 collective-permute-done.16.refs_3_
  44.9 0.9 %shard_map.84 = bf16[4,384,128]{2,1,0:T(8,128)(2,1)} custom-call(bf16[384,128]{1,0:T(8,128)(2,1)S(1)} %shard_map.82.refs_0_, bf16[384,128]{1,0:T(8,128)(2,1)S(1)} %collective-permute-done.14.refs_1_, bf16[384,128]{1,0:T(8,128)(2,1)S(1)} %collective-permute-done.15.refs_2_, bf16[384,128]{1,0:T(8,128)(2,1)S(1)} %collective-permute-done.16.refs_3_, ...), custom_call_target="tpu_custom_call" | custom-call | tf_op jit(solution)/shard_map/pallas_call | solution.py:410
  (5 shorter events, 0.1 us)
Async XLA Ops:
  0.0 8.7 %copy-start = (bf16[512,3,128]{2,0,1:T(8,128)(2,1)S(1)}, bf16[512,3,128]{2,0,1:T(8,128)(2,1)}, u32[]{:S(2)}) copy-start(bf16[512,3,128]{2,0,1:T(8,128)(2,1)} %param.9) | copy-start | bytes 1179652
  0.0 8.7 %collective-permute-start = (bf16[4,384,128]{2,1,0:T(8,128)(2,1)}, bf16[4,384,128]{2,1,0:T(8,128)(2,1)S(1)}, u32[]{:S(2)}, u32[]{:S(2)}) collective-permute-start(bf16[4,384,128]{2,1,0:T(8,128)(2,1)} %records_ref.3), channel_id=1, source_target_pairs={{0,1},{1,0},{2,3},{3,2},{4,5},{5,4},{6,7},{7,6},{8,9},{9,8},{10,11... | collective-permute-start | bytes 1179656 | tf_op jit(solution)/shard_map/ppermute | solution.py:93
  1.4 6.0 %collective-permute-start.1 = (bf16[384,128]{1,0:T(8,128)(2,1)S(1)}, bf16[384,128]{1,0:T(8,128)(2,1)S(1)}, u32[]{:S(2)}, u32[]{:S(2)}) collective-permute-start(bf16[384,128]{1,0:T(8,128)(2,1)S(1)} %shard_map.73.own_ref), channel_id=1, source_target_pairs={{0,2},{1,3},{2,0},{3,1},{4,6},{5,7},{6,4},{7,5},{8,10},{9,11},{10,... | collective-permute-start | bytes 294920 | tf_op jit(solution)/shard_map/ppermute | solution.py:93
  4.0 4.7 %copy-start.3 = (f32[512]{0:T(512)S(1)}, f32[512]{0:T(512)}, u32[]{:S(2)}) copy-start(f32[512]{0:T(512)} %param.8) | copy-start | bytes 6148
  5.1 3.7 %copy-start.2 = (f32[3,3,128]{2,1,0:T(4,128)S(1)}, f32[3,3,128]{2,1,0:T(4,128)}, u32[]{:S(2)}) copy-start(f32[3,3,128]{2,1,0:T(4,128)} %refs_2_.3) | copy-start | bytes 13828
  5.1 7.2 %collective-permute-start.4 = (bf16[768,128]{1,0:T(8,128)(2,1)S(1)}, bf16[768,128]{1,0:T(8,128)(2,1)S(1)}, u32[]{:S(2)}, u32[]{:S(2)}) collective-permute-start(bf16[768,128]{1,0:T(8,128)(2,1)S(1)} %get-tuple-element.35.own_ref), channel_id=1, source_target_pairs={{0,2},{1,3},{2,0},{3,1},{4,6},{5,7},{6,4},{7,5},{8,10},{9,11},{10,... | collective-permute-start | bytes 589832 | tf_op jit(solution)/shard_map/ppermute | solution.py:93
  7.4 1.3 %collective-permute-start.2 = (bf16[384,128]{1,0:T(8,128)(2,1)S(1)}, bf16[384,128]{1,0:T(8,128)(2,1)S(1)}, u32[]{:S(2)}, u32[]{:S(2)}) collective-permute-start(bf16[384,128]{1,0:T(8,128)(2,1)S(1)} %collective-permute-done.1.across_ref), channel_id=1, source_target_pairs={{0,1},{1,0},{2,3},{3,2},{4,5},{5,4},{6,7},{7,6},{8,9},{9,8},{10,11... | collective-permute-start | bytes 294920 | tf_op jit(solution)/shard_map/ppermute | solution.py:93
  9.4 10.2 %collective-permute-start.3 = (bf16[416,128]{1,0:T(8,128)(2,1)S(1)}, bf16[416,128]{1,0:T(8,128)(2,1)S(1)}, u32[]{:S(2)}, u32[]{:S(2)}) collective-permute-start(bf16[416,128]{1,0:T(8,128)(2,1)S(1)} %get-tuple-element.34), channel_id=1, source_target_pairs={{0,8},{4,12},{8,0},{12,4},{1,9},{5,13},{9,1},{13,5},{2,10},{6,14},... | collective-permute-start | bytes 319496 | tf_op jit(solution)/shard_map/ppermute | solution.py:89
  12.3 2.5 %collective-permute-start.5 = (bf16[384,128]{1,0:T(8,128)(2,1)S(1)}, bf16[384,128]{1,0:T(8,128)(2,1)S(1)}, u32[]{:S(2)}, u32[]{:S(2)}) collective-permute-start(bf16[384,128]{1,0:T(8,128)(2,1)S(1)} %get-tuple-element.62), channel_id=1, source_target_pairs={{0,1},{1,0},{2,3},{3,2},{4,5},{5,4},{6,7},{7,6},{8,9},{9,8},{10,11... | collective-permute-start | bytes 294920 | tf_op jit(solution)/shard_map/ppermute | solution.py:93
  12.4 2.4 %collective-permute-start.6 = (bf16[384,128]{1,0:T(8,128)(2,1)S(1)}, bf16[384,128]{1,0:T(8,128)(2,1)S(1)}, u32[]{:S(2)}, u32[]{:S(2)}) collective-permute-start(bf16[384,128]{1,0:T(8,128)(2,1)S(1)} %get-tuple-element.61), channel_id=1, source_target_pairs={{0,1},{1,0},{2,3},{3,2},{4,5},{5,4},{6,7},{7,6},{8,9},{9,8},{10,11... | collective-permute-start | bytes 294920 | tf_op jit(solution)/shard_map/ppermute | solution.py:93
  12.9 6.7 %collective-permute-start.9 = (bf16[384,128]{1,0:T(8,128)(2,1)S(1)}, bf16[384,128]{1,0:T(8,128)(2,1)S(1)}, u32[]{:S(2)}, u32[]{:S(2)}) collective-permute-start(bf16[384,128]{1,0:T(8,128)(2,1)S(1)} %get-tuple-element.39.own_ref), channel_id=1, source_target_pairs={{0,2},{1,3},{2,0},{3,1},{4,6},{5,7},{6,4},{7,5},{8,10},{9,11},{10,... | collective-permute-start | bytes 294920 | tf_op jit(solution)/shard_map/ppermute | solution.py:93
  15.7 7.7 %collective-permute-start.7 = (bf16[416,128]{1,0:T(8,128)(2,1)S(1)}, bf16[416,128]{1,0:T(8,128)(2,1)S(1)}, u32[]{:S(2)}, u32[]{:S(2)}) collective-permute-start(bf16[416,128]{1,0:T(8,128)(2,1)S(1)} %get-tuple-element.37), channel_id=1, source_target_pairs={{0,4},{4,8},{8,12},{12,0},{1,5},{5,9},{9,13},{13,1},{2,6},{6,10},{... | collective-permute-start | bytes 319496 | tf_op jit(solution)/shard_map/ppermute | solution.py:89
  17.4 2.3 %copy-start.4 = (f32[128]{0:T(128)S(1)}, f32[128]{0:T(128)}, u32[]{:S(2)}) copy-start(f32[128]{0:T(128)} %param.12) | copy-start | bytes 1540
  17.4 6.7 %collective-permute-start.8 = (bf16[416,128]{1,0:T(8,128)(2,1)S(1)}, bf16[416,128]{1,0:T(8,128)(2,1)S(1)}, u32[]{:S(2)}, u32[]{:S(2)}) collective-permute-start(bf16[416,128]{1,0:T(8,128)(2,1)S(1)} %get-tuple-element.38), channel_id=1, source_target_pairs={{0,12},{4,0},{8,4},{12,8},{1,13},{5,1},{9,5},{13,9},{2,14},{6,2},{... | collective-permute-start | bytes 319496 | tf_op jit(solution)/shard_map/ppermute | solution.py:89
  19.6 1.3 %collective-permute-start.10 = (bf16[384,128]{1,0:T(8,128)(2,1)S(1)}, bf16[384,128]{1,0:T(8,128)(2,1)S(1)}, u32[]{:S(2)}, u32[]{:S(2)}) collective-permute-start(bf16[384,128]{1,0:T(8,128)(2,1)S(1)} %collective-permute-done.9.across_ref), channel_id=1, source_target_pairs={{0,1},{1,0},{2,3},{3,2},{4,5},{5,4},{6,7},{7,6},{8,9},{9,8},{10,11... | collective-permute-start | bytes 294920 | tf_op jit(solution)/shard_map/ppermute | solution.py:93
  24.0 5.3 %copy-start.1 = (bf16[128,512]{1,0:T(8,128)(2,1)S(1)}, bf16[128,512]{1,0:T(8,128)(2,1)}, u32[]{:S(2)}) copy-start(bf16[128,512]{1,0:T(8,128)(2,1)} %refs_8_.1) | copy-start | bytes 393220
  26.1 5.4 %collective-permute-start.13 = (bf16[400,128]{1,0:T(8,128)(2,1)S(1)}, bf16[400,128]{1,0:T(8,128)(2,1)S(1)}, u32[]{:S(2)}, u32[]{:S(2)}) collective-permute-start(bf16[400,128]{1,0:T(8,128)(2,1)S(1)} %get-tuple-element.50), channel_id=1, source_target_pairs={{0,12},{4,0},{8,4},{12,8},{1,13},{5,1},{9,5},{13,9},{2,14},{6,2},{... | collective-permute-start | bytes 307208 | tf_op jit(solution)/shard_map/ppermute | solution.py:89
  28.3 6.5 %collective-permute-start.12 = (bf16[400,128]{1,0:T(8,128)(2,1)S(1)}, bf16[400,128]{1,0:T(8,128)(2,1)S(1)}, u32[]{:S(2)}, u32[]{:S(2)}) collective-permute-start(bf16[400,128]{1,0:T(8,128)(2,1)S(1)} %get-tuple-element.45), channel_id=1, source_target_pairs={{0,4},{4,8},{8,12},{12,0},{1,5},{5,9},{9,13},{13,1},{2,6},{6,10},{... | collective-permute-start | bytes 307208 | tf_op jit(solution)/shard_map/ppermute | solution.py:89
  28.3 9.6 %collective-permute-start.11 = (bf16[400,128]{1,0:T(8,128)(2,1)S(1)}, bf16[400,128]{1,0:T(8,128)(2,1)S(1)}, u32[]{:S(2)}, u32[]{:S(2)}) collective-permute-start(bf16[400,128]{1,0:T(8,128)(2,1)S(1)} %get-tuple-element.44), channel_id=1, source_target_pairs={{0,8},{4,12},{8,0},{12,4},{1,9},{5,13},{9,1},{13,5},{2,10},{6,14},... | collective-permute-start | bytes 307208 | tf_op jit(solution)/shard_map/ppermute | solution.py:89
  29.4 12.6 %collective-permute-start.18 = (bf16[640,128]{1,0:T(8,128)(2,1)S(1)}, bf16[640,128]{1,0:T(8,128)(2,1)S(1)}, u32[]{:S(2)}, u32[]{:S(2)}) collective-permute-start(bf16[640,128]{1,0:T(8,128)(2,1)S(1)} %get-tuple-element.48.refs_0_), channel_id=1, source_target_pairs={{0,2},{1,3},{2,0},{3,1},{4,6},{5,7},{6,4},{7,5},{8,10},{9,11},{10,... | collective-permute-start | bytes 491528 | tf_op jit(solution)/shard_map/ppermute | solution.py:93
  31.3 12.2 %collective-permute-start.17 = (bf16[512,128]{1,0:T(8,128)(2,1)S(1)}, bf16[512,128]{1,0:T(8,128)(2,1)S(1)}, u32[]{:S(2)}, u32[]{:S(2)}) collective-permute-start(bf16[512,128]{1,0:T(8,128)(2,1)S(1)} %get-tuple-element.56), channel_id=1, source_target_pairs={{0,1},{1,0},{2,3},{3,2},{4,5},{5,4},{6,7},{7,6},{8,9},{9,8},{10,11... | collective-permute-start | bytes 393224 | tf_op jit(solution)/shard_map/ppermute | solution.py:93
  34.8 7.1 %collective-permute-start.21 = (bf16[768,128]{1,0:T(8,128)(2,1)S(1)}, bf16[768,128]{1,0:T(8,128)(2,1)S(1)}, u32[]{:S(2)}, u32[]{:S(2)}) collective-permute-start(bf16[768,128]{1,0:T(8,128)(2,1)S(1)} %shard_map.81.refs_4_), channel_id=1, source_target_pairs={{0,2},{1,3},{2,0},{3,1},{4,6},{5,7},{6,4},{7,5},{8,10},{9,11},{10,... | collective-permute-start | bytes 589832 | tf_op jit(solution)/shard_map/ppermute | solution.py:93
  37.7 6.3 %collective-permute-start.20 = (bf16[768,128]{1,0:T(8,128)(2,1)S(1)}, bf16[768,128]{1,0:T(8,128)(2,1)S(1)}, u32[]{:S(2)}, u32[]{:S(2)}) collective-permute-start(bf16[768,128]{1,0:T(8,128)(2,1)S(1)} %shard_map.81.refs_4_), channel_id=1, source_target_pairs={{0,1},{1,0},{2,3},{3,2},{4,5},{5,4},{6,7},{7,6},{8,9},{9,8},{10,11... | collective-permute-start | bytes 589832 | tf_op jit(solution)/shard_map/ppermute | solution.py:93
  37.9 5.5 %collective-permute-start.15 = (bf16[384,128]{1,0:T(8,128)(2,1)S(1)}, bf16[384,128]{1,0:T(8,128)(2,1)S(1)}, u32[]{:S(2)}, u32[]{:S(2)}) collective-permute-start(bf16[384,128]{1,0:T(8,128)(2,1)S(1)} %shard_map.82.refs_0_), channel_id=1, source_target_pairs={{0,2},{1,3},{2,0},{3,1},{4,6},{5,7},{6,4},{7,5},{8,10},{9,11},{10,... | collective-permute-start | bytes 294920 | tf_op jit(solution)/shard_map/ppermute | solution.py:93
  41.9 2.0 %collective-permute-start.22 = (bf16[768,128]{1,0:T(8,128)(2,1)S(1)}, bf16[768,128]{1,0:T(8,128)(2,1)S(1)}, u32[]{:S(2)}, u32[]{:S(2)}) collective-permute-start(bf16[768,128]{1,0:T(8,128)(2,1)S(1)} %collective-permute-done.21.refs_6_), channel_id=1, source_target_pairs={{0,1},{1,0},{2,3},{3,2},{4,5},{5,4},{6,7},{7,6},{8,9},{9,8},{10,11... | collective-permute-start | bytes 589832 | tf_op jit(solution)/shard_map/ppermute | solution.py:93
  42.0 2.0 %collective-permute-start.19 = (bf16[640,128]{1,0:T(8,128)(2,1)S(1)}, bf16[640,128]{1,0:T(8,128)(2,1)S(1)}, u32[]{:S(2)}, u32[]{:S(2)}) collective-permute-start(bf16[640,128]{1,0:T(8,128)(2,1)S(1)} %collective-permute-done.18.refs_2_), channel_id=1, source_target_pairs={{0,1},{1,0},{2,3},{3,2},{4,5},{5,4},{6,7},{7,6},{8,9},{9,8},{10,11... | collective-permute-start | bytes 491528 | tf_op jit(solution)/shard_map/ppermute | solution.py:93
  43.5 1.3 %collective-permute-start.14 = (bf16[384,128]{1,0:T(8,128)(2,1)S(1)}, bf16[384,128]{1,0:T(8,128)(2,1)S(1)}, u32[]{:S(2)}, u32[]{:S(2)}) collective-permute-start(bf16[384,128]{1,0:T(8,128)(2,1)S(1)} %shard_map.82.refs_0_), channel_id=1, source_target_pairs={{0,1},{1,0},{2,3},{3,2},{4,5},{5,4},{6,7},{7,6},{8,9},{9,8},{10,11... | collective-permute-start | bytes 294920 | tf_op jit(solution)/shard_map/ppermute | solution.py:93
  43.5 1.5 %collective-permute-start.16 = (bf16[384,128]{1,0:T(8,128)(2,1)S(1)}, bf16[384,128]{1,0:T(8,128)(2,1)S(1)}, u32[]{:S(2)}, u32[]{:S(2)}) collective-permute-start(bf16[384,128]{1,0:T(8,128)(2,1)S(1)} %collective-permute-done.15.refs_2_), channel_id=1, source_target_pairs={{0,1},{1,0},{2,3},{3,2},{4,5},{5,4},{6,7},{7,6},{8,9},{9,8},{10,11... | collective-permute-start | bytes 294920 | tf_op jit(solution)/shard_map/ppermute | solution.py:93
